TPU v7x, 512 devices: a whole 4x8x8 slice. The times are simulated.
512 devices in a mesh: lat: 16 (over z_lo, x, core), lon: 32 (over y, z_hi).
Axes of the slice: x: 4, y: 8, z: 8 (z_hi: 4, z_lo: 2; z = z_hi * 2 + z_lo), core: 2. Of those that a mesh axis runs over, the one named last changes fastest.
Arguments:
- tokens: bfloat16 [2, 96, 384, 192], P(None, 'lat', 'lon'), may hold values from -6 to 6
- gain_one: float32 [192], replicated, may hold values from 0.1 to 1.9
- gain_two: float32 [192], replicated, may hold values from 0.1 to 1.9
- qkv_weight: bfloat16 [192, 576], replicated, may hold values from -0.4375 to 0.4375
- proj_weight: bfloat16 [192, 192], replicated, may hold values from -0.4375 to 0.4375
- up_weight: bfloat16 [192, 768], replicated, may hold values from -0.4375 to 0.4375
- down_weight: bfloat16 [768, 192], replicated, may hold values from -0.21875 to 0.21875
- bias_table: float32 [6, 1, 16, 3312], P(None, None, 'lat'), may hold values from -6 to 306
- pos_index: int32 [144, 144], replicated, may hold values from 0 to 3311
- mask_ids: int32 [2, 96, 384], P(None, 'lat', 'lon'), may hold values from 0 to 2
- cotangent: bfloat16 [2, 96, 384, 192], P(None, 'lat', 'lon'), may hold values from -6 to 6
Outputs:
- output: bfloat16 [2, 96, 384, 192], P(None, 'lat', 'lon')
- delta_tokens: bfloat16 [2, 96, 384, 192], P(None, 'lat', 'lon')
- grad_gain_one: float32 [192], replicated
- grad_gain_two: float32 [192], replicated
- grad_qkv: float32 [192, 576], replicated
- grad_proj: float32 [192, 192], replicated
- grad_up: float32 [192, 768], replicated
- grad_down: float32 [768, 192], replicated
- grad_bias: float32 [6, 1, 16, 3312], P(None, None, 'lat')
All inputs are finite; a program needn't handle non-finite values.
Results may differ from a plain program's by a relative error of at most 0.025.
Values may be sent and summed in bfloat16 or wider, within the bound.
No kernel may reach another device: no remote copies, remote signals or barrier semaphores. Data moves between devices by JAX's collectives and lax.ppermute only.
A program may use at most 64 MiB of HBM per device.

v0:
```python
import math

import jax
import jax.numpy as jnp
from jax import lax
from jax.sharding import PartitionSpec as P

HEADS = 6
WZ = 2
WLAT = 6
WLON = 12
WT = 144
NPOS = 3312


EPS = 1e-05


def passed_along(x, axis, by):
    peers = lax.axis_size(axis)
    return lax.ppermute(x, axis, [(i, (i + by) % peers) for i in range(peers)])


def norm_stats(values):
    widened = values.astype(jnp.float32)
    center = widened - jnp.mean(widened, axis=-1, keepdims=True)
    spread = jnp.mean(center * center, axis=-1, keepdims=True)
    inverse = lax.rsqrt(spread + EPS)
    return (center * inverse, inverse)


def norm_back(delta_hidden, normal, inverse, gain):
    grad_gain = jnp.sum((delta_hidden * normal).reshape(-1, normal.shape[-1]), axis=0)
    delta_normal = delta_hidden * gain
    delta_input = inverse * (
        delta_normal
        - jnp.mean(delta_normal, axis=-1, keepdims=True)
        - normal * jnp.mean(delta_normal * normal, axis=-1, keepdims=True)
    )
    return (delta_input, grad_gain)


def gelu_pair(up_proj):
    cumulative = 0.5 * (1.0 + lax.erf(up_proj * 0.7071067811865476))
    density = jnp.exp(-0.5 * up_proj * up_proj) * 0.3989422804014327
    return (up_proj * cumulative, cumulative + up_proj * density)


def mlp_block(middle, gain_two, up_weight, down_weight, cotangent):
    normal, inverse = norm_stats(middle)
    normed = (normal * gain_two).astype(jnp.bfloat16)
    up_proj = jnp.dot(normed, up_weight, preferred_element_type=jnp.float32)
    active, slope = gelu_pair(up_proj)
    active = active.astype(jnp.bfloat16)
    output = (
        middle.astype(jnp.float32)
        + jnp.dot(active, down_weight, preferred_element_type=jnp.float32)
    ).astype(jnp.bfloat16)
    grad_down = jnp.dot(active.T, cotangent, preferred_element_type=jnp.float32)
    delta_act = jnp.dot(cotangent, down_weight.T, preferred_element_type=jnp.float32)
    delta_up = (delta_act * slope).astype(jnp.bfloat16)
    grad_up = jnp.dot(normed.T, delta_up, preferred_element_type=jnp.float32)
    delta_hidden = jnp.dot(delta_up, up_weight.T, preferred_element_type=jnp.float32)
    delta_input, grad_gain = norm_back(delta_hidden, normal, inverse, gain_two)
    delta_middle = (cotangent.astype(jnp.float32) + delta_input).astype(jnp.bfloat16)
    return (output, delta_middle, grad_gain, grad_up, grad_down)


def to_windows(layout):
    levels, lat_rows, lon_cols, features = layout.shape
    layout = layout.reshape(
        levels // WZ, WZ, lat_rows // WLAT, WLAT, lon_cols // WLON, WLON, features
    )
    layout = layout.transpose(2, 0, 4, 1, 3, 5, 6)
    return layout.reshape(
        lat_rows // WLAT, levels // WZ, lon_cols // WLON, WZ * WLAT * WLON, features
    )


def from_windows(windows, levels, lat_rows, lon_cols):
    features = windows.shape[-1]
    windows = windows.reshape(
        lat_rows // WLAT, levels // WZ, lon_cols // WLON, WZ, WLAT, WLON, features
    )
    windows = windows.transpose(1, 3, 0, 4, 2, 5, 6)
    return windows.reshape(levels, lat_rows, lon_cols, features)


def roll_grid(layout, toward):
    layout = jnp.roll(layout, toward, axis=0)
    rows_half = WLAT // 2
    cols_half = WLON // 2
    row_count = layout.shape[1]
    row_piece = layout[:, :rows_half] if toward < 0 else layout[:, row_count - rows_half :]
    row_got = passed_along(row_piece, "lat", toward)
    layout = jnp.concatenate(
        (
            (layout[:, rows_half:], row_got)
            if toward < 0
            else (row_got, layout[:, : row_count - rows_half])
        ),
        axis=1,
    )
    col_count = layout.shape[2]
    col_piece = layout[:, :, :cols_half] if toward < 0 else layout[:, :, col_count - cols_half :]
    col_got = passed_along(col_piece, "lon", toward)
    layout = jnp.concatenate(
        (
            (layout[:, :, cols_half:], col_got)
            if toward < 0
            else (col_got, layout[:, :, : col_count - cols_half])
        ),
        axis=2,
    )
    return layout


def bias_pairs(bias_table, pos_index):
    head_count, level_blocks, lat_blocks = bias_table.shape[:3]
    picked = jnp.take(bias_table, pos_index.reshape(-1), axis=3)
    picked = picked.reshape(head_count, level_blocks, lat_blocks, WT, WT).transpose(2, 1, 0, 3, 4)
    return picked[:, :, None]


def table_grad(delta_type, pos_index):
    lat_blocks, level_blocks, head_count = delta_type.shape[:3]
    flattened = delta_type.reshape(lat_blocks, level_blocks, head_count, WT * WT).transpose(
        3, 2, 1, 0
    )
    summed = jax.ops.segment_sum(flattened, pos_index.reshape(-1), num_segments=NPOS)
    return summed.transpose(1, 2, 3, 0)


def attend(windows, mask_win, bias_win, qkv_weight):
    leading = windows.shape[:-2]
    features = windows.shape[-1]
    head_size = features // HEADS
    packed = jnp.dot(
        windows.reshape(-1, features), qkv_weight, preferred_element_type=jnp.float32
    ).astype(jnp.bfloat16)
    packed = packed.reshape(leading + (WT, 3, HEADS, head_size))
    queries = packed[..., 0, :, :]
    key_heads = packed[..., 1, :, :]
    values = packed[..., 2, :, :]
    factor = head_size ** (-0.5)
    scores = (
        jnp.einsum("...phd,...rhd->...hpr", queries, key_heads, preferred_element_type=jnp.float32)
        * factor
        + bias_win
    )
    allowed = mask_win[..., None, :, None] == mask_win[..., None, None, :]
    scores = jnp.where(allowed, scores, -1e30)
    row_top = jnp.max(scores, axis=-1, keepdims=True)
    weight = jnp.exp(scores - row_top)
    attn_prob = weight / jnp.sum(weight, axis=-1, keepdims=True)
    rounded = attn_prob.astype(jnp.bfloat16)
    mixture = jnp.einsum(
        "...hpr,...rhd->...phd", rounded, values, preferred_element_type=jnp.float32
    ).astype(jnp.bfloat16)
    return (
        mixture.reshape(leading + (WT, features)),
        (queries, key_heads, values, attn_prob, rounded),
    )


def attend_back(windows, qkv_weight, stored, delta_mixture):
    queries, key_heads, values, attn_prob, rounded = stored
    leading = windows.shape[:-2]
    features = windows.shape[-1]
    head_size = features // HEADS
    factor = head_size ** (-0.5)
    delta_heads = delta_mixture.reshape(leading + (WT, HEADS, head_size))
    delta_probs = jnp.einsum(
        "...phd,...rhd->...hpr", delta_heads, values, preferred_element_type=jnp.float32
    )
    delta_values = jnp.einsum(
        "...hpr,...phd->...rhd", rounded, delta_heads, preferred_element_type=jnp.float32
    )
    delta_scores = attn_prob * (
        delta_probs - jnp.sum(delta_probs * attn_prob, axis=-1, keepdims=True)
    )
    delta_low = delta_scores.astype(jnp.bfloat16)
    delta_query = (
        jnp.einsum(
            "...hpr,...rhd->...phd", delta_low, key_heads, preferred_element_type=jnp.float32
        )
        * factor
    )
    delta_keys = (
        jnp.einsum("...hpr,...phd->...rhd", delta_low, queries, preferred_element_type=jnp.float32)
        * factor
    )
    delta_packed = (
        jnp.stack((delta_query, delta_keys, delta_values), axis=-3)
        .astype(jnp.bfloat16)
        .reshape(-1, 3 * features)
    )
    flattened = windows.reshape(-1, features)
    grad_qkv = jnp.dot(flattened.T, delta_packed, preferred_element_type=jnp.float32)
    delta_window = jnp.dot(delta_packed, qkv_weight.T, preferred_element_type=jnp.float32).astype(
        jnp.bfloat16
    )
    return (delta_window.reshape(leading + (WT, features)), grad_qkv, delta_scores)


def local(
    tokens,
    gain_one,
    gain_two,
    qkv_weight,
    proj_weight,
    up_weight,
    down_weight,
    bias_table,
    pos_index,
    mask_ids,
    cotangent,
):
    levels, lat_rows, lon_cols, features = tokens.shape
    normal_one, inverse_one = norm_stats(tokens)
    normed = (normal_one * gain_one).astype(jnp.bfloat16)
    windows = to_windows(roll_grid(normed, -1))
    mask_win = to_windows(mask_ids[..., None])[..., 0]
    bias_win = bias_pairs(bias_table, pos_index)
    mixture, stored = attend(windows, mask_win, bias_win, qkv_weight)
    flat_mix = mixture.reshape(-1, features)
    attn_win = jnp.dot(flat_mix, proj_weight, preferred_element_type=jnp.float32).astype(
        jnp.bfloat16
    )
    attention = roll_grid(
        from_windows(attn_win.reshape(mixture.shape), levels, lat_rows, lon_cols), 1
    )
    middle = (tokens.astype(jnp.float32) + attention.astype(jnp.float32)).astype(jnp.bfloat16)
    output, delta_middle, grad_gain_two, grad_up, grad_down = mlp_block(
        middle.reshape(-1, features),
        gain_two,
        up_weight,
        down_weight,
        cotangent.reshape(-1, features),
    )
    output = output.reshape(tokens.shape)
    delta_middle = delta_middle.reshape(tokens.shape)
    delta_attn = to_windows(roll_grid(delta_middle, -1))
    flat_delta = delta_attn.reshape(-1, features)
    grad_proj = jnp.dot(flat_mix.T, flat_delta, preferred_element_type=jnp.float32)
    delta_mixture = (
        jnp.dot(flat_delta, proj_weight.T, preferred_element_type=jnp.float32)
        .astype(jnp.bfloat16)
        .reshape(mixture.shape)
    )
    delta_window, grad_qkv, delta_scores = attend_back(windows, qkv_weight, stored, delta_mixture)
    local_bias = table_grad(jnp.sum(delta_scores, axis=2), pos_index)
    delta_normed = roll_grid(from_windows(delta_window, levels, lat_rows, lon_cols), 1)
    delta_input, grad_gain_one = norm_back(
        delta_normed.astype(jnp.float32), normal_one, inverse_one, gain_one
    )
    delta_tokens = (delta_middle.astype(jnp.float32) + delta_input).astype(jnp.bfloat16)
    totals = lax.psum(
        (grad_gain_one, grad_gain_two, grad_qkv, grad_proj, grad_up, grad_down), ("lat", "lon")
    )
    grad_bias = lax.psum(local_bias.astype(jnp.bfloat16), "lon").astype(jnp.float32)
    factor = 1.0 / math.sqrt(
        levels * lat_rows * lon_cols * lax.axis_size("lat") * lax.axis_size("lon")
    )
    return (
        output,
        delta_tokens,
        totals[0] * factor,
        totals[1] * factor,
        totals[2] * factor,
        totals[3] * factor,
        totals[4] * factor,
        totals[5] * factor,
        grad_bias,
    )


def solution(mesh):
    in_specs = (
        P(None, "lat", "lon", None),
        P(),
        P(),
        P(),
        P(),
        P(),
        P(),
        P(None, None, "lat", None),
        P(),
        P(None, "lat", "lon"),
        P(None, "lat", "lon", None),
    )
    out_specs = (
        P(None, "lat", "lon", None),
        P(None, "lat", "lon", None),
        P(),
        P(),
        P(),
        P(),
        P(),
        P(),
        P(None, None, "lat", None),
    )
    return jax.shard_map(local, mesh=mesh, in_specs=in_specs, out_specs=out_specs, check_vma=False)
```

profile of v0, /device:TPU:1, one launch (start us, length us, event | category | flops | bytes accessed | tf_op | source)
XLA Modules:
  0.0 708.1 jit_solution(8504700657193047525)
XLA Ops:
  7.2 1.0 convert_reduce_fusion
  8.3 1.1 fusion.31
  9.4 1.0 fusion.26
  10.4 8.8 %collective-permute-start = (bf16[2,3,12,192]{3,2,1,0:T(8,128)(2,1)S(1)}, bf16[2,3,12,192]{3,2,1,0:T(8,128)(2,1)S(1)}, u32[]{:S(2)}, u32[]{:S(2)}) collective-permute-start(bf16[2,3,12,192]{3,2,1,0:T(8,128)(2,1)S(1)} %get-tuple-element.52), channel_id=1, source_target_pairs={{0,480},{32,0},{64,32},{96,64},{128,96},{160,128},{192,160},{224,1... | collective-permute-start | bytes 82952 | tf_op jit(solution)/shard_map/ppermute | solution.py:21
  19.2 1.1 reshape.329
  20.6 1.0 compare_and_fusion
  22.4 8.2 %collective-permute-start.1 = (bf16[2,6,6,192]{3,2,1,0:T(8,128)(2,1)S(1)}, bf16[2,6,6,192]{3,2,1,0:T(8,128)(2,1)S(1)}, u32[]{:S(2)}, u32[]{:S(2)}) collective-permute-start(bf16[2,6,6,192]{3,2,1,0:T(8,128)(2,1)S(1)} %get-tuple-element.50), channel_id=1, source_target_pairs={{0,31},{1,0},{2,1},{3,2},{4,3},{5,4},{6,5},{7,6},{8,7},{9,8},{10,9... | collective-permute-start | bytes 82952 | tf_op jit(solution)/shard_map/ppermute | solution.py:21
  31.4 38.7 %gather_fusion = f32[20736,6]{1,0:T(8,128)} fusion(f32[6,3312]{0,1:T(8,128)S(1)} %bitcast.78, s32[21504]{0:T(1024)S(1)} %pad_clamp_fusion), kind=kCustom, calls=%fused_computation | custom fusion | bytes 1078272 | tf_op jit(solution)/shard_map/jit(_take)/gather | solution.py:120
  70.1 11.7 %copy.46 = f32[6,144,144]{1,2,0:T(8,128)S(1)} copy(f32[6,144,144]{0,2,1:T(8,128)} %bitcast.79) | data formatting | bytes 995328 | tf_op jit(solution)/shard_map/jit(_take)/gather | solution.py:120
  84.9 3.3 collective-permute-start.2
  88.2 2.7 collective-permute-done.2
  90.9 1.9 collective-permute-start.3
  93.7 6.3 collective-permute-done.3
  100.8 1.2 fusion.5
  102.5 1.2 fusion.45
  103.9 8.0 %collective-permute-start.4 = (bf16[2,3,12,192]{3,2,1,0:T(8,128)(2,1)S(1)}, bf16[2,3,12,192]{3,2,1,0:T(8,128)(2,1)S(1)}, u32[]{:S(2)}, u32[]{:S(2)}) collective-permute-start(bf16[2,3,12,192]{3,2,1,0:T(8,128)(2,1)S(1)} %get-tuple-element.46), channel_id=1, source_target_pairs={{0,480},{32,0},{64,32},{96,64},{128,96},{160,128},{192,160},{224,1... | collective-permute-start | bytes 82952 | tf_op jit(solution)/shard_map/ppermute | solution.py:21
  111.9 1.1 fusion.59
  113.0 1.9 collective-permute-start.5
  115.0 1.2 fusion.8
  117.0 2.3 collective-permute-done.5
  119.7 1.0 convolution_bitcast_fusion
  122.7 1.1 fusion.57
  124.4 2.1 collective-permute-start.6
  126.5 6.2 copy.54
  132.7 112.8 %scatter_custom_fusion = f32[3312,6]{1,0:T(8,128)S(1)} fusion(s32[20736]{0:T(1024)} %reshape.352, f32[20736,6]{1,0:T(8,128)} %copy.54, f32[]{:T(128)} %constant.16.clone.1), kind=kCustom, calls=%fused_computation.24 | custom fusion | flops 124416 | bytes 80000 | tf_op jit(solution)/shard_map/scatter-add | solution.py:130
  247.4 1.9 collective-permute-start.7
  249.3 144.2 %psum.55 = bf16[6,1,1,3312]{0,3,2,1:T(8,128)(2,1)S(1)} all-reduce(bf16[6,1,1,3312]{0,3,2,1:T(8,128)(2,1)S(1)} %convert_bitcast_fusion), channel_id=1, replica_groups=mesh['lat'=16,'lon'=32] {'lon'}, use_global_device_ids=true, to_apply=%region_20.21 | all-reduce | flops 19872 | bytes 79488 | tf_op jit(solution)/shard_map/psum | solution.py:261
  393.5 1.0 copy.57
  395.7 123.6 %all-reduce = (f32[192]{0:T(256)S(1)}, f32[192]{0:T(256)S(1)}) all-reduce(f32[192]{0:T(256)S(1)} %get-tuple-element.29, f32[192]{0:T(256)S(1)} %get-tuple-element.27), channel_id=1, replica_groups=mesh['lat'=16,'lon'=32] {'lat','lon'}, use_global_device_ids=true, to_apply=%region_12.13 | all-reduce | flops 384 | bytes 3072 | tf_op jit(solution)/shard_map/psum | solution.py:258
  520.4 175.5 %all-reduce.4.cloned.1.call-done = (f32[192,576]{1,0:T(8,128)}, f32[192,192]{1,0:T(8,128)}, f32[192,768]{1,0:T(8,128)}, f32[768,192]{0,1:T(8,128)}) async-done(((f32[192,576]{1,0:T(8,128)}, f32[192,192]{1,0:T(8,128)}, f32[192,768]{1,0:T(8,128)}, f32[768,192]{0,1:T(8,128)}), (f32[192,576]{1,0:T(8,128)}, f32[192,192]{1,0:T(8,128)}, f32[192,768]{1,0:T(8,128)}, ...) | async-done | bytes 1769488 | tf_op jit(solution)/shard_map/psum | solution.py:258
  695.9 1.9 broadcast_multiply_fusion.2
  697.9 1.6 broadcast_multiply_fusion.3
  (128 shorter events, 16.7 us)
Async XLA Ops:
  7.2 93.3 %copy-start = (bf16[192,768]{1,0:T(8,128)(2,1)S(1)}, bf16[192,768]{1,0:T(8,128)(2,1)}, u32[]{:S(2)}) copy-start(bf16[192,768]{1,0:T(8,128)(2,1)} %param.16) | copy-start | bytes 884740
  7.2 23.6 %copy-start.16 = (f32[6,1,1,3312]{3,2,1,0:T(1,128)S(1)}, f32[6,1,1,3312]{3,2,1,0:T(1,128)}, u32[]{:S(2)}) copy-start(f32[6,1,1,3312]{3,2,1,0:T(1,128)} %param.18) | copy-start | bytes 238468
  7.2 688.7 %all-reduce.4.cloned.1.call-start = ((), (), s32[]{:S(2)}) async-start(), calls=%async_computation | async-start | bytes 3735552 | tf_op jit(solution)/shard_map/psum | solution.py:258
  10.4 11.9 %collective-permute-start = (bf16[2,3,12,192]{3,2,1,0:T(8,128)(2,1)S(1)}, bf16[2,3,12,192]{3,2,1,0:T(8,128)(2,1)S(1)}, u32[]{:S(2)}, u32[]{:S(2)}) collective-permute-start(bf16[2,3,12,192]{3,2,1,0:T(8,128)(2,1)S(1)} %get-tuple-element.52), channel_id=1, source_target_pairs={{0,480},{32,0},{64,32},{96,64},{128,96},{160,128},{192,160},{224,1... | collective-permute-start | bytes 82952 | tf_op jit(solution)/shard_map/ppermute | solution.py:21
  22.4 59.3 %collective-permute-start.1 = (bf16[2,6,6,192]{3,2,1,0:T(8,128)(2,1)S(1)}, bf16[2,6,6,192]{3,2,1,0:T(8,128)(2,1)S(1)}, u32[]{:S(2)}, u32[]{:S(2)}) collective-permute-start(bf16[2,6,6,192]{3,2,1,0:T(8,128)(2,1)S(1)} %get-tuple-element.50), channel_id=1, source_target_pairs={{0,31},{1,0},{2,1},{3,2},{4,3},{5,4},{6,5},{7,6},{8,7},{9,8},{10,9... | collective-permute-start | bytes 82952 | tf_op jit(solution)/shard_map/ppermute | solution.py:21
  70.1 11.8 %copy-start.3 = (bf16[192,576]{1,0:T(8,128)(2,1)S(1)}, bf16[192,576]{1,0:T(8,128)(2,1)}, u32[]{:S(2)}) copy-start(bf16[192,576]{1,0:T(8,128)(2,1)} %param.14) | copy-start | bytes 663556
  81.8 0.6 copy-start.5
  83.7 0.9 copy-start.11
  83.7 9.2 %copy-start.2 = (s32[144,144]{1,0:T(8,128)S(1)}, s32[144,144]{1,0:T(8,128)}, u32[]{:S(2)}) copy-start(s32[144,144]{1,0:T(8,128)} %param.19) | copy-start | bytes 248836
  83.7 9.9 %copy-start.17 = (bf16[2,6,12,192]{3,0,2,1:T(2,128)(2,1)S(1)}, bf16[2,6,12,192]{3,0,2,1:T(2,128)(2,1)}, u32[]{:S(2)}) copy-start(bf16[2,6,12,192]{3,0,2,1:T(2,128)(2,1)} %param.21) | copy-start | bytes 165892
  84.0 9.6 %copy-start.13 = (bf16[6,32,144]{2,1,0:T(8,128)(2,1)}, bf16[6,32,144]{2,1,0:T(8,128)(2,1)S(1)}, u32[]{:S(2)}) copy-start(bf16[6,32,144]{2,1,0:T(8,128)(2,1)S(1)} %convolution_convert_fusion.1) | copy-start | bytes 165892
  84.1 15.9 %copy-start.1 = (bf16[2,6,12,192]{3,0,2,1:T(2,128)(2,1)S(1)}, bf16[2,6,12,192]{3,0,2,1:T(2,128)(2,1)}, u32[]{:S(2)}) copy-start(bf16[2,6,12,192]{3,0,2,1:T(2,128)(2,1)} %param.11) | copy-start | bytes 165892
  84.1 16.5 %copy-start.18 = (f32[192]{0:T(256)S(1)}, f32[192]{0:T(256)}, u32[]{:S(2)}) copy-start(f32[192]{0:T(256)} %param.13) | copy-start | bytes 2308
  84.9 6.0 collective-permute-start.2
  90.9 9.1 %collective-permute-start.3 = (bf16[2,6,6,192]{3,2,1,0:T(8,128)(2,1)S(1)}, bf16[2,6,6,192]{3,2,1,0:T(8,128)(2,1)S(1)}, u32[]{:S(2)}, u32[]{:S(2)}) collective-permute-start(bf16[2,6,6,192]{3,2,1,0:T(8,128)(2,1)S(1)} %fusion.42), channel_id=1, source_target_pairs={{0,1},{1,2},{2,3},{3,4},{4,5},{5,6},{6,7},{7,8},{8,9},{9,10},{10,1... | collective-permute-start | bytes 82952 | tf_op jit(solution)/shard_map/ppermute | solution.py:21
  103.8 15.5 %copy-start.12 = (bf16[192,192]{1,0:T(8,128)(2,1)S(1)}, bf16[192,192]{1,0:T(8,128)(2,1)}, u32[]{:S(2)}) copy-start(bf16[192,192]{1,0:T(8,128)(2,1)} %param.15) | copy-start | bytes 221188
  103.9 9.1 %collective-permute-start.4 = (bf16[2,3,12,192]{3,2,1,0:T(8,128)(2,1)S(1)}, bf16[2,3,12,192]{3,2,1,0:T(8,128)(2,1)S(1)}, u32[]{:S(2)}, u32[]{:S(2)}) collective-permute-start(bf16[2,3,12,192]{3,2,1,0:T(8,128)(2,1)S(1)} %get-tuple-element.46), channel_id=1, source_target_pairs={{0,480},{32,0},{64,32},{96,64},{128,96},{160,128},{192,160},{224,1... | collective-permute-start | bytes 82952 | tf_op jit(solution)/shard_map/ppermute | solution.py:21
  113.0 6.2 collective-permute-start.5
  119.4 1.3 copy-start.7
  121.2 0.9 copy-start.15
  121.4 1.0 copy-start.4
  121.6 1.0 copy-start.6
  124.4 122.9 %collective-permute-start.6 = (bf16[2,3,12,192]{3,2,1,0:T(8,128)(2,1)S(1)}, bf16[2,3,12,192]{3,2,1,0:T(8,128)(2,1)S(1)}, u32[]{:S(2)}, u32[]{:S(2)}) collective-permute-start(bf16[2,3,12,192]{3,2,1,0:T(8,128)(2,1)S(1)} %get-tuple-element.41), channel_id=1, source_target_pairs={{0,32},{32,64},{64,96},{96,128},{128,160},{160,192},{192,224},{224... | collective-permute-start | bytes 82952 | tf_op jit(solution)/shard_map/ppermute | solution.py:21
  245.6 0.9 copy-start.8
  245.6 0.9 copy-start.14
  247.4 147.2 %collective-permute-start.7 = (bf16[2,6,6,192]{3,2,1,0:T(8,128)(2,1)S(1)}, bf16[2,6,6,192]{3,2,1,0:T(8,128)(2,1)S(1)}, u32[]{:S(2)}, u32[]{:S(2)}) collective-permute-start(bf16[2,6,6,192]{3,2,1,0:T(8,128)(2,1)S(1)} %fusion.40), channel_id=1, source_target_pairs={{0,1},{1,2},{2,3},{3,4},{4,5},{5,6},{6,7},{7,8},{8,9},{9,10},{10,1... | collective-permute-start | bytes 82952 | tf_op jit(solution)/shard_map/ppermute | solution.py:21
  393.5 1.0 copy-start.19
  695.9 3.6 copy-start.10
  695.9 4.4 copy-start.9
Sparse Core Ops, SparseCore 0:
  394.7 301.2 all-reduce.3
where the time goes:
time: 709 us; the launch traced here: 708 us
  blocking collectives  268 us (38%)
  waiting for transfers between devices  187 us (26%)
  other arithmetic  126 us (18%)
  local copies, waits for them, and re-layouts  65.9 us (9%)
  starting transfers between devices  36.1 us (5%)
  between operations  14.8 us (2%)
  matrix products  10.7 us (2%)
    psum x1, waiting for transfers between devices, local(): lax.psum((grad_gain_one, grad_gain_two, grad_qkv, grad_proj, grad_up, gra...  175 us
    psum x1, blocking collectives, local(): lax.psum(local_bias.astype(jnp.bfloat16), 'lon').astype(jnp.float32)  144 us
    psum x1, blocking collectives, local(): lax.psum((grad_gain_one, grad_gain_two, grad_qkv, grad_proj, grad_up, gra...  124 us
    scatter-add x1, other arithmetic, table_grad(): jax.ops.segment_sum(flattened, pos_index.reshape(-1), num_segments=NPOS)  113 us
    gather x2, local copies, waits for them, and re-layouts, bias_pairs(): picked = jnp.take(bias_table, pos_index.reshape(-1), axis=3)  50.3 us
    ppermute x8, starting transfers between devices, passed_along(): return lax.ppermute(x, axis, [(i, (i + by) % peers) for i in range(peers)])  36.1 us
  transfers between devices with their start and end apart: 9, of which 4 were waited for; matrix products, arithmetic and copies ran while one was open for 26% of the time, Pallas kernels for 0%

commit v1 on v0

v1 whole, which is shorter than its diff:
```python
import jax
import jax.numpy as jnp
from jax import lax
from jax.experimental import pallas as pl
from jax.experimental.pallas import tpu as pltpu
from jax.sharding import PartitionSpec as P

HEADS = 6
WT = 144
NPOS = 3312
C = 192
HID = 768
HEAD = C // HEADS
SLOTS = 26
LANES = 128
TOKENS = 73728
TAIL = WT - LANES
ROWS = WT + 2 * TAIL
GROWS = 3584
BROWS = 160
EPS = 1e-05
F32 = jnp.float32
BF16 = jnp.bfloat16


def dot(a, b):
    return lax.dot_general(a, b, (((1,), (0,)), ((), ())), preferred_element_type=F32)


def dot_nt(a, b):
    return lax.dot_general(a, b, (((1,), (1,)), ((), ())), preferred_element_type=F32)


def dot_tn(a, b):
    return lax.dot_general(a, b, (((0,), (0,)), ((), ())), preferred_element_type=F32)


def norm_stats(widened):
    center = widened - jnp.mean(widened, axis=-1, keepdims=True)
    spread = jnp.mean(center * center, axis=-1, keepdims=True)
    inverse = lax.rsqrt(spread + EPS)
    return center * inverse, inverse


def norm_back(delta_hidden, normal, inverse, gain):
    grad_gain = jnp.sum(delta_hidden * normal, axis=0, keepdims=True)
    delta_normal = delta_hidden * gain
    delta_input = inverse * (
        delta_normal
        - jnp.mean(delta_normal, axis=-1, keepdims=True)
        - normal * jnp.mean(delta_normal * normal, axis=-1, keepdims=True)
    )
    return delta_input, grad_gain


def gather_kernel(table_ref, pos_ref, bias_ref, flat_ref):
    def rows(i, carry):
        at = pl.ds(pl.multiple_of(i * 8, 8), 8)
        pos = pos_ref[at, :]
        lane = jnp.bitwise_and(pos, LANES - 1)
        slot = jnp.right_shift(pos, 7)
        held = [jnp.zeros((8, LANES), F32)] * HEADS
        for g in range(SLOTS):
            here = slot == g
            for h in range(HEADS):
                row = jnp.broadcast_to(table_ref[h, g : g + 1, :], (8, LANES))
                got = jnp.take_along_axis(row, lane, axis=1)
                held[h] = jnp.where(here, got, held[h])
        for h in range(HEADS):
            flat_ref[h, at, :] = held[h]
        return carry

    lax.fori_loop(0, ROWS // 8, rows, 0)
    for h in range(HEADS):
        at = h * WT
        bias_ref[at : at + WT, :LANES] = flat_ref[h, :WT, :]
        bias_ref[at : at + LANES, LANES:] = flat_ref[h, WT : WT + TAIL, :].T
        bias_ref[at + LANES : at + WT, LANES:] = flat_ref[h, WT + TAIL :, :].T[:TAIL]


def bias_pairs(table, pos_flat):
    return pl.pallas_call(
        gather_kernel,
        out_shape=jax.ShapeDtypeStruct((HEADS * WT, WT), F32),
        scratch_shapes=[pltpu.VMEM((HEADS, ROWS, LANES), F32)],
        name="bias_pairs",
        compiler_params=pltpu.CompilerParams(vmem_limit_bytes=16 * 1024 * 1024),
        cost_estimate=pl.CostEstimate(flops=10_000_000, bytes_accessed=1_200_000, transcendentals=0),
    )(table, pos_flat)


def flat_pairs(pos_index):
    turned = pos_index[:, LANES:].T
    rest = jnp.pad(turned[:, LANES:], ((0, 0), (0, LANES - TAIL)))
    return jnp.concatenate((pos_index[:, :LANES], turned[:, :LANES], rest), axis=0)


def block_kernel(
    x_ref,
    cot_ref,
    gain_one_ref,
    gain_two_ref,
    qkv_ref,
    proj_ref,
    up_ref,
    down_ref,
    bias_ref,
    mask_row_ref,
    mask_col_ref,
    pos_ref,
    out_ref,
    delta_ref,
    grads_ref,
    grad_bias_ref,
    scores_ref,
    prob_ref,
    low_ref,
    pairs_ref,
    sums_ref,
):
    factor = HEAD ** (-0.5)
    x = x_ref[...].astype(F32)
    gain_one = gain_one_ref[...]
    gain_two = gain_two_ref[...]
    normal_one, inverse_one = norm_stats(x)
    normed = (normal_one * gain_one).astype(BF16)
    queries = dot(normed, qkv_ref[0]).astype(BF16)
    keys = dot(normed, qkv_ref[1]).astype(BF16)
    values = dot(normed, qkv_ref[2]).astype(BF16)
    head_of = lax.broadcasted_iota(jnp.int32, (WT, C), 1) // HEAD
    allowed = mask_col_ref[...] == mask_row_ref[...]

    def by_head(a):
        return jnp.concatenate([jnp.where(head_of == h, a, jnp.zeros_like(a)) for h in range(HEADS)], axis=0)

    def joined(a):
        out = a[:WT]
        for h in range(1, HEADS):
            out = jnp.where(head_of == h, a[h * WT : (h + 1) * WT], out)
        return out

    queries_by = by_head(queries)
    scores_ref[...] = dot_nt(queries_by, keys)
    for h in range(HEADS):
        at = pl.ds(h * WT, WT)
        scores = scores_ref[at, :] * factor + bias_ref[at, :]
        scores = jnp.where(allowed, scores, -1e30)
        weight = jnp.exp(scores - jnp.max(scores, axis=-1, keepdims=True))
        prob = weight * (1.0 / jnp.sum(weight, axis=-1, keepdims=True))
        prob_ref[at, :] = prob
        low_ref[at, :] = prob.astype(BF16)
    mixture = joined(dot(low_ref[...], values)).astype(BF16)
    attention = dot(mixture, proj_ref[...]).astype(BF16)

    middle = (x + attention.astype(F32)).astype(BF16)
    widened = middle.astype(F32)
    normal_two, inverse_two = norm_stats(widened)
    normed_two = (normal_two * gain_two).astype(BF16)
    cot = cot_ref[...]
    up_proj = dot(normed_two, up_ref[...])
    cumulative = 0.5 * (1.0 + lax.erf(up_proj * 0.7071067811865476))
    density = jnp.exp(-0.5 * up_proj * up_proj) * 0.3989422804014327
    active = (up_proj * cumulative).astype(BF16)
    out_ref[...] = (widened + dot(active, down_ref[...])).astype(BF16)
    grad_down = dot_tn(active, cot)
    grads_ref[1152:1920] = grad_down[:, :LANES].astype(BF16)
    grads_ref[1920:2304] = jnp.concatenate(
        (grad_down[:384, LANES:], grad_down[384:, LANES:]), axis=1
    ).astype(BF16)
    delta_act = dot_nt(cot, down_ref[...])
    delta_up = (delta_act * (cumulative + up_proj * density)).astype(BF16)
    grad_up = dot_tn(normed_two, delta_up).astype(BF16)
    for t in range(6):
        grads_ref[C * t : C * (t + 1)] = grad_up[:, LANES * t : LANES * (t + 1)]
    delta_hidden = dot_nt(delta_up, up_ref[...])
    delta_input, grad_gain_two = norm_back(delta_hidden, normal_two, inverse_two, gain_two)
    delta_middle = (cot.astype(F32) + delta_input).astype(BF16)

    grad_proj = dot_tn(mixture, delta_middle)
    mixture_by = by_head(dot_nt(delta_middle, proj_ref[...]).astype(BF16))
    delta_value = dot_tn(low_ref[...], mixture_by)
    scores_ref[...] = dot_nt(mixture_by, values)
    for h in range(HEADS):
        at = pl.ds(h * WT, WT)
        prob = prob_ref[at, :]
        delta_prob = scores_ref[at, :]
        scores = prob * (delta_prob - jnp.sum(delta_prob * prob, axis=-1, keepdims=True))
        low_ref[at, :] = scores.astype(BF16)
        turned = scores[:, LANES:].T
        pairs_ref[h, :WT, :] = scores[:, :LANES]
        pairs_ref[h, WT : WT + TAIL, :] = turned[:, :LANES]
        pairs_ref[h, WT + TAIL :, :] = jnp.zeros((TAIL, LANES), F32)
        pairs_ref[h, WT + TAIL :, :TAIL] = turned[:, LANES:]
    delta_query = joined(dot(low_ref[...], keys)) * factor
    delta_key = dot_tn(low_ref[...], queries_by) * factor
    delta_normed = jnp.zeros((WT, C), F32)
    parts = []
    for k, part in enumerate((delta_query, delta_key, delta_value)):
        part = part.astype(BF16)
        parts.append(dot_tn(normed, part))
        delta_normed = delta_normed + dot_nt(part, qkv_ref[k])
    parts.append(grad_proj)
    for k in range(4):
        grads_ref[2304 + C * k : 2304 + C * (k + 1)] = parts[k][:, :LANES].astype(BF16)
    for k in range(2):
        grads_ref[3072 + C * k : 3072 + C * (k + 1)] = jnp.concatenate(
            (parts[2 * k][:, LANES:], parts[2 * k + 1][:, LANES:]), axis=1
        ).astype(BF16)
    delta_normed = delta_normed.astype(BF16).astype(F32)
    delta_input, grad_gain_one = norm_back(delta_normed, normal_one, inverse_one, gain_one)
    delta_ref[...] = (delta_middle.astype(F32) + delta_input).astype(BF16)
    gains = jnp.concatenate((grad_gain_one, grad_gain_two), axis=0)
    wide = jnp.concatenate((gains, jnp.zeros((2, 2 * LANES - C), F32)), axis=1)
    grads_ref[3456:3584] = jnp.concatenate(
        (wide[:, :LANES], wide[:, LANES:], jnp.zeros((124, LANES), F32)), axis=0
    ).astype(BF16)

    sums_ref[...] = jnp.zeros_like(sums_ref)
    slot_ids = lax.broadcasted_iota(jnp.int32, (32, LANES), 0)
    lane_ids = lax.broadcasted_iota(jnp.int32, (LANES, LANES), 0)

    def rows(i, carry):
        spread, onehot = [], []
        for j in range(8):
            at = pl.ds(i * 8 + j, 1)
            pos = pos_ref[at, :]
            here = slot_ids == jnp.right_shift(pos, 7)
            lane = jnp.bitwise_and(pos, LANES - 1)
            onehot.append(jnp.where(lane_ids == lane, 1.0, 0.0).astype(BF16))
            spread.append(
                jnp.concatenate(
                    [jnp.where(here, pairs_ref[h, at, :], 0.0).astype(BF16) for h in range(HEADS)], axis=0
                )
            )
        sums_ref[...] += dot_nt(jnp.concatenate(spread, axis=1), jnp.concatenate(onehot, axis=1))
        return carry

    lax.fori_loop(0, ROWS // 8, rows, 0)
    grad_bias_ref[...] = sums_ref[...].astype(BF16)


def block(*args):
    shapes = [
        ((WT, C), BF16),
        ((WT, C), BF16),
        ((GROWS, LANES), BF16),
        ((HEADS * 32, LANES), BF16),
    ]
    return pl.pallas_call(
        block_kernel,
        out_shape=[jax.ShapeDtypeStruct(s, d) for s, d in shapes],
        scratch_shapes=[
            pltpu.VMEM((HEADS * WT, WT), F32),
            pltpu.VMEM((HEADS * WT, WT), F32),
            pltpu.VMEM((HEADS * WT, WT), BF16),
            pltpu.VMEM((HEADS, ROWS, LANES), F32),
            pltpu.VMEM((HEADS * 32, LANES), F32),
        ],
        name="block",
        compiler_params=pltpu.CompilerParams(vmem_limit_bytes=24 * 1024 * 1024),
        cost_estimate=pl.CostEstimate(flops=2_000_000_000, bytes_accessed=5_000_000, transcendentals=300_000),
    )(*args)


def unpack_kernel(grads_ref, gain_one_ref, gain_two_ref, qkv_ref, proj_ref, up_ref, down_ref):
    factor = TOKENS ** (-0.5)

    def rows(start, count):
        return grads_ref[start : start + count].astype(F32) * factor

    for t in range(6):
        up_ref[:, LANES * t : LANES * (t + 1)] = rows(C * t, C)
    half = rows(1920, 384)
    down_ref[:, :LANES] = rows(1152, 768)
    down_ref[:384, LANES:] = half[:, :64]
    down_ref[384:, LANES:] = half[:, 64:]
    full = [rows(2304 + C * k, C) for k in range(4)]
    halves = [rows(3072 + C * k, C) for k in range(2)]
    query, key, value, proj = [
        jnp.concatenate((full[k], halves[k // 2][:, 64 * (k % 2) : 64 * (k % 2 + 1)]), axis=1) for k in range(4)
    ]
    qkv_ref[...] = jnp.concatenate((query, key, value), axis=1)
    proj_ref[...] = proj
    gains = rows(3456, 16)
    for k, ref in enumerate((gain_one_ref, gain_two_ref)):
        ref[...] = jnp.concatenate((gains[k : k + 1], gains[k + 2 : k + 3, : C - LANES]), axis=1)


def unpack(grads):
    shapes = [(1, C), (1, C), (C, 3 * C), (C, C), (C, HID), (HID, C)]
    return pl.pallas_call(
        unpack_kernel,
        out_shape=[jax.ShapeDtypeStruct(s, F32) for s in shapes],
        name="unpack",
        compiler_params=pltpu.CompilerParams(vmem_limit_bytes=16 * 1024 * 1024),
        cost_estimate=pl.CostEstimate(flops=500_000, bytes_accessed=2_700_000, transcendentals=0),
    )(grads)


def neighbours(by):
    lat, lon = lax.axis_size("lat"), lax.axis_size("lon")
    return [
        (i * lon + j, (i + by) % lat * lon + (j + by) % lon) for i in range(lat) for j in range(lon)
    ]


def ring(axis, by):
    peers = lax.axis_size(axis)
    return [(i, (i + by) % peers) for i in range(peers)]


def shift_in(grid):
    from_lat = lax.ppermute(grid[:, :, :3, 6:], "lat", ring("lat", -1))
    from_lon = lax.ppermute(grid[:, :, 3:, :6], "lon", ring("lon", -1))
    from_both = lax.ppermute(grid[:, :, :3, :6], ("lat", "lon"), neighbours(-1))
    top = jnp.concatenate((grid[:, :, 3:, 6:], from_lon), axis=3)
    low = jnp.concatenate((from_lat, from_both), axis=3)
    return jnp.concatenate((top, low), axis=2)[:, ::-1]


def shift_out(grid, between):
    rows_got = lax.ppermute(grid[:, :, 3:], "lat", ring("lat", 1))
    between(0)
    grid = jnp.concatenate((rows_got, grid[:, :, :3]), axis=2)
    cols_got = lax.ppermute(grid[:, :, :, 6:], "lon", ring("lon", 1))
    between(1)
    return jnp.concatenate((cols_got, grid[:, :, :, :6]), axis=3)


def spread_over(axis, groups=None):
    return lambda parts: lax.all_to_all(parts, axis, 0, 0, axis_index_groups=groups)


def total(parts):
    return jnp.sum(parts.astype(F32), axis=0).astype(BF16)


def reduce_grads(grads, local_bias):
    lat, lon = lax.axis_size("lat"), lax.axis_size("lon")
    far = 4
    near = lon // far
    over_near = spread_over("lon", [[n * far + f for n in range(near)] for f in range(far)])
    over_far = spread_over("lon", [[n * far + f for f in range(far)] for n in range(near)])
    over_lat = spread_over("lat")

    def same(part, count):
        return jnp.broadcast_to(part[None], (count,) + part.shape)

    share = GROWS // lat
    mine = total(over_lat(grads.reshape(lat, share, LANES)))
    both = jnp.concatenate((mine, local_bias), axis=0)
    part = total(over_near(both.reshape(near, -1, LANES)))
    part = total(over_far(same(part, far)))
    both = over_near(same(part, near)).reshape(both.shape)
    grads = over_lat(same(both[:share], lat)).reshape(GROWS, LANES)
    return grads, both[share:]


def local(
    tokens,
    gain_one,
    gain_two,
    qkv_weight,
    proj_weight,
    up_weight,
    down_weight,
    bias_table,
    pos_index,
    mask_ids,
    cotangent,
):
    grid = tokens.shape
    moved = shift_in(jnp.stack((tokens, cotangent)))
    pos_flat = flat_pairs(pos_index)
    table = jnp.pad(bias_table.reshape(HEADS, NPOS), ((0, 0), (0, SLOTS * LANES - NPOS)))
    bias = bias_pairs(table.reshape(HEADS, SLOTS, LANES), pos_flat)
    weights = qkv_weight.reshape(C, 3, C).transpose(1, 0, 2)
    out, delta, grads, local_bias = block(
        moved[0].reshape(WT, C),
        moved[1].reshape(WT, C),
        gain_one.reshape(1, C),
        gain_two.reshape(1, C),
        weights,
        proj_weight,
        up_weight,
        down_weight,
        bias,
        mask_ids.reshape(1, WT),
        mask_ids.reshape(WT, 1),
        pos_flat,
    )
    back = shift_out(jnp.stack((out, delta)).reshape((2,) + grid)[:, ::-1], lambda stage: None)
    local_bias = local_bias.reshape(HEADS, 32, LANES)[:, :SLOTS].reshape(HEADS * SLOTS, LANES)
    grads, grad_bias = reduce_grads(grads, jnp.pad(local_bias, ((0, BROWS - HEADS * SLOTS), (0, 0))))
    totals = unpack(grads)
    grad_bias = grad_bias[: HEADS * SLOTS].reshape(HEADS, SLOTS * LANES)[:, :NPOS].astype(F32)
    return (
        back[0],
        back[1],
        totals[0].reshape(C),
        totals[1].reshape(C),
        *totals[2:],
        grad_bias.reshape(HEADS, 1, 1, NPOS),
    )


def solution(mesh):
    in_specs = (
        P(None, "lat", "lon", None),
        P(),
        P(),
        P(),
        P(),
        P(),
        P(),
        P(None, None, "lat", None),
        P(),
        P(None, "lat", "lon"),
        P(None, "lat", "lon", None),
    )
    out_specs = (
        P(None, "lat", "lon", None),
        P(None, "lat", "lon", None),
        P(),
        P(),
        P(),
        P(),
        P(),
        P(),
        P(None, None, "lat", None),
    )
    return jax.shard_map(local, mesh=mesh, in_specs=in_specs, out_specs=out_specs, check_vma=False)
```

time: 709 us -> 138 us (0.19)
  blocking collectives: 268 us -> 21.5 us
  waiting for transfers between devices: 187 us -> 38.5 us
  other arithmetic: 126 us -> 1.65 us
  local copies, waits for them, and re-layouts: 65.9 us -> 11.8 us
  Pallas kernels: 0 us -> 17.1 us
  between operations: 14.8 us -> 0.98 us
  matrix products: 10.7 us -> 0 us
  starting transfers between devices: 36.1 us -> 44 us
    psum x2 -> x0, blocking collectives: 268 us -> none  [the longest x1 144 us: local(): lax.psum(local_bias.astype(jnp.bfloat16), 'lon').astype(jnp.float32)]
    psum x1 -> x0, waiting for transfers between devices: 175 us -> none  [local(): lax.psum((grad_gain_one, grad_gain_two, grad_qkv, grad_proj, grad_up, gra...]
    scatter-add x1 -> x0, other arithmetic: 113 us -> none  [table_grad(): jax.ops.segment_sum(flattened, pos_index.reshape(-1), num_segments=NPOS)]
    gather x2 -> x0, local copies, waits for them, and re-layouts: 50.3 us -> none  [bias_pairs(): picked = jnp.take(bias_table, pos_index.reshape(-1), axis=3)]
    all_to_all x0 -> x3, waiting for transfers between devices: none -> 21.9 us  [spread_over(): lax.all_to_all(parts, axis, 0, 0, axis_index_groups=groups)]
    all_to_all x0 -> x2, blocking collectives: none -> 21.5 us  [spread_over(): lax.all_to_all(parts, axis, 0, 0, axis_index_groups=groups)]
    pallas_call x0 -> x3, Pallas kernels: none -> 17.1 us  [the longest x1 10.5 us: block(): pl.pallas_call(block_kernel, out_shape=[jax.ShapeDtypeStruct(s, d) for s,...]
    all_to_all x0 -> x3, starting transfers between devices: none -> 17 us  [spread_over(): lax.all_to_all(parts, axis, 0, 0, axis_index_groups=groups)]
  transfers between devices with their start and end apart: 9 -> 8, of which waited for: 4 -> 4; matrix products, arithmetic and copies ran while one was open for 26% -> 2% of each run, Pallas kernels for 0% -> 4%
where the time goes in v1:
time: 138 us; the launch traced here: 135 us
  starting transfers between devices  44 us (32%)
  waiting for transfers between devices  38.5 us (28%)
  blocking collectives  21.5 us (16%)
  Pallas kernels  17.1 us (12%)
  local copies, waits for them, and re-layouts  11.8 us (9%)
  other arithmetic  1.65 us (1%)
    all_to_all x3, waiting for transfers between devices, spread_over(): lax.all_to_all(parts, axis, 0, 0, axis_index_groups=groups)  21.9 us
    all_to_all x2, blocking collectives, spread_over(): lax.all_to_all(parts, axis, 0, 0, axis_index_groups=groups)  21.5 us
    all_to_all x3, starting transfers between devices, spread_over(): lax.all_to_all(parts, axis, 0, 0, axis_index_groups=groups)  17 us
    ppermute x1, starting transfers between devices, shift_in(): from_lon = lax.ppermute(grid[:, :, 3:, :6], 'lon', ring('lon', -1))  14.4 us
    pallas_call x1, Pallas kernels, block(): pl.pallas_call(block_kernel, out_shape=[jax.ShapeDtypeStruct(s, d) for s,...  10.5 us
    ppermute x1, waiting for transfers between devices, shift_out(): rows_got = lax.ppermute(grid[:, :, 3:], 'lat', ring('lat', 1))  8.36 us
    ppermute x1, waiting for transfers between devices, shift_out(): cols_got = lax.ppermute(grid[:, :, :, 6:], 'lon', ring('lon', 1))  8.25 us
    unnamed x25, local copies, waits for them, and re-layouts  6.79 us
  transfers between devices with their start and end apart: 8, of which 4 were waited for; matrix products, arithmetic and copies ran while one was open for 2% of the time, Pallas kernels for 4%

profile of v1, /device:TPU:1, one launch (start us, length us, event | category | flops | bytes accessed | tf_op | source)
XLA Modules:
  0.0 135.5 jit_solution(15109873060637205949)
XLA Ops:
  0.6 1.1 fusion.5
  1.7 14.4 %collective-permute-start = (bf16[2,2,3,6,192]{4,1,3,2,0:T(2,128)(2,1)S(1)}, bf16[2,2,3,6,192]{4,1,3,2,0:T(2,128)(2,1)S(1)}, u32[]{:S(2)}, u32[]{:S(2)}) collective-permute-start(bf16[2,2,3,6,192]{4,1,3,2,0:T(2,128)(2,1)S(1)} %get-tuple-element.63), channel_id=1, source_target_pairs={{0,31},{1,0},{2,1},{3,2},{4,3},{5,4},{6,5},{7,6},{8,7},{9,8},{10,9... | collective-permute-start | bytes 82952 | tf_op jit(solution)/shard_map/ppermute | solution.py:314
  16.1 3.0 %collective-permute-start.2 = (bf16[2,2,3,6,192]{4,1,3,2,0:T(2,128)(2,1)S(1)}, bf16[2,2,3,6,192]{4,1,3,2,0:T(2,128)(2,1)S(1)}, u32[]{:S(2)}, u32[]{:S(2)}) collective-permute-start(bf16[2,2,3,6,192]{4,1,3,2,0:T(2,128)(2,1)S(1)} %get-tuple-element.64), channel_id=1, source_target_pairs={{0,511},{1,480},{2,481},{3,482},{4,483},{5,484},{6,485},{7,486},{8... | collective-permute-start | bytes 82952 | tf_op jit(solution)/shard_map/ppermute | solution.py:315
  19.2 3.8 %collective-permute-start.1 = (bf16[2,2,3,6,192]{4,1,3,2,0:T(2,128)(2,1)S(1)}, bf16[2,2,3,6,192]{4,1,3,2,0:T(2,128)(2,1)S(1)}, u32[]{:S(2)}, u32[]{:S(2)}) collective-permute-start(bf16[2,2,3,6,192]{4,1,3,2,0:T(2,128)(2,1)S(1)} %get-tuple-element.65), channel_id=1, source_target_pairs={{0,480},{32,0},{64,32},{96,64},{128,96},{160,128},{192,160},{224,1... | collective-permute-start | bytes 82952 | tf_op jit(solution)/shard_map/ppermute | solution.py:313
  23.1 0.9 slice-done.1
  24.0 0.7 copy-done.7
  24.8 0.7 copy-done.6
  25.6 0.9 copy-done.5
  26.8 0.8 copy-done.4
  27.8 5.4 %bias_pairs.1.bias_ref = f32[864,144]{1,0:T(8,128)S(1)} custom-call(f32[6,26,128]{2,1,0:T(8,128)S(1)} %reshape.84.table_ref, s32[176,128]{1,0:T(8,128)S(1)} %pad_add_fusion.pos_ref), custom_call_target="tpu_custom_call" | custom-call | flops 10000000 | bytes 1200000 | tf_op jit(solution)/shard_map/bias_pairs/pallas_call | solution.py:82
  33.6 0.4 slice.81
  34.1 0.4 slice.79
  35.0 0.5 copy-done.1
  35.5 10.5 %block.1 = (bf16[144,192]{1,0:T(8,128)(2,1)S(1)}, bf16[144,192]{1,0:T(8,128)(2,1)S(1)}, bf16[3584,128]{1,0:T(8,128)(2,1)}, bf16[192,128]{1,0:T(8,128)(2,1)S(1)}) custom-call(bf16[144,192]{1,0:T(8,128)(2,1)S(1)} %reshape_squeeze.6.x_ref, bf16[144,192]{1,0:T(8,128)(2,1)S(1)} %reshape_squeeze.7.cot_ref, f32[1,192]{1,0:T(1,128)S(1)} %bitcast.25, ...), custom_call_target="tpu_custom_call" | custom-call | flops 2000000000 | bytes 5000000 | tf_op jit(solution)/shard_map/block/pallas_call | solution.py:249
  45.9 5.4 %all-to-all-start = ((bf16[16,224,128]{2,1,0:T(8,128)(2,1)}), bf16[16,224,128]{2,1,0:T(8,128)(2,1)S(1)}, u32[]{:S(2)}, u32[]{:S(2)}) async-start(bf16[16,224,128]{2,1,0:T(8,128)(2,1)} %bitcast.9), calls=%async_computation | async-start | bytes 1835008 | tf_op jit(solution)/shard_map/all_to_all | solution.py:331
  51.4 14.5 %all-to-all-done = bf16[16,224,128]{2,1,0:T(8,128)(2,1)S(1)} async-done(((bf16[16,224,128]{2,1,0:T(8,128)(2,1)}), bf16[16,224,128]{2,1,0:T(8,128)(2,1)S(1)}, u32[]{:S(2)}, u32[]{:S(2)}) %all-to-all-start) | async-done | bytes 917536 | tf_op jit(solution)/shard_map/all_to_all | solution.py:331
  66.0 11.4 %all_to_all.25 = bf16[8,48,128]{2,1,0:T(8,128)(2,1)S(1)} all-to-all(bf16[8,48,128]{2,1,0:T(8,128)(2,1)S(1)} %bitcast.31), channel_id=1, replica_groups={{0,4,8,12,16,20,24,28},{1,5,9,13,17,21,25,29},{2,6,10,14,18,22,26,30},{..., dimensions={0} | all-to-all | bytes 196608 | tf_op jit(solution)/shard_map/all_to_all | solution.py:331
  77.4 10.1 %all_to_all.26 = bf16[4,48,128]{2,1,0:T(8,128)(2,1)S(1)} all-to-all(bf16[4,48,128]{2,1,0:T(8,128)(2,1)S(1)} %broadcast_in_dim.6), channel_id=1, replica_groups={{0,1,2,3},{4,5,6,7},{8,9,10,11},{12,13,14,15},{16,17,18,19},{20,21,22,2..., dimensions={0} | all-to-all | bytes 98304 | tf_op jit(solution)/shard_map/all_to_all | solution.py:331
  87.5 0.7 broadcast_in_dim.7
  88.2 3.4 %all-to-all-start.3 = ((bf16[8,48,128]{2,1,0:T(8,128)(2,1)}), bf16[8,48,128]{2,1,0:T(8,128)(2,1)S(1)}, u32[]{:S(2)}, u32[]{:S(2)}) async-start(bf16[8,48,128]{2,1,0:T(8,128)(2,1)} %broadcast_in_dim.7), calls=%async_computation.3 | async-start | bytes 196608 | tf_op jit(solution)/shard_map/all_to_all | solution.py:331
  91.6 7.4 %all-to-all-done.3 = bf16[8,48,128]{2,1,0:T(8,128)(2,1)S(1)} async-done(((bf16[8,48,128]{2,1,0:T(8,128)(2,1)}), bf16[8,48,128]{2,1,0:T(8,128)(2,1)S(1)}, u32[]{:S(2)}, u32[]{:S(2)}) %all-to-all-start.3) | async-done | bytes 98336 | tf_op jit(solution)/shard_map/all_to_all | solution.py:331
  99.1 1.1 broadcast_in_dim.8
  100.1 8.2 %all-to-all-start.4 = ((bf16[16,224,128]{2,1,0:T(8,128)(2,1)}), bf16[16,224,128]{2,1,0:T(8,128)(2,1)S(1)}, u32[]{:S(2)}, u32[]{:S(2)}) async-start(bf16[16,224,128]{2,1,0:T(8,128)(2,1)} %broadcast_in_dim.8), calls=%async_computation.4 | async-start | bytes 1835008 | tf_op jit(solution)/shard_map/all_to_all | solution.py:331
  108.4 3.5 %collective-permute-start.3 = (bf16[2,2,3,12,192]{4,3,2,1,0:T(8,128)(2,1)S(1)}, bf16[2,2,3,12,192]{4,3,2,1,0:T(8,128)(2,1)S(1)}, u32[]{:S(2)}, u32[]{:S(2)}) collective-permute-start(bf16[2,2,3,12,192]{4,3,2,1,0:T(8,128)(2,1)S(1)} %slice.87), channel_id=1, source_target_pairs={{0,32},{32,64},{64,96},{96,128},{128,160},{160,192},{192,224},{224... | collective-permute-start | bytes 165896 | tf_op jit(solution)/shard_map/ppermute | solution.py:322
  112.0 8.4 %collective-permute-done.3 = bf16[2,2,3,12,192]{4,3,2,1,0:T(8,128)(2,1)S(1)} collective-permute-done((bf16[2,2,3,12,192]{4,3,2,1,0:T(8,128)(2,1)S(1)}, bf16[2,2,3,12,192]{4,3,2,1,0:T(8,128)(2,1)S(1)}, u32[]{:S(2)}, u32[]{:S(2)}) %collective-permute-start.3) | collective-permute-done | bytes 55328 | tf_op jit(solution)/shard_map/ppermute | solution.py:322
  120.4 2.2 %collective-permute-start.4 = (bf16[2,2,6,6,192]{4,3,2,1,0:T(8,128)(2,1)S(1)}, bf16[2,2,6,6,192]{4,3,2,1,0:T(8,128)(2,1)S(1)}, u32[]{:S(2)}, u32[]{:S(2)}) collective-permute-start(bf16[2,2,6,6,192]{4,3,2,1,0:T(8,128)(2,1)S(1)} %fusion.3), channel_id=1, source_target_pairs={{0,1},{1,2},{2,3},{3,4},{4,5},{5,6},{6,7},{7,8},{8,9},{9,10},{10,1... | collective-permute-start | bytes 165896 | tf_op jit(solution)/shard_map/ppermute | solution.py:325
  122.6 8.2 %collective-permute-done.4 = bf16[2,2,6,6,192]{4,3,2,1,0:T(8,128)(2,1)S(1)} collective-permute-done((bf16[2,2,6,6,192]{4,3,2,1,0:T(8,128)(2,1)S(1)}, bf16[2,2,6,6,192]{4,3,2,1,0:T(8,128)(2,1)S(1)}, u32[]{:S(2)}, u32[]{:S(2)}) %collective-permute-start.4) | collective-permute-done | bytes 55328 | tf_op jit(solution)/shard_map/ppermute | solution.py:325
  131.0 0.7 copy.51
  131.7 0.7 copy.50
  132.5 0.7 reshape.99
  133.2 1.2 unpack.1
  134.4 1.1 copy.52
  (57 shorter events, 2.2 us)
Async XLA Ops:
  1.7 31.5 %collective-permute-start = (bf16[2,2,3,6,192]{4,1,3,2,0:T(2,128)(2,1)S(1)}, bf16[2,2,3,6,192]{4,1,3,2,0:T(2,128)(2,1)S(1)}, u32[]{:S(2)}, u32[]{:S(2)}) collective-permute-start(bf16[2,2,3,6,192]{4,1,3,2,0:T(2,128)(2,1)S(1)} %get-tuple-element.63), channel_id=1, source_target_pairs={{0,31},{1,0},{2,1},{3,2},{4,3},{5,4},{6,5},{7,6},{8,7},{9,8},{10,9... | collective-permute-start | bytes 82952 | tf_op jit(solution)/shard_map/ppermute | solution.py:314
  16.1 17.1 %collective-permute-start.2 = (bf16[2,2,3,6,192]{4,1,3,2,0:T(2,128)(2,1)S(1)}, bf16[2,2,3,6,192]{4,1,3,2,0:T(2,128)(2,1)S(1)}, u32[]{:S(2)}, u32[]{:S(2)}) collective-permute-start(bf16[2,2,3,6,192]{4,1,3,2,0:T(2,128)(2,1)S(1)} %get-tuple-element.64), channel_id=1, source_target_pairs={{0,511},{1,480},{2,481},{3,482},{4,483},{5,484},{6,485},{7,486},{8... | collective-permute-start | bytes 82952 | tf_op jit(solution)/shard_map/ppermute | solution.py:315
  19.1 3.8 %slice-start = ((s32[144,144]{1,0:T(8,128)}), s32[144,16]{1,0:T(8,128)S(1)}, s32[]{:S(2)}) async-start(s32[144,144]{1,0:T(8,128)} %param.19), calls=%async_computation.5 | async-start | bytes 147456 | tf_op jit(solution)/shard_map/slice | solution.py:93
  19.2 14.1 %collective-permute-start.1 = (bf16[2,2,3,6,192]{4,1,3,2,0:T(2,128)(2,1)S(1)}, bf16[2,2,3,6,192]{4,1,3,2,0:T(2,128)(2,1)S(1)}, u32[]{:S(2)}, u32[]{:S(2)}) collective-permute-start(bf16[2,2,3,6,192]{4,1,3,2,0:T(2,128)(2,1)S(1)} %get-tuple-element.65), channel_id=1, source_target_pairs={{0,480},{32,0},{64,32},{96,64},{128,96},{160,128},{192,160},{224,1... | collective-permute-start | bytes 82952 | tf_op jit(solution)/shard_map/ppermute | solution.py:313
  23.0 0.9 slice-start.1
  23.9 0.7 copy-start.7
  24.6 0.9 copy-start.6
  25.5 0.9 copy-start.5
  26.7 1.0 copy-start.4
  34.1 1.0 copy-start
  34.6 0.9 copy-start.1
  34.6 0.9 copy-start.3
  34.6 0.9 copy-start.2
  45.9 19.9 %all-to-all-start = ((bf16[16,224,128]{2,1,0:T(8,128)(2,1)}), bf16[16,224,128]{2,1,0:T(8,128)(2,1)S(1)}, u32[]{:S(2)}, u32[]{:S(2)}) async-start(bf16[16,224,128]{2,1,0:T(8,128)(2,1)} %bitcast.9), calls=%async_computation | async-start | bytes 1835008 | tf_op jit(solution)/shard_map/all_to_all | solution.py:331
  88.2 10.9 %all-to-all-start.3 = ((bf16[8,48,128]{2,1,0:T(8,128)(2,1)}), bf16[8,48,128]{2,1,0:T(8,128)(2,1)S(1)}, u32[]{:S(2)}, u32[]{:S(2)}) async-start(bf16[8,48,128]{2,1,0:T(8,128)(2,1)} %broadcast_in_dim.7), calls=%async_computation.3 | async-start | bytes 196608 | tf_op jit(solution)/shard_map/all_to_all | solution.py:331
  100.1 33.1 %all-to-all-start.4 = ((bf16[16,224,128]{2,1,0:T(8,128)(2,1)}), bf16[16,224,128]{2,1,0:T(8,128)(2,1)S(1)}, u32[]{:S(2)}, u32[]{:S(2)}) async-start(bf16[16,224,128]{2,1,0:T(8,128)(2,1)} %broadcast_in_dim.8), calls=%async_computation.4 | async-start | bytes 1835008 | tf_op jit(solution)/shard_map/all_to_all | solution.py:331
  108.4 11.9 %collective-permute-start.3 = (bf16[2,2,3,12,192]{4,3,2,1,0:T(8,128)(2,1)S(1)}, bf16[2,2,3,12,192]{4,3,2,1,0:T(8,128)(2,1)S(1)}, u32[]{:S(2)}, u32[]{:S(2)}) collective-permute-start(bf16[2,2,3,12,192]{4,3,2,1,0:T(8,128)(2,1)S(1)} %slice.87), channel_id=1, source_target_pairs={{0,32},{32,64},{64,96},{96,128},{128,160},{160,192},{192,224},{224... | collective-permute-start | bytes 165896 | tf_op jit(solution)/shard_map/ppermute | solution.py:322
  120.4 10.5 %collective-permute-start.4 = (bf16[2,2,6,6,192]{4,3,2,1,0:T(8,128)(2,1)S(1)}, bf16[2,2,6,6,192]{4,3,2,1,0:T(8,128)(2,1)S(1)}, u32[]{:S(2)}, u32[]{:S(2)}) collective-permute-start(bf16[2,2,6,6,192]{4,3,2,1,0:T(8,128)(2,1)S(1)} %fusion.3), channel_id=1, source_target_pairs={{0,1},{1,2},{2,3},{3,4},{4,5},{5,6},{6,7},{7,8},{8,9},{9,10},{10,1... | collective-permute-start | bytes 165896 | tf_op jit(solution)/shard_map/ppermute | solution.py:325

commit v2 on v1

v2 whole, which is shorter than its diff:
```python
import jax
import jax.numpy as jnp
from jax import lax
from jax.experimental import pallas as pl
from jax.experimental.pallas import tpu as pltpu
from jax.sharding import PartitionSpec as P

HEADS = 6
WT = 144
NPOS = 3312
C = 192
HID = 768
HEAD = C // HEADS
SLOTS = 26
LANES = 128
TOKENS = 73728
TAIL = WT - LANES
ROWS = WT + 2 * TAIL
GROWS = 3584
BROWS = 160
EPS = 1e-05
F32 = jnp.float32
BF16 = jnp.bfloat16


def dot(a, b):
    return lax.dot_general(a, b, (((1,), (0,)), ((), ())), preferred_element_type=F32)


def dot_nt(a, b):
    return lax.dot_general(a, b, (((1,), (1,)), ((), ())), preferred_element_type=F32)


def dot_tn(a, b):
    return lax.dot_general(a, b, (((0,), (0,)), ((), ())), preferred_element_type=F32)


def norm_stats(widened):
    center = widened - jnp.mean(widened, axis=-1, keepdims=True)
    spread = jnp.mean(center * center, axis=-1, keepdims=True)
    inverse = lax.rsqrt(spread + EPS)
    return center * inverse, inverse


def norm_back(delta_hidden, normal, inverse, gain):
    grad_gain = jnp.sum(delta_hidden * normal, axis=0, keepdims=True)
    delta_normal = delta_hidden * gain
    delta_input = inverse * (
        delta_normal
        - jnp.mean(delta_normal, axis=-1, keepdims=True)
        - normal * jnp.mean(delta_normal * normal, axis=-1, keepdims=True)
    )
    return delta_input, grad_gain


def gather_kernel(table_ref, pos_ref, mask_ref, bias_ref, flat_pos_ref, slots_ref, flat_ref):
    half = WT // 2
    pos = pos_ref[...]
    pos = jnp.concatenate((pos[half:], pos[:half]), axis=0)
    pos = jnp.concatenate((pos[:, half:], pos[:, :half]), axis=1)
    turned = pos[:, LANES:].T
    flat_pos_ref[:WT] = pos[:, :LANES]
    flat_pos_ref[WT : WT + TAIL] = turned[:, :LANES]
    flat_pos_ref[WT + TAIL :] = jnp.zeros((TAIL, LANES), jnp.int32)
    flat_pos_ref[WT + TAIL :, :TAIL] = turned[:, LANES:]
    for h in range(HEADS):
        for g in range(SLOTS):
            count = min(LANES, NPOS - g * LANES)
            slots_ref[h, g : g + 1, :count] = table_ref[h, :, g * LANES : g * LANES + count]

    def rows(i, carry):
        at = pl.ds(pl.multiple_of(i * 8, 8), 8)
        pos = flat_pos_ref[at, :]
        lane = jnp.bitwise_and(pos, LANES - 1)
        slot = jnp.right_shift(pos, 7)
        held = [jnp.zeros((8, LANES), F32)] * HEADS
        for g in range(SLOTS):
            here = slot == g
            for h in range(HEADS):
                row = jnp.broadcast_to(slots_ref[h, g : g + 1, :], (8, LANES))
                got = jnp.take_along_axis(row, lane, axis=1)
                held[h] = jnp.where(here, got, held[h])
        for h in range(HEADS):
            flat_ref[h, at, :] = held[h]
        return carry

    lax.fori_loop(0, ROWS // 8, rows, 0)
    mask = jnp.broadcast_to(mask_ref[...], (WT, WT))
    allowed = mask == mask.T
    for h in range(HEADS):
        tail = jnp.concatenate((flat_ref[h, WT : WT + TAIL, :].T, flat_ref[h, WT + TAIL :, :].T[:TAIL]), axis=0)
        at = pl.ds(h * WT, WT)
        bias_ref[at, :LANES] = jnp.where(allowed[:, :LANES], flat_ref[h, :WT, :], -1e30)
        bias_ref[at, LANES:] = jnp.where(allowed[:, LANES:], tail, -1e30)


def bias_pairs(table, pos_index, mask_row):
    return pl.pallas_call(
        gather_kernel,
        out_shape=[jax.ShapeDtypeStruct((HEADS * WT, WT), F32), jax.ShapeDtypeStruct((ROWS, LANES), jnp.int32)],
        scratch_shapes=[pltpu.VMEM((HEADS, SLOTS, LANES), F32), pltpu.VMEM((HEADS, ROWS, LANES), F32)],
        name="bias_pairs",
        compiler_params=pltpu.CompilerParams(vmem_limit_bytes=16 * 1024 * 1024),
        cost_estimate=pl.CostEstimate(flops=10_000_000, bytes_accessed=1_200_000, transcendentals=0),
    )(table, pos_index, mask_row)


def scatter_kernel(pairs_ref, pos_ref, out_ref, sums_ref, packed_ref):
    sums_ref[...] = jnp.zeros_like(sums_ref)
    slot_ids = lax.broadcasted_iota(jnp.int32, (32, LANES), 0)
    lane_ids = lax.broadcasted_iota(jnp.int32, (LANES, LANES), 0)

    def rows(i, carry):
        spread, onehot = [], []
        for j in range(8):
            at = pl.ds(i * 8 + j, 1)
            pos = pos_ref[at, :]
            here = slot_ids == jnp.right_shift(pos, 7)
            lane = jnp.bitwise_and(pos, LANES - 1)
            onehot.append(jnp.where(lane_ids == lane, 1.0, 0.0).astype(BF16))
            spread.append(
                jnp.concatenate(
                    [jnp.where(here, pairs_ref[h, at, :], 0.0).astype(BF16) for h in range(HEADS)], axis=0
                )
            )
        sums_ref[...] += dot_nt(jnp.concatenate(spread, axis=1), jnp.concatenate(onehot, axis=1))
        return carry

    lax.fori_loop(0, ROWS // 8, rows, 0)
    packed_ref[...] = jnp.zeros_like(packed_ref)
    for h in range(HEADS):
        packed_ref[h * SLOTS : (h + 1) * SLOTS] = sums_ref[h * 32 : h * 32 + SLOTS]
    out_ref[...] = packed_ref[...].astype(BF16)


def bias_grad(pairs, pos_flat):
    return pl.pallas_call(
        scatter_kernel,
        out_shape=jax.ShapeDtypeStruct((BROWS, LANES), BF16),
        scratch_shapes=[pltpu.VMEM((HEADS * 32, LANES), F32), pltpu.VMEM((BROWS, LANES), F32)],
        name="bias_grad",
        compiler_params=pltpu.CompilerParams(vmem_limit_bytes=16 * 1024 * 1024),
        cost_estimate=pl.CostEstimate(flops=1_100_000_000, bytes_accessed=700_000, transcendentals=0),
    )(pairs, pos_flat)


def block_kernel(
    x_ref,
    cot_ref,
    gain_one_ref,
    gain_two_ref,
    qkv_ref,
    proj_ref,
    up_ref,
    down_ref,
    bias_ref,
    out_ref,
    delta_ref,
    grads_ref,
    pairs_ref,
    scores_ref,
    prob_ref,
    low_ref,
):
    factor = HEAD ** (-0.5)
    x = x_ref[...].astype(F32)
    gain_one = gain_one_ref[...]
    gain_two = gain_two_ref[...]
    normal_one, inverse_one = norm_stats(x)
    normed = (normal_one * gain_one).astype(BF16)
    packed = dot(normed, qkv_ref[...]).astype(BF16)
    queries, keys, values = packed[:, :C], packed[:, C : 2 * C], packed[:, 2 * C :]
    head_of = lax.broadcasted_iota(jnp.int32, (WT, C), 1) // HEAD

    def by_head(a):
        return jnp.concatenate([jnp.where(head_of == h, a, jnp.zeros_like(a)) for h in range(HEADS)], axis=0)

    def joined(a):
        out = a[:WT]
        for h in range(1, HEADS):
            out = jnp.where(head_of == h, a[h * WT : (h + 1) * WT], out)
        return out

    queries_by = by_head(queries)
    scores_ref[...] = dot_nt(queries_by, keys)
    for h in range(HEADS):
        at = pl.ds(h * WT, WT)
        scores = scores_ref[at, :] * factor + bias_ref[at, :]
        weight = jnp.exp(scores - jnp.max(scores, axis=-1, keepdims=True))
        prob = weight * (1.0 / jnp.sum(weight, axis=-1, keepdims=True))
        prob_ref[at, :] = prob
        low_ref[at, :] = prob.astype(BF16)
    mixture = joined(dot(low_ref[...], values)).astype(BF16)
    attention = dot(mixture, proj_ref[...]).astype(BF16)

    middle = (x + attention.astype(F32)).astype(BF16)
    widened = middle.astype(F32)
    normal_two, inverse_two = norm_stats(widened)
    normed_two = (normal_two * gain_two).astype(BF16)
    cot = cot_ref[...]
    up_proj = dot(normed_two, up_ref[...])
    cumulative = 0.5 * (1.0 + lax.erf(up_proj * 0.7071067811865476))
    density = jnp.exp(-0.5 * up_proj * up_proj) * 0.3989422804014327
    active = (up_proj * cumulative).astype(BF16)
    out_ref[...] = (widened + dot_nt(active, down_ref[...])).astype(BF16)
    grad_down = dot_tn(cot, active).astype(BF16)
    delta_act = dot(cot, down_ref[...])
    delta_up = (delta_act * (cumulative + up_proj * density)).astype(BF16)
    grad_up = dot_tn(normed_two, delta_up).astype(BF16)
    for t in range(6):
        grads_ref[C * t : C * (t + 1)] = grad_up[:, LANES * t : LANES * (t + 1)]
        grads_ref[C * (t + 6) : C * (t + 7)] = grad_down[:, LANES * t : LANES * (t + 1)]
    delta_hidden = dot_nt(delta_up, up_ref[...])
    delta_input, grad_gain_two = norm_back(delta_hidden, normal_two, inverse_two, gain_two)
    delta_middle = (cot.astype(F32) + delta_input).astype(BF16)

    grad_proj = dot_tn(mixture, delta_middle)
    mixture_by = by_head(dot_nt(delta_middle, proj_ref[...]).astype(BF16))
    delta_value = dot_tn(low_ref[...], mixture_by)
    scores_ref[...] = dot_nt(mixture_by, values)
    for h in range(HEADS):
        at = pl.ds(h * WT, WT)
        prob = prob_ref[at, :]
        delta_prob = scores_ref[at, :]
        scores = prob * (delta_prob - jnp.sum(delta_prob * prob, axis=-1, keepdims=True))
        low_ref[at, :] = scores.astype(BF16)
        turned = scores[:, LANES:].T
        pairs_ref[h, :WT, :] = scores[:, :LANES]
        pairs_ref[h, WT : WT + TAIL, :] = turned[:, :LANES]
        pairs_ref[h, WT + TAIL :, :] = jnp.zeros((TAIL, LANES), F32)
        pairs_ref[h, WT + TAIL :, :TAIL] = turned[:, LANES:]
    delta_query = joined(dot(low_ref[...], keys)) * factor
    delta_key = dot_tn(low_ref[...], queries_by) * factor
    delta_packed = jnp.concatenate((delta_query, delta_key, delta_value), axis=1).astype(BF16)
    delta_normed = dot_nt(delta_packed, qkv_ref[...])
    grad_qkv = dot_tn(normed, delta_packed)
    for t in range(4):
        grads_ref[C * (t + 12) : C * (t + 13)] = grad_qkv[:, LANES * t : LANES * (t + 1)].astype(BF16)
    grads_ref[C * 16 : C * 17] = grad_proj[:, :LANES].astype(BF16)
    grads_ref[C * 17 : C * 18] = jnp.concatenate((grad_qkv[:, 4 * LANES :], grad_proj[:, LANES:]), axis=1).astype(BF16)
    delta_normed = delta_normed.astype(BF16).astype(F32)
    delta_input, grad_gain_one = norm_back(delta_normed, normal_one, inverse_one, gain_one)
    delta_ref[...] = (delta_middle.astype(F32) + delta_input).astype(BF16)
    gains = jnp.concatenate((grad_gain_one, grad_gain_two), axis=0)
    wide = jnp.concatenate((gains, jnp.zeros((2, 2 * LANES - C), F32)), axis=1)
    grads_ref[C * 18 :] = jnp.concatenate(
        (wide[:, :LANES], wide[:, LANES:], jnp.zeros((124, LANES), F32)), axis=0
    ).astype(BF16)


def block(*args):
    shapes = [
        ((WT, C), BF16),
        ((WT, C), BF16),
        ((GROWS, LANES), BF16),
        ((HEADS, ROWS, LANES), F32),
    ]
    return pl.pallas_call(
        block_kernel,
        out_shape=[jax.ShapeDtypeStruct(s, d) for s, d in shapes],
        scratch_shapes=[
            pltpu.VMEM((HEADS * WT, WT), F32),
            pltpu.VMEM((HEADS * WT, WT), F32),
            pltpu.VMEM((HEADS * WT, WT), BF16),
        ],
        name="block",
        compiler_params=pltpu.CompilerParams(vmem_limit_bytes=24 * 1024 * 1024),
        cost_estimate=pl.CostEstimate(flops=900_000_000, bytes_accessed=4_000_000, transcendentals=300_000),
    )(*args)


def unpack_kernel(grads_ref, gain_one_ref, gain_two_ref, qkv_ref, proj_ref, up_ref, down_ref):
    factor = TOKENS ** (-0.5)

    def rows(start, count):
        return grads_ref[start : start + count].astype(F32) * factor

    for t in range(6):
        at = slice(LANES * t, LANES * (t + 1))
        up_ref[:, at] = rows(C * t, C)
        down_ref[:, at] = rows(C * (t + 6), C)
        if t < 4:
            qkv_ref[:, at] = rows(C * (t + 12), C)
    halves = rows(C * 17, C)
    qkv_ref[:, 4 * LANES :] = halves[:, :64]
    proj_ref[:, :LANES] = rows(C * 16, C)
    proj_ref[:, LANES:] = halves[:, 64:]
    gains = rows(C * 18, 16)
    for k, ref in enumerate((gain_one_ref, gain_two_ref)):
        ref[...] = jnp.concatenate((gains[k : k + 1], gains[k + 2 : k + 3, : C - LANES]), axis=1)


def unpack(grads):
    shapes = [(1, C), (1, C), (C, 3 * C), (C, C), (C, HID), (C, HID)]
    return pl.pallas_call(
        unpack_kernel,
        out_shape=[jax.ShapeDtypeStruct(s, F32) for s in shapes],
        name="unpack",
        compiler_params=pltpu.CompilerParams(vmem_limit_bytes=16 * 1024 * 1024),
        cost_estimate=pl.CostEstimate(flops=500_000, bytes_accessed=2_700_000, transcendentals=0),
    )(grads)


def neighbours(by):
    lat, lon = lax.axis_size("lat"), lax.axis_size("lon")
    return [
        (i * lon + j, (i + by) % lat * lon + (j + by) % lon) for i in range(lat) for j in range(lon)
    ]


def ring(axis, by):
    peers = lax.axis_size(axis)
    return [(i, (i + by) % peers) for i in range(peers)]


def shift_in(grid):
    from_lat = lax.ppermute(grid[:, :, :3, 6:], "lat", ring("lat", -1))
    from_lon = lax.ppermute(grid[:, :, 3:, :6], "lon", ring("lon", -1))
    from_both = lax.ppermute(grid[:, :, :3, :6], ("lat", "lon"), neighbours(-1))
    top = jnp.concatenate((grid[:, :, 3:, 6:], from_lon), axis=3)
    low = jnp.concatenate((from_lat, from_both), axis=3)
    return jnp.concatenate((top, low), axis=2)


def spread_over(axis, groups=None):
    return lambda parts: lax.all_to_all(parts, axis, 0, 0, axis_index_groups=groups)


def total(parts):
    return jnp.sum(parts.astype(F32), axis=0).astype(BF16)


def finish(grid, grads, pairs, pos_flat):
    lat, lon = lax.axis_size("lat"), lax.axis_size("lon")
    far = 4
    near = lon // far
    over_near = spread_over("lon", [[n * far + f for n in range(near)] for f in range(far)])
    over_far = spread_over("lon", [[n * far + f for f in range(far)] for n in range(near)])
    over_lat = spread_over("lat")

    def same(part, count):
        return jnp.broadcast_to(part[None], (count,) + part.shape)

    share = GROWS // lat
    mine = total(over_lat(grads.reshape(lat, share, LANES)))
    both = jnp.concatenate((mine, bias_grad(pairs, pos_flat)), axis=0)
    both, grid = lax.optimization_barrier((both, grid))
    rows_got = lax.ppermute(grid[:, :, 3:], "lat", ring("lat", 1))
    part = total(over_near(both.reshape(near, -1, LANES)))
    part = total(over_far(same(part, far)))
    part, rows_got = lax.optimization_barrier((part, rows_got))
    grid = jnp.concatenate((rows_got, grid[:, :, :3]), axis=2)
    cols_got = lax.ppermute(grid[:, :, :, 6:], "lon", ring("lon", 1))
    both = over_near(same(part, near)).reshape(both.shape)
    both, cols_got = lax.optimization_barrier((both, cols_got))
    grid = jnp.concatenate((cols_got, grid[:, :, :, :6]), axis=3)
    grads = over_lat(same(both[:share], lat)).reshape(GROWS, LANES)
    return grid, grads, both[share:]


def local(
    tokens,
    gain_one,
    gain_two,
    qkv_weight,
    proj_weight,
    up_weight,
    down_weight,
    bias_table,
    pos_index,
    mask_ids,
    cotangent,
):
    grid = tokens.shape
    moved = shift_in(jnp.stack((tokens, cotangent)))
    bias, pos_flat = bias_pairs(bias_table.reshape(HEADS, 1, NPOS), pos_index, mask_ids[::-1].reshape(1, WT))
    out, delta, grads, pairs = block(
        moved[0].reshape(WT, C),
        moved[1].reshape(WT, C),
        gain_one.reshape(1, C),
        gain_two.reshape(1, C),
        qkv_weight,
        proj_weight,
        up_weight,
        down_weight.T,
        bias,
    )
    back, grads, grad_bias = finish(jnp.stack((out, delta)).reshape((2,) + grid), grads, pairs, pos_flat)
    totals = unpack(grads)
    grad_bias = grad_bias[: HEADS * SLOTS].reshape(HEADS, SLOTS * LANES)[:, :NPOS].astype(F32)
    return (
        back[0],
        back[1],
        totals[0].reshape(C),
        totals[1].reshape(C),
        *totals[2:5],
        totals[5].T,
        grad_bias.reshape(HEADS, 1, 1, NPOS),
    )


def solution(mesh):
    in_specs = (
        P(None, "lat", "lon", None),
        P(),
        P(),
        P(),
        P(),
        P(),
        P(),
        P(None, None, "lat", None),
        P(),
        P(None, "lat", "lon"),
        P(None, "lat", "lon", None),
    )
    out_specs = (
        P(None, "lat", "lon", None),
        P(None, "lat", "lon", None),
        P(),
        P(),
        P(),
        P(),
        P(),
        P(),
        P(None, None, "lat", None),
    )
    return jax.shard_map(local, mesh=mesh, in_specs=in_specs, out_specs=out_specs, check_vma=False)
```

time: 138 us -> 118 us (0.86)
  blocking collectives: 21.5 us -> 11.4 us
  waiting for transfers between devices: 38.5 us -> 31.6 us
  local copies, waits for them, and re-layouts: 11.8 us -> 5.9 us
  starting transfers between devices: 44 us -> 47.5 us
    all_to_all x2 -> x1, blocking collectives: 21.5 us -> 11.4 us  [spread_over(): lax.all_to_all(parts, axis, 0, 0, axis_index_groups=groups)]
    ppermute x2, waiting for transfers between devices: 16.6 us -> 7.03 us  [the longest x1 7.03 us: finish(): cols_got = lax.ppermute(grid[:, :, :, 6:], 'lon', ring('lon', 1))]
    pallas_call x1 -> x2, Pallas kernels: 5.42 us -> 11.7 us  [the longest x1 6 us: bias_grad(): pl.pallas_call(scatter_kernel, out_shape=jax.ShapeDtypeStruct((BROWS, LAN...]
    pallas_call x1, Pallas kernels: 10.5 us -> 4.82 us  [block(): pl.pallas_call(block_kernel, out_shape=[jax.ShapeDtypeStruct(s, d) for s,...]
    unnamed x25 -> x20, local copies, waits for them, and re-layouts: 6.79 us -> 2.4 us
    all_to_all x3 -> x4, starting transfers between devices: 17 us -> 20.8 us  [spread_over(): lax.all_to_all(parts, axis, 0, 0, axis_index_groups=groups)]
    all_to_all x3 -> x4, waiting for transfers between devices: 21.9 us -> 24.6 us  [spread_over(): lax.all_to_all(parts, axis, 0, 0, axis_index_groups=groups)]
  transfers between devices with their start and end apart: 8 -> 9, of which waited for: 4 -> 4; matrix products, arithmetic and copies ran while one was open for 2% -> 2% of each run, Pallas kernels for 4% -> 10%
where the time goes in v2:
time: 118 us; the launch traced here: 117 us
  starting transfers between devices  47.5 us (40%)
  waiting for transfers between devices  31.6 us (27%)
  Pallas kernels  17.8 us (15%)
  blocking collectives  11.4 us (10%)
  local copies, waits for them, and re-layouts  5.9 us (5%)
  other arithmetic  1.72 us (1%)
    all_to_all x4, waiting for transfers between devices, spread_over(): lax.all_to_all(parts, axis, 0, 0, axis_index_groups=groups)  24.6 us
    all_to_all x4, starting transfers between devices, spread_over(): lax.all_to_all(parts, axis, 0, 0, axis_index_groups=groups)  20.8 us
    ppermute x1, starting transfers between devices, shift_in(): from_lon = lax.ppermute(grid[:, :, 3:, :6], 'lon', ring('lon', -1))  14.4 us
    all_to_all x1, blocking collectives, spread_over(): lax.all_to_all(parts, axis, 0, 0, axis_index_groups=groups)  11.4 us
    ppermute x1, waiting for transfers between devices, finish(): cols_got = lax.ppermute(grid[:, :, :, 6:], 'lon', ring('lon', 1))  7.03 us
    pallas_call x1, Pallas kernels, bias_grad(): pl.pallas_call(scatter_kernel, out_shape=jax.ShapeDtypeStruct((BROWS, LAN...  6 us
    pallas_call x1, Pallas kernels, bias_pairs(): pl.pallas_call(gather_kernel, out_shape=[jax.ShapeDtypeStruct((HEADS * WT...  5.65 us
    pallas_call x1, Pallas kernels, block(): pl.pallas_call(block_kernel, out_shape=[jax.ShapeDtypeStruct(s, d) for s,...  4.82 us
  transfers between devices with their start and end apart: 9, of which 4 were waited for; matrix products, arithmetic and copies ran while one was open for 2% of the time, Pallas kernels for 10%

profile of v2, /device:TPU:1, one launch (start us, length us, event | category | flops | bytes accessed | tf_op | source)
XLA Modules:
  0.0 116.9 jit_solution(13140105499040280553)
XLA Ops:
  0.7 1.1 fusion.3
  1.8 14.4 %collective-permute-start = (bf16[2,2,3,6,192]{4,1,3,2,0:T(2,128)(2,1)S(1)}, bf16[2,2,3,6,192]{4,1,3,2,0:T(2,128)(2,1)S(1)}, u32[]{:S(2)}, u32[]{:S(2)}) collective-permute-start(bf16[2,2,3,6,192]{4,1,3,2,0:T(2,128)(2,1)S(1)} %get-tuple-element.70), channel_id=1, source_target_pairs={{0,31},{1,0},{2,1},{3,2},{4,3},{5,4},{6,5},{7,6},{8,7},{9,8},{10,9... | collective-permute-start | bytes 82952 | tf_op jit(solution)/shard_map/ppermute | solution.py:318
  16.2 3.0 %collective-permute-start.2 = (bf16[2,2,3,6,192]{4,1,3,2,0:T(2,128)(2,1)S(1)}, bf16[2,2,3,6,192]{4,1,3,2,0:T(2,128)(2,1)S(1)}, u32[]{:S(2)}, u32[]{:S(2)}) collective-permute-start(bf16[2,2,3,6,192]{4,1,3,2,0:T(2,128)(2,1)S(1)} %get-tuple-element.71), channel_id=1, source_target_pairs={{0,511},{1,480},{2,481},{3,482},{4,483},{5,484},{6,485},{7,486},{8... | collective-permute-start | bytes 82952 | tf_op jit(solution)/shard_map/ppermute | solution.py:319
  19.2 3.7 %collective-permute-start.1 = (bf16[2,2,3,6,192]{4,1,3,2,0:T(2,128)(2,1)S(1)}, bf16[2,2,3,6,192]{4,1,3,2,0:T(2,128)(2,1)S(1)}, u32[]{:S(2)}, u32[]{:S(2)}) collective-permute-start(bf16[2,2,3,6,192]{4,1,3,2,0:T(2,128)(2,1)S(1)} %get-tuple-element.72), channel_id=1, source_target_pairs={{0,480},{32,0},{64,32},{96,64},{128,96},{160,128},{192,160},{224,1... | collective-permute-start | bytes 82952 | tf_op jit(solution)/shard_map/ppermute | solution.py:317
  23.1 5.6 %bias_pairs.1 = (f32[864,144]{1,0:T(8,128)S(1)}, s32[176,128]{1,0:T(8,128)S(1)}) custom-call(f32[6,1,3312]{2,1,0:T(1,128)S(1)} %bitcast.18, s32[144,144]{1,0:T(8,128)S(1)} %copy-done, s32[1,144]{1,0:T(1,128)S(1)} %reshape.68.mask_ref), custom_call_target="tpu_custom_call" | custom-call | flops 10000000 | bytes 1200000 | tf_op jit(solution)/shard_map/bias_pairs/pallas_call | solution.py:98
  28.7 0.2 maximum_maximum_fusion
  29.0 0.1 fusion.6
  29.3 0.6 copy-done.4
  29.9 0.2 copy-done.3
  30.1 0.1 copy-done.2
  30.2 4.8 %block.1 = (bf16[144,192]{1,0:T(8,128)(2,1)S(1)}, bf16[144,192]{1,0:T(8,128)(2,1)S(1)}, bf16[3584,128]{1,0:T(8,128)(2,1)}, f32[6,176,128]{2,1,0:T(8,128)S(1)}) custom-call(bf16[144,192]{1,0:T(8,128)(2,1)S(1)} %reshape_squeeze.6.x_ref, bf16[144,192]{1,0:T(8,128)(2,1)S(1)} %reshape_squeeze.7.cot_ref, f32[1,192]{1,0:T(1,128)S(1)} %bitcast.20, ...), custom_call_target="tpu_custom_call" | custom-call | flops 900000000 | bytes 4000000 | tf_op jit(solution)/shard_map/block/pallas_call | solution.py:258
  35.1 5.4 %all-to-all-start = ((bf16[16,224,128]{2,1,0:T(8,128)(2,1)}), bf16[16,224,128]{2,1,0:T(8,128)(2,1)S(1)}, u32[]{:S(2)}, u32[]{:S(2)}) async-start(bf16[16,224,128]{2,1,0:T(8,128)(2,1)} %bitcast.6), calls=%async_computation | async-start | bytes 1835008 | tf_op jit(solution)/shard_map/all_to_all | solution.py:326
  40.6 6.0 %bias_grad.1 = bf16[160,128]{1,0:T(8,128)(2,1)S(1)} custom-call(f32[6,176,128]{2,1,0:T(8,128)S(1)} %get-tuple-element.29.pairs_ref, s32[176,128]{1,0:T(8,128)S(1)} %get-tuple-element.30.pos_ref), custom_call_target="tpu_custom_call" | custom-call | flops 1100000000 | bytes 700000 | tf_op jit(solution)/shard_map/bias_grad/pallas_call | solution.py:137
  46.6 8.4 %all-to-all-done = bf16[16,224,128]{2,1,0:T(8,128)(2,1)S(1)} async-done(((bf16[16,224,128]{2,1,0:T(8,128)(2,1)}), bf16[16,224,128]{2,1,0:T(8,128)(2,1)S(1)}, u32[]{:S(2)}, u32[]{:S(2)}) %all-to-all-start) | async-done | bytes 917536 | tf_op jit(solution)/shard_map/all_to_all | solution.py:326
  55.0 0.1 reduce_sum.36
  55.1 11.4 %all_to_all.25 = bf16[8,48,128]{2,1,0:T(8,128)(2,1)S(1)} all-to-all(bf16[8,48,128]{2,1,0:T(8,128)(2,1)S(1)} %bitcast.24), channel_id=1, replica_groups={{0,4,8,12,16,20,24,28},{1,5,9,13,17,21,25,29},{2,6,10,14,18,22,26,30},{..., dimensions={0} | all-to-all | bytes 196608 | tf_op jit(solution)/shard_map/all_to_all | solution.py:326
  66.5 0.6 broadcast_in_dim.6
  67.2 3.4 %all-to-all-start.2 = ((bf16[4,48,128]{2,1,0:T(8,128)(2,1)}), bf16[4,48,128]{2,1,0:T(8,128)(2,1)S(1)}, u32[]{:S(2)}, u32[]{:S(2)}) async-start(bf16[4,48,128]{2,1,0:T(8,128)(2,1)} %broadcast_in_dim.6), calls=%async_computation.2 | async-start | bytes 98304 | tf_op jit(solution)/shard_map/all_to_all | solution.py:326
  70.5 2.8 %collective-permute-start.3 = (bf16[2,2,3,12,192]{4,3,2,1,0:T(8,128)(2,1)S(1)}, bf16[2,2,3,12,192]{4,3,2,1,0:T(8,128)(2,1)S(1)}, u32[]{:S(2)}, u32[]{:S(2)}) collective-permute-start(bf16[2,2,3,12,192]{4,3,2,1,0:T(8,128)(2,1)S(1)} %get-tuple-element.65), channel_id=1, source_target_pairs={{0,32},{32,64},{64,96},{96,128},{128,160},{160,192},{192,224},{224... | collective-permute-start | bytes 165896 | tf_op jit(solution)/shard_map/ppermute | solution.py:348
  73.4 4.1 %all-to-all-done.2 = bf16[4,48,128]{2,1,0:T(8,128)(2,1)S(1)} async-done(((bf16[4,48,128]{2,1,0:T(8,128)(2,1)}), bf16[4,48,128]{2,1,0:T(8,128)(2,1)S(1)}, u32[]{:S(2)}, u32[]{:S(2)}) %all-to-all-start.2) | async-done | bytes 49184 | tf_op jit(solution)/shard_map/all_to_all | solution.py:326
  77.5 0.7 broadcast_in_dim.7
  78.1 3.4 %all-to-all-start.3 = ((bf16[8,48,128]{2,1,0:T(8,128)(2,1)}), bf16[8,48,128]{2,1,0:T(8,128)(2,1)S(1)}, u32[]{:S(2)}, u32[]{:S(2)}) async-start(bf16[8,48,128]{2,1,0:T(8,128)(2,1)} %broadcast_in_dim.7), calls=%async_computation.3 | async-start | bytes 196608 | tf_op jit(solution)/shard_map/all_to_all | solution.py:326
  81.6 2.8 %collective-permute-start.4 = (bf16[2,2,6,6,192]{4,3,2,1,0:T(8,128)(2,1)S(1)}, bf16[2,2,6,6,192]{4,3,2,1,0:T(8,128)(2,1)S(1)}, u32[]{:S(2)}, u32[]{:S(2)}) collective-permute-start(bf16[2,2,6,6,192]{4,3,2,1,0:T(8,128)(2,1)S(1)} %fusion.1), channel_id=1, source_target_pairs={{0,1},{1,2},{2,3},{3,4},{4,5},{5,6},{6,7},{7,8},{8,9},{9,10},{10,1... | collective-permute-start | bytes 165896 | tf_op jit(solution)/shard_map/ppermute | solution.py:353
  84.4 7.0 %collective-permute-done.4 = bf16[2,2,6,6,192]{4,3,2,1,0:T(8,128)(2,1)S(1)} collective-permute-done((bf16[2,2,6,6,192]{4,3,2,1,0:T(8,128)(2,1)S(1)}, bf16[2,2,6,6,192]{4,3,2,1,0:T(8,128)(2,1)S(1)}, u32[]{:S(2)}, u32[]{:S(2)}) %collective-permute-start.4) | collective-permute-done | bytes 55328 | tf_op jit(solution)/shard_map/ppermute | solution.py:353
  91.4 1.1 broadcast_in_dim.8
  92.5 8.6 %all-to-all-start.4 = ((bf16[16,224,128]{2,1,0:T(8,128)(2,1)}), bf16[16,224,128]{2,1,0:T(8,128)(2,1)S(1)}, u32[]{:S(2)}, u32[]{:S(2)}) async-start(bf16[16,224,128]{2,1,0:T(8,128)(2,1)} %broadcast_in_dim.8), calls=%async_computation.4 | async-start | bytes 1835008 | tf_op jit(solution)/shard_map/all_to_all | solution.py:326
  101.1 0.1 fusion
  101.2 0.7 copy.34
  102.0 0.7 reshape.79
  102.7 0.7 copy.33
  103.4 12.2 %all-to-all-done.4 = bf16[16,224,128]{2,1,0:T(8,128)(2,1)S(1)} async-done(((bf16[16,224,128]{2,1,0:T(8,128)(2,1)}), bf16[16,224,128]{2,1,0:T(8,128)(2,1)S(1)}, u32[]{:S(2)}, u32[]{:S(2)}) %all-to-all-start.4) | async-done | bytes 917536 | tf_op jit(solution)/shard_map/all_to_all | solution.py:326
  115.6 1.3 %unpack.1 = (f32[1,192]{1,0:T(1,128)}, f32[1,192]{1,0:T(1,128)}, f32[192,576]{1,0:T(8,128)}, f32[192,192]{1,0:T(8,128)}, f32[192,768]{1,0:T(8,128)}, /*index=5*/f32[192,768]{1,0:T(8,128)}) custom-call(bf16[3584,128]{1,0:T(8,128)(2,1)S(1)} %bitcast.17), custom_call_target="tpu_custom_call" | custom-call | flops 500000 | bytes 2700000 | tf_op jit(solution)/shard_map/unpack/pallas_call | solution.py:295
  (40 shorter events, 0.6 us)
Async XLA Ops:
  0.6 22.3 %copy-start.8 = (s32[2,6,12]{2,0,1:T(2,128)S(1)}, s32[2,6,12]{2,0,1:T(2,128)}, u32[]{:S(2)}) copy-start(s32[2,6,12]{2,0,1:T(2,128)} %param.20) | copy-start | bytes 1732
  0.7 22.4 %copy-start = (s32[144,144]{1,0:T(8,128)S(1)}, s32[144,144]{1,0:T(8,128)}, u32[]{:S(2)}) copy-start(s32[144,144]{1,0:T(8,128)} %pos_ref.1) | copy-start | bytes 248836
  0.7 22.4 %copy-start.1 = (f32[6,1,1,3312]{3,2,1,0:T(1,128)S(1)}, f32[6,1,1,3312]{3,2,1,0:T(1,128)}, u32[]{:S(2)}) copy-start(f32[6,1,1,3312]{3,2,1,0:T(1,128)} %param.18) | copy-start | bytes 238468
  1.8 26.9 %collective-permute-start = (bf16[2,2,3,6,192]{4,1,3,2,0:T(2,128)(2,1)S(1)}, bf16[2,2,3,6,192]{4,1,3,2,0:T(2,128)(2,1)S(1)}, u32[]{:S(2)}, u32[]{:S(2)}) collective-permute-start(bf16[2,2,3,6,192]{4,1,3,2,0:T(2,128)(2,1)S(1)} %get-tuple-element.70), channel_id=1, source_target_pairs={{0,31},{1,0},{2,1},{3,2},{4,3},{5,4},{6,5},{7,6},{8,7},{9,8},{10,9... | collective-permute-start | bytes 82952 | tf_op jit(solution)/shard_map/ppermute | solution.py:318
  16.2 12.5 %collective-permute-start.2 = (bf16[2,2,3,6,192]{4,1,3,2,0:T(2,128)(2,1)S(1)}, bf16[2,2,3,6,192]{4,1,3,2,0:T(2,128)(2,1)S(1)}, u32[]{:S(2)}, u32[]{:S(2)}) collective-permute-start(bf16[2,2,3,6,192]{4,1,3,2,0:T(2,128)(2,1)S(1)} %get-tuple-element.71), channel_id=1, source_target_pairs={{0,511},{1,480},{2,481},{3,482},{4,483},{5,484},{6,485},{7,486},{8... | collective-permute-start | bytes 82952 | tf_op jit(solution)/shard_map/ppermute | solution.py:319
  19.2 9.5 %collective-permute-start.1 = (bf16[2,2,3,6,192]{4,1,3,2,0:T(2,128)(2,1)S(1)}, bf16[2,2,3,6,192]{4,1,3,2,0:T(2,128)(2,1)S(1)}, u32[]{:S(2)}, u32[]{:S(2)}) collective-permute-start(bf16[2,2,3,6,192]{4,1,3,2,0:T(2,128)(2,1)S(1)} %get-tuple-element.72), channel_id=1, source_target_pairs={{0,480},{32,0},{64,32},{96,64},{128,96},{160,128},{192,160},{224,1... | collective-permute-start | bytes 82952 | tf_op jit(solution)/shard_map/ppermute | solution.py:317
  29.0 0.9 copy-start.4
  29.1 1.0 copy-start.3
  29.1 1.1 copy-start.2
  29.2 1.0 copy-start.5
  29.2 1.0 copy-start.7
  29.3 1.0 copy-start.6
  35.1 19.9 %all-to-all-start = ((bf16[16,224,128]{2,1,0:T(8,128)(2,1)}), bf16[16,224,128]{2,1,0:T(8,128)(2,1)S(1)}, u32[]{:S(2)}, u32[]{:S(2)}) async-start(bf16[16,224,128]{2,1,0:T(8,128)(2,1)} %bitcast.6), calls=%async_computation | async-start | bytes 1835008 | tf_op jit(solution)/shard_map/all_to_all | solution.py:326
  67.2 10.3 %all-to-all-start.2 = ((bf16[4,48,128]{2,1,0:T(8,128)(2,1)}), bf16[4,48,128]{2,1,0:T(8,128)(2,1)S(1)}, u32[]{:S(2)}, u32[]{:S(2)}) async-start(bf16[4,48,128]{2,1,0:T(8,128)(2,1)} %broadcast_in_dim.6), calls=%async_computation.2 | async-start | bytes 98304 | tf_op jit(solution)/shard_map/all_to_all | solution.py:326
  70.5 6.9 %collective-permute-start.3 = (bf16[2,2,3,12,192]{4,3,2,1,0:T(8,128)(2,1)S(1)}, bf16[2,2,3,12,192]{4,3,2,1,0:T(8,128)(2,1)S(1)}, u32[]{:S(2)}, u32[]{:S(2)}) collective-permute-start(bf16[2,2,3,12,192]{4,3,2,1,0:T(8,128)(2,1)S(1)} %get-tuple-element.65), channel_id=1, source_target_pairs={{0,32},{32,64},{64,96},{96,128},{128,160},{160,192},{192,224},{224... | collective-permute-start | bytes 165896 | tf_op jit(solution)/shard_map/ppermute | solution.py:348
  78.1 13.3 %all-to-all-start.3 = ((bf16[8,48,128]{2,1,0:T(8,128)(2,1)}), bf16[8,48,128]{2,1,0:T(8,128)(2,1)S(1)}, u32[]{:S(2)}, u32[]{:S(2)}) async-start(bf16[8,48,128]{2,1,0:T(8,128)(2,1)} %broadcast_in_dim.7), calls=%async_computation.3 | async-start | bytes 196608 | tf_op jit(solution)/shard_map/all_to_all | solution.py:326
  81.6 9.8 %collective-permute-start.4 = (bf16[2,2,6,6,192]{4,3,2,1,0:T(8,128)(2,1)S(1)}, bf16[2,2,6,6,192]{4,3,2,1,0:T(8,128)(2,1)S(1)}, u32[]{:S(2)}, u32[]{:S(2)}) collective-permute-start(bf16[2,2,6,6,192]{4,3,2,1,0:T(8,128)(2,1)S(1)} %fusion.1), channel_id=1, source_target_pairs={{0,1},{1,2},{2,3},{3,4},{4,5},{5,6},{6,7},{7,8},{8,9},{9,10},{10,1... | collective-permute-start | bytes 165896 | tf_op jit(solution)/shard_map/ppermute | solution.py:353
  92.5 23.1 %all-to-all-start.4 = ((bf16[16,224,128]{2,1,0:T(8,128)(2,1)}), bf16[16,224,128]{2,1,0:T(8,128)(2,1)S(1)}, u32[]{:S(2)}, u32[]{:S(2)}) async-start(bf16[16,224,128]{2,1,0:T(8,128)(2,1)} %broadcast_in_dim.8), calls=%async_computation.4 | async-start | bytes 1835008 | tf_op jit(solution)/shard_map/all_to_all | solution.py:326

commit v3 on v2

--- a/solution.py
+++ b/solution.py
@@ -17,6 +17,7 @@
 TAIL = WT - LANES
 ROWS = WT + 2 * TAIL
 GROWS = 3584
+STEP = 44
 BROWS = 160
 EPS = 1e-05
 F32 = jnp.float32
@@ -66,25 +67,28 @@
     for h in range(HEADS):
         for g in range(SLOTS):
             count = min(LANES, NPOS - g * LANES)
-            slots_ref[h, g : g + 1, :count] = table_ref[h, :, g * LANES : g * LANES + count]
+            row = table_ref[h, :, g * LANES : g * LANES + count]
+            slots_ref[h, g, :, :count] = jnp.broadcast_to(row, (8, count))
 
     def rows(i, carry):
-        at = pl.ds(pl.multiple_of(i * 8, 8), 8)
-        pos = flat_pos_ref[at, :]
-        lane = jnp.bitwise_and(pos, LANES - 1)
-        slot = jnp.right_shift(pos, 7)
-        held = [jnp.zeros((8, LANES), F32)] * HEADS
+        ats = [pl.ds(pl.multiple_of(i * 16 + 8 * k, 8), 8) for k in range(2)]
+        pos = [flat_pos_ref[at, :] for at in ats]
+        lane = [jnp.bitwise_and(p, LANES - 1) for p in pos]
+        slot = [jnp.right_shift(p, 7) for p in pos]
+        held = [[jnp.zeros((8, LANES), F32)] * HEADS for _ in ats]
         for g in range(SLOTS):
-            here = slot == g
+            here = [s == g for s in slot]
             for h in range(HEADS):
-                row = jnp.broadcast_to(slots_ref[h, g : g + 1, :], (8, LANES))
-                got = jnp.take_along_axis(row, lane, axis=1)
-                held[h] = jnp.where(here, got, held[h])
-        for h in range(HEADS):
-            flat_ref[h, at, :] = held[h]
+                row = slots_ref[h, g]
+                for k in range(2):
+                    got = jnp.take_along_axis(row, lane[k], axis=1)
+                    held[k][h] = jnp.where(here[k], got, held[k][h])
+        for k, at in enumerate(ats):
+            for h in range(HEADS):
+                flat_ref[h, at, :] = held[k][h]
         return carry
 
-    lax.fori_loop(0, ROWS // 8, rows, 0)
+    lax.fori_loop(0, ROWS // 16, rows, 0)
     mask = jnp.broadcast_to(mask_ref[...], (WT, WT))
     allowed = mask == mask.T
     for h in range(HEADS):
@@ -98,7 +102,7 @@
     return pl.pallas_call(
         gather_kernel,
         out_shape=[jax.ShapeDtypeStruct((HEADS * WT, WT), F32), jax.ShapeDtypeStruct((ROWS, LANES), jnp.int32)],
-        scratch_shapes=[pltpu.VMEM((HEADS, SLOTS, LANES), F32), pltpu.VMEM((HEADS, ROWS, LANES), F32)],
+        scratch_shapes=[pltpu.VMEM((HEADS, SLOTS, 8, LANES), F32), pltpu.VMEM((HEADS, ROWS, LANES), F32)],
         name="bias_pairs",
         compiler_params=pltpu.CompilerParams(vmem_limit_bytes=16 * 1024 * 1024),
         cost_estimate=pl.CostEstimate(flops=10_000_000, bytes_accessed=1_200_000, transcendentals=0),
@@ -112,21 +116,22 @@
 
     def rows(i, carry):
         spread, onehot = [], []
-        for j in range(8):
-            at = pl.ds(i * 8 + j, 1)
+        for j in range(STEP):
+            at = pl.ds(i * STEP + j, 1)
             pos = pos_ref[at, :]
-            here = slot_ids == jnp.right_shift(pos, 7)
+            slot = jnp.where(slot_ids == jnp.right_shift(pos, 7), 1.0, 0.0).astype(BF16)
             lane = jnp.bitwise_and(pos, LANES - 1)
             onehot.append(jnp.where(lane_ids == lane, 1.0, 0.0).astype(BF16))
             spread.append(
                 jnp.concatenate(
-                    [jnp.where(here, pairs_ref[h, at, :], 0.0).astype(BF16) for h in range(HEADS)], axis=0
+                    [slot * jnp.broadcast_to(pairs_ref[h, at, :], (32, LANES)).astype(BF16) for h in range(HEADS)],
+                    axis=0,
                 )
             )
         sums_ref[...] += dot_nt(jnp.concatenate(spread, axis=1), jnp.concatenate(onehot, axis=1))
         return carry
 
-    lax.fori_loop(0, ROWS // 8, rows, 0)
+    lax.fori_loop(0, ROWS // STEP, rows, 0)
     packed_ref[...] = jnp.zeros_like(packed_ref)
     for h in range(HEADS):
         packed_ref[h * SLOTS : (h + 1) * SLOTS] = sums_ref[h * 32 : h * 32 + SLOTS]
@@ -147,8 +152,7 @@
 def block_kernel(
     x_ref,
     cot_ref,
-    gain_one_ref,
-    gain_two_ref,
+    gains_ref,
     qkv_ref,
     proj_ref,
     up_ref,
@@ -164,8 +168,7 @@
 ):
     factor = HEAD ** (-0.5)
     x = x_ref[...].astype(F32)
-    gain_one = gain_one_ref[...]
-    gain_two = gain_two_ref[...]
+    gain_one, gain_two = gains_ref[0:1], gains_ref[1:2]
     normal_one, inverse_one = norm_stats(x)
     normed = (normal_one * gain_one).astype(BF16)
     packed = dot(normed, qkv_ref[...]).astype(BF16)
@@ -269,25 +272,35 @@
     )(*args)
 
 
-def unpack_kernel(grads_ref, gain_one_ref, gain_two_ref, qkv_ref, proj_ref, up_ref, down_ref):
+def unpack_kernel(grads_ref, *refs):
+    outs, held, sems = refs[:6], refs[6:12], refs[12]
+    gain_one_ref, gain_two_ref, qkv_ref, proj_ref, up_ref, down_ref = held
     factor = TOKENS ** (-0.5)
+    copies = [pltpu.make_async_copy(held[k], outs[k], sems.at[k]) for k in range(6)]
 
     def rows(start, count):
         return grads_ref[start : start + count].astype(F32) * factor
 
     for t in range(6):
-        at = slice(LANES * t, LANES * (t + 1))
-        up_ref[:, at] = rows(C * t, C)
-        down_ref[:, at] = rows(C * (t + 6), C)
-        if t < 4:
-            qkv_ref[:, at] = rows(C * (t + 12), C)
+        up_ref[:, LANES * t : LANES * (t + 1)] = rows(C * t, C)
+    copies[4].start()
+    for t in range(6):
+        down_ref[:, LANES * t : LANES * (t + 1)] = rows(C * (t + 6), C)
+    copies[5].start()
     halves = rows(C * 17, C)
+    for t in range(4):
+        qkv_ref[:, LANES * t : LANES * (t + 1)] = rows(C * (t + 12), C)
     qkv_ref[:, 4 * LANES :] = halves[:, :64]
+    copies[2].start()
     proj_ref[:, :LANES] = rows(C * 16, C)
     proj_ref[:, LANES:] = halves[:, 64:]
+    copies[3].start()
     gains = rows(C * 18, 16)
     for k, ref in enumerate((gain_one_ref, gain_two_ref)):
         ref[...] = jnp.concatenate((gains[k : k + 1], gains[k + 2 : k + 3, : C - LANES]), axis=1)
+        copies[k].start()
+    for copy in copies:
+        copy.wait()
 
 
 def unpack(grads):
@@ -295,6 +308,9 @@
     return pl.pallas_call(
         unpack_kernel,
         out_shape=[jax.ShapeDtypeStruct(s, F32) for s in shapes],
+        in_specs=[pl.BlockSpec(memory_space=pltpu.VMEM)],
+        out_specs=[pl.BlockSpec(memory_space=pl.ANY)] * 6,
+        scratch_shapes=[pltpu.VMEM(s, F32) for s in shapes] + [pltpu.SemaphoreType.DMA((6,))],
         name="unpack",
         compiler_params=pltpu.CompilerParams(vmem_limit_bytes=16 * 1024 * 1024),
         cost_estimate=pl.CostEstimate(flops=500_000, bytes_accessed=2_700_000, transcendentals=0),
@@ -332,30 +348,41 @@
 
 def finish(grid, grads, pairs, pos_flat):
     lat, lon = lax.axis_size("lat"), lax.axis_size("lon")
-    far = 4
-    near = lon // far
-    over_near = spread_over("lon", [[n * far + f for n in range(near)] for f in range(far)])
-    over_far = spread_over("lon", [[n * far + f for f in range(far)] for n in range(near)])
-    over_lat = spread_over("lat")
+    low, far = 2, 4
+    high = lon // (low * far)
+    place = lambda h, l, f: (h * low + l) * far + f
+    over_low = spread_over(
+        ("lat", "lon"),
+        [[i * lon + place(h, l, f) for i in range(lat) for l in range(low)] for h in range(high) for f in range(far)],
+    )
+    over_high = spread_over("lon", [[place(h, l, f) for h in range(high)] for l in range(low) for f in range(far)])
+    over_far = spread_over("lon", [[place(h, l, f) for f in range(far)] for h in range(high) for l in range(low)])
+    other = [(j, j ^ far) for j in range(lon)]
 
     def same(part, count):
         return jnp.broadcast_to(part[None], (count,) + part.shape)
 
-    share = GROWS // lat
-    mine = total(over_lat(grads.reshape(lat, share, LANES)))
-    both = jnp.concatenate((mine, bias_grad(pairs, pos_flat)), axis=0)
-    both, grid = lax.optimization_barrier((both, grid))
+    share = GROWS // (lat * low)
+    mine = total(over_low(grads.reshape(lat * low, share, LANES)))
+    own = bias_grad(pairs, pos_flat).reshape(low, BROWS // low, LANES)
+    at = lax.axis_index("lon") // far % low
+    kept = lax.dynamic_index_in_dim(own, at, 0, keepdims=False)
+    given = lax.dynamic_index_in_dim(own, 1 - at, 0, keepdims=False)
+    bias = total(jnp.stack((kept, lax.ppermute(given, "lon", other))))
+    both = jnp.concatenate((mine, bias), axis=0)
     rows_got = lax.ppermute(grid[:, :, 3:], "lat", ring("lat", 1))
-    part = total(over_near(both.reshape(near, -1, LANES)))
-    part = total(over_far(same(part, far)))
-    part, rows_got = lax.optimization_barrier((part, rows_got))
+    both = total(over_high(same(both, high)))
+    both, rows_got = lax.optimization_barrier((both, rows_got))
     grid = jnp.concatenate((rows_got, grid[:, :, :3]), axis=2)
     cols_got = lax.ppermute(grid[:, :, :, 6:], "lon", ring("lon", 1))
-    both = over_near(same(part, near)).reshape(both.shape)
+    both = total(over_far(same(both, far)))
     both, cols_got = lax.optimization_barrier((both, cols_got))
     grid = jnp.concatenate((cols_got, grid[:, :, :, :6]), axis=3)
-    grads = over_lat(same(both[:share], lat)).reshape(GROWS, LANES)
-    return grid, grads, both[share:]
+    grads = over_low(same(both[:share], lat * low)).reshape(GROWS, LANES)
+    kept = both[share:]
+    given = lax.ppermute(kept, "lon", other)
+    first, second = jnp.where(at == 0, kept, given), jnp.where(at == 0, given, kept)
+    return grid, grads, jnp.concatenate((first, second), axis=0).astype(F32)
 
 
 def local(
@@ -377,8 +404,7 @@
     out, delta, grads, pairs = block(
         moved[0].reshape(WT, C),
         moved[1].reshape(WT, C),
-        gain_one.reshape(1, C),
-        gain_two.reshape(1, C),
+        jnp.stack((gain_one, gain_two)),
         qkv_weight,
         proj_weight,
         up_weight,
@@ -387,7 +413,7 @@
     )
     back, grads, grad_bias = finish(jnp.stack((out, delta)).reshape((2,) + grid), grads, pairs, pos_flat)
     totals = unpack(grads)
-    grad_bias = grad_bias[: HEADS * SLOTS].reshape(HEADS, SLOTS * LANES)[:, :NPOS].astype(F32)
+    grad_bias = grad_bias[: HEADS * SLOTS].reshape(HEADS, SLOTS * LANES)[:, :NPOS]
     return (
         back[0],
         back[1],

time: 118 us -> 109 us (0.924)
  blocking collectives: 11.4 us -> 0 us
  starting transfers between devices: 47.5 us -> 54.3 us
  Pallas kernels: 17.8 us -> 14 us
  waiting for transfers between devices: 31.6 us -> 30.1 us
    ppermute x0 -> x2, waiting for transfers between devices: none -> 13.8 us  [the longest x1 7.66 us: finish(): given = lax.ppermute(kept, 'lon', other)]
    ppermute x1, starting transfers between devices: 14.4 us -> 2.17 us  [shift_in(): from_lon = lax.ppermute(grid[:, :, 3:, :6], 'lon', ring('lon', -1))]
    ppermute x1, starting transfers between devices: 3.01 us -> 15 us  [shift_in(): from_both = lax.ppermute(grid[:, :, :3, :6], ('lat', 'lon'), neighbours(-1))]
    all_to_all x1 -> x0, blocking collectives: 11.4 us -> none  [spread_over(): lax.all_to_all(parts, axis, 0, 0, axis_index_groups=groups)]
    all_to_all x4, waiting for transfers between devices: 24.6 us -> 13.7 us  [spread_over(): lax.all_to_all(parts, axis, 0, 0, axis_index_groups=groups)]
    ppermute x0 -> x2, starting transfers between devices: none -> 6.57 us  [the longest x1 3.29 us: finish(): given = lax.ppermute(kept, 'lon', other)]
    ppermute x1, waiting for transfers between devices: 7.03 us -> 2.67 us  [finish(): cols_got = lax.ppermute(grid[:, :, :, 6:], 'lon', ring('lon', 1))]
    pallas_call x1, Pallas kernels: 6 us -> 2.98 us  [bias_grad(): pl.pallas_call(scatter_kernel, out_shape=jax.ShapeDtypeStruct((BROWS, LAN...]
  transfers between devices with their start and end apart: 9 -> 11, of which waited for: 4 -> 7; matrix products, arithmetic and copies ran while one was open for 2% -> 2% of each run, Pallas kernels for 10% -> 7%
where the time goes in v3:
time: 109 us; the launch traced here: 108 us
  starting transfers between devices  54.3 us (50%)
  waiting for transfers between devices  30.1 us (28%)
  Pallas kernels  14 us (13%)
  local copies, waits for them, and re-layouts  6.75 us (6%)
  other arithmetic  1.74 us (2%)
    all_to_all x4, starting transfers between devices, spread_over(): lax.all_to_all(parts, axis, 0, 0, axis_index_groups=groups)  20.4 us
    ppermute x1, starting transfers between devices, shift_in(): from_both = lax.ppermute(grid[:, :, :3, :6], ('lat', 'lon'), neighbours(-1))  15 us
    all_to_all x4, waiting for transfers between devices, spread_over(): lax.all_to_all(parts, axis, 0, 0, axis_index_groups=groups)  13.7 us
    ppermute x1, waiting for transfers between devices, finish(): given = lax.ppermute(kept, 'lon', other)  7.66 us
    ppermute x1, waiting for transfers between devices, finish(): bias = total(jnp.stack((kept, lax.ppermute(given, 'lon', other))))  6.1 us
    pallas_call x1, Pallas kernels, bias_pairs(): pl.pallas_call(gather_kernel, out_shape=[jax.ShapeDtypeStruct((HEADS * WT...  4.86 us
    pallas_call x1, Pallas kernels, block(): pl.pallas_call(block_kernel, out_shape=[jax.ShapeDtypeStruct(s, d) for s,...  4.83 us
    ppermute x1, starting transfers between devices, finish(): cols_got = lax.ppermute(grid[:, :, :, 6:], 'lon', ring('lon', 1))  4.27 us
  transfers between devices with their start and end apart: 11, of which 7 were waited for; matrix products, arithmetic and copies ran while one was open for 2% of the time, Pallas kernels for 7%

profile of v3, /device:TPU:1, one launch (start us, length us, event | category | flops | bytes accessed | tf_op | source)
XLA Modules:
  0.0 107.9 jit_solution(8487117817326029600)
XLA Ops:
  0.7 1.1 %fusion.3 = (bf16[2,2,3,6,192]{4,1,3,2,0:T(2,128)(2,1)S(1)}, bf16[2,2,3,6,192]{4,1,3,2,0:T(2,128)(2,1)S(1)}, bf16[2,2,3,6,192]{4,1,3,2,0:T(2,128)(2,1)S(1)}, bf16[2,2,3,6,192]{4,1,3,2,0:T(2,128)(2,1)S(1)}) fusion(bf16[1,2,6,12,192]{4,1,3,2,0:T(2,128)(2,1)} %bitcast.25, bf16[1,2,6,12,192]{4,1,3,2,0:T(2,128)(2,1)} %bitcast.26), kind=kLoop, calls=%fused_computation.18 | loop fusion | flops 55296 | bytes 221184 | tf_op jit(solution)/shard_map/stack | solution.py:402
  1.8 15.0 %collective-permute-start.2 = (bf16[2,2,3,6,192]{4,1,3,2,0:T(2,128)(2,1)S(1)}, bf16[2,2,3,6,192]{4,1,3,2,0:T(2,128)(2,1)S(1)}, u32[]{:S(2)}, u32[]{:S(2)}) collective-permute-start(bf16[2,2,3,6,192]{4,1,3,2,0:T(2,128)(2,1)S(1)} %get-tuple-element.67), channel_id=1, source_target_pairs={{0,511},{1,480},{2,481},{3,482},{4,483},{5,484},{6,485},{7,486},{8... | collective-permute-start | bytes 82952 | tf_op jit(solution)/shard_map/ppermute | solution.py:335
  16.8 3.9 %collective-permute-start.1 = (bf16[2,2,3,6,192]{4,1,3,2,0:T(2,128)(2,1)S(1)}, bf16[2,2,3,6,192]{4,1,3,2,0:T(2,128)(2,1)S(1)}, u32[]{:S(2)}, u32[]{:S(2)}) collective-permute-start(bf16[2,2,3,6,192]{4,1,3,2,0:T(2,128)(2,1)S(1)} %get-tuple-element.68), channel_id=1, source_target_pairs={{0,480},{32,0},{64,32},{96,64},{128,96},{160,128},{192,160},{224,1... | collective-permute-start | bytes 82952 | tf_op jit(solution)/shard_map/ppermute | solution.py:333
  20.7 2.2 %collective-permute-start = (bf16[2,2,3,6,192]{4,1,3,2,0:T(2,128)(2,1)S(1)}, bf16[2,2,3,6,192]{4,1,3,2,0:T(2,128)(2,1)S(1)}, u32[]{:S(2)}, u32[]{:S(2)}) collective-permute-start(bf16[2,2,3,6,192]{4,1,3,2,0:T(2,128)(2,1)S(1)} %get-tuple-element.66), channel_id=1, source_target_pairs={{0,31},{1,0},{2,1},{3,2},{4,3},{5,4},{6,5},{7,6},{8,7},{9,8},{10,9... | collective-permute-start | bytes 82952 | tf_op jit(solution)/shard_map/ppermute | solution.py:334
  22.9 0.7 copy-done.7
  23.8 4.9 %bias_pairs.1 = (f32[864,144]{1,0:T(8,128)S(1)}, s32[176,128]{1,0:T(8,128)S(1)}) custom-call(f32[6,1,3312]{2,1,0:T(1,128)S(1)} %bitcast.21, s32[144,144]{1,0:T(8,128)S(1)} %copy-done, s32[1,144]{1,0:T(1,128)S(1)} %reshape.61.mask_ref), custom_call_target="tpu_custom_call" | custom-call | flops 10000000 | bytes 1200000 | tf_op jit(solution)/shard_map/bias_pairs/pallas_call | solution.py:102
  28.6 0.2 maximum_maximum_fusion
  29.2 0.7 copy-done.4
  30.1 4.8 %block.1 = (bf16[144,192]{1,0:T(8,128)(2,1)S(1)}, bf16[144,192]{1,0:T(8,128)(2,1)S(1)}, bf16[3584,128]{1,0:T(8,128)(2,1)}, f32[6,176,128]{2,1,0:T(8,128)S(1)}) custom-call(bf16[144,192]{1,0:T(8,128)(2,1)S(1)} %reshape_squeeze.6.x_ref, bf16[144,192]{1,0:T(8,128)(2,1)S(1)} %reshape_squeeze.7.cot_ref, f32[2,192]{1,0:T(2,128)S(1)} %pad_maximum_fusion.4.gains_ref, ...), custom_call_target="tpu_custom_call" | custom-call | flops 900000000 | bytes 4000000 | tf_op jit(solution)/shard_map/block/pallas_call | solution.py:261
  35.0 5.6 %all-to-all-start = ((bf16[32,112,128]{2,1,0:T(8,128)(2,1)}), bf16[32,112,128]{2,1,0:T(8,128)(2,1)S(1)}, u32[]{:S(2)}, u32[]{:S(2)}) async-start(bf16[32,112,128]{2,1,0:T(8,128)(2,1)} %bitcast.6), calls=%async_computation | async-start | bytes 1835008 | tf_op jit(solution)/shard_map/all_to_all | solution.py:342
  40.7 3.0 %bias_grad.1 = bf16[160,128]{1,0:T(8,128)(2,1)S(1)} custom-call(f32[6,176,128]{2,1,0:T(8,128)S(1)} %get-tuple-element.27.pairs_ref, s32[176,128]{1,0:T(8,128)S(1)} %get-tuple-element.28.pos_ref), custom_call_target="tpu_custom_call" | custom-call | flops 1100000000 | bytes 700000 | tf_op jit(solution)/shard_map/bias_grad/pallas_call | solution.py:142
  43.7 3.3 %collective-permute-start.3 = (bf16[80,128]{1,0:T(8,128)(2,1)S(1)}, bf16[80,128]{1,0:T(8,128)(2,1)S(1)}, u32[]{:S(2)}, u32[]{:S(2)}) collective-permute-start(bf16[80,128]{1,0:T(8,128)(2,1)S(1)} %dynamic-slice_bitcast_fusion), channel_id=1, source_target_pairs={{0,4},{1,5},{2,6},{3,7},{4,0},{5,1},{6,2},{7,3},{8,12},{9,13},{10,... | collective-permute-start | bytes 61448 | tf_op jit(solution)/shard_map/ppermute | solution.py:371
  47.0 6.1 %collective-permute-done.3 = bf16[80,128]{1,0:T(8,128)(2,1)S(1)} collective-permute-done((bf16[80,128]{1,0:T(8,128)(2,1)S(1)}, bf16[80,128]{1,0:T(8,128)(2,1)S(1)}, u32[]{:S(2)}, u32[]{:S(2)}) %collective-permute-start.3) | collective-permute-done | bytes 20512 | tf_op jit(solution)/shard_map/ppermute | solution.py:371
  53.1 2.5 %all-to-all-done = bf16[32,112,128]{2,1,0:T(8,128)(2,1)S(1)} async-done(((bf16[32,112,128]{2,1,0:T(8,128)(2,1)}), bf16[32,112,128]{2,1,0:T(8,128)(2,1)S(1)}, u32[]{:S(2)}, u32[]{:S(2)}) %all-to-all-start) | async-done | bytes 917536 | tf_op jit(solution)/shard_map/all_to_all | solution.py:342
  55.7 0.7 broadcast_in_dim.6
  56.4 3.8 %all-to-all-start.1 = ((bf16[4,192,128]{2,1,0:T(8,128)(2,1)}), bf16[4,192,128]{2,1,0:T(8,128)(2,1)S(1)}, u32[]{:S(2)}, u32[]{:S(2)}) async-start(bf16[4,192,128]{2,1,0:T(8,128)(2,1)} %broadcast_in_dim.6), calls=%async_computation.1 | async-start | bytes 393216 | tf_op jit(solution)/shard_map/all_to_all | solution.py:342
  60.2 1.9 %collective-permute-start.4 = (bf16[2,2,3,12,192]{4,3,2,1,0:T(8,128)(2,1)S(1)}, bf16[2,2,3,12,192]{4,3,2,1,0:T(8,128)(2,1)S(1)}, u32[]{:S(2)}, u32[]{:S(2)}) collective-permute-start(bf16[2,2,3,12,192]{4,3,2,1,0:T(8,128)(2,1)S(1)} %get-tuple-element.61), channel_id=1, source_target_pairs={{0,32},{32,64},{64,96},{96,128},{128,160},{160,192},{192,224},{224... | collective-permute-start | bytes 165896 | tf_op jit(solution)/shard_map/ppermute | solution.py:373
  62.2 6.2 %all-to-all-done.1 = bf16[4,192,128]{2,1,0:T(8,128)(2,1)S(1)} async-done(((bf16[4,192,128]{2,1,0:T(8,128)(2,1)}), bf16[4,192,128]{2,1,0:T(8,128)(2,1)S(1)}, u32[]{:S(2)}, u32[]{:S(2)}) %all-to-all-start.1) | async-done | bytes 196640 | tf_op jit(solution)/shard_map/all_to_all | solution.py:342
  68.5 0.7 broadcast_in_dim.7
  69.2 3.4 %all-to-all-start.2 = ((bf16[4,192,128]{2,1,0:T(8,128)(2,1)}), bf16[4,192,128]{2,1,0:T(8,128)(2,1)S(1)}, u32[]{:S(2)}, u32[]{:S(2)}) async-start(bf16[4,192,128]{2,1,0:T(8,128)(2,1)} %broadcast_in_dim.7), calls=%async_computation.2 | async-start | bytes 393216 | tf_op jit(solution)/shard_map/all_to_all | solution.py:342
  72.6 4.3 %collective-permute-start.5 = (bf16[2,2,6,6,192]{4,3,2,1,0:T(8,128)(2,1)S(1)}, bf16[2,2,6,6,192]{4,3,2,1,0:T(8,128)(2,1)S(1)}, u32[]{:S(2)}, u32[]{:S(2)}) collective-permute-start(bf16[2,2,6,6,192]{4,3,2,1,0:T(8,128)(2,1)S(1)} %fusion.1), channel_id=1, source_target_pairs={{0,1},{1,2},{2,3},{3,4},{4,5},{5,6},{6,7},{7,8},{8,9},{9,10},{10,1... | collective-permute-start | bytes 165896 | tf_op jit(solution)/shard_map/ppermute | solution.py:377
  76.9 3.3 %all-to-all-done.2 = bf16[4,192,128]{2,1,0:T(8,128)(2,1)S(1)} async-done(((bf16[4,192,128]{2,1,0:T(8,128)(2,1)}), bf16[4,192,128]{2,1,0:T(8,128)(2,1)S(1)}, u32[]{:S(2)}, u32[]{:S(2)}) %all-to-all-start.2) | async-done | bytes 196640 | tf_op jit(solution)/shard_map/all_to_all | solution.py:342
  80.2 2.7 %collective-permute-done.5 = bf16[2,2,6,6,192]{4,3,2,1,0:T(8,128)(2,1)S(1)} collective-permute-done((bf16[2,2,6,6,192]{4,3,2,1,0:T(8,128)(2,1)S(1)}, bf16[2,2,6,6,192]{4,3,2,1,0:T(8,128)(2,1)S(1)}, u32[]{:S(2)}, u32[]{:S(2)}) %collective-permute-start.5) | collective-permute-done | bytes 55328 | tf_op jit(solution)/shard_map/ppermute | solution.py:377
  82.9 1.1 broadcast_in_dim.8
  83.9 7.7 %all-to-all-start.3 = ((bf16[32,112,128]{2,1,0:T(8,128)(2,1)}), bf16[32,112,128]{2,1,0:T(8,128)(2,1)S(1)}, u32[]{:S(2)}, u32[]{:S(2)}) async-start(bf16[32,112,128]{2,1,0:T(8,128)(2,1)} %broadcast_in_dim.8), calls=%async_computation.3 | async-start | bytes 1835008 | tf_op jit(solution)/shard_map/all_to_all | solution.py:342
  91.6 3.3 %collective-permute-start.6 = (bf16[80,128]{1,0:T(8,128)(2,1)S(1)}, bf16[80,128]{1,0:T(8,128)(2,1)S(1)}, u32[]{:S(2)}, u32[]{:S(2)}) collective-permute-start(bf16[80,128]{1,0:T(8,128)(2,1)S(1)} %slice.63), channel_id=1, source_target_pairs={{0,4},{1,5},{2,6},{3,7},{4,0},{5,1},{6,2},{7,3},{8,12},{9,13},{10,... | collective-permute-start | bytes 61448 | tf_op jit(solution)/shard_map/ppermute | solution.py:383
  95.0 0.7 copy.33
  95.8 0.7 copy.34
  96.5 7.7 %collective-permute-done.6 = bf16[80,128]{1,0:T(8,128)(2,1)S(1)} collective-permute-done((bf16[80,128]{1,0:T(8,128)(2,1)S(1)}, bf16[80,128]{1,0:T(8,128)(2,1)S(1)}, u32[]{:S(2)}, u32[]{:S(2)}) %collective-permute-start.6) | collective-permute-done | bytes 20512 | tf_op jit(solution)/shard_map/ppermute | solution.py:383
  104.2 0.7 reshape.71
  104.9 1.7 %all-to-all-done.3 = bf16[32,112,128]{2,1,0:T(8,128)(2,1)S(1)} async-done(((bf16[32,112,128]{2,1,0:T(8,128)(2,1)}), bf16[32,112,128]{2,1,0:T(8,128)(2,1)S(1)}, u32[]{:S(2)}, u32[]{:S(2)}) %all-to-all-start.3) | async-done | bytes 917536 | tf_op jit(solution)/shard_map/all_to_all | solution.py:342
  106.6 1.3 %unpack.1 = (f32[1,192]{1,0:T(1,128)}, f32[1,192]{1,0:T(1,128)}, f32[192,576]{1,0:T(8,128)}, f32[192,192]{1,0:T(8,128)}, f32[192,768]{1,0:T(8,128)}, /*index=5*/f32[192,768]{1,0:T(8,128)}) custom-call(bf16[3584,128]{1,0:T(8,128)(2,1)S(1)} %bitcast.20), custom_call_target="tpu_custom_call" | custom-call | flops 500000 | bytes 2700000 | tf_op jit(solution)/shard_map/unpack/pallas_call | solution.py:308
  (49 shorter events, 1.2 us)
Async XLA Ops:
  0.6 23.1 %copy-start = (s32[144,144]{1,0:T(8,128)S(1)}, s32[144,144]{1,0:T(8,128)}, u32[]{:S(2)}) copy-start(s32[144,144]{1,0:T(8,128)} %pos_ref.1) | copy-start | bytes 248836
  0.7 23.1 %copy-start.1 = (f32[6,1,1,3312]{3,2,1,0:T(1,128)S(1)}, f32[6,1,1,3312]{3,2,1,0:T(1,128)}, u32[]{:S(2)}) copy-start(f32[6,1,1,3312]{3,2,1,0:T(1,128)} %param.18) | copy-start | bytes 238468
  1.8 21.1 %copy-start.8 = (f32[192]{0:T(256)S(1)}, f32[192]{0:T(256)}, u32[]{:S(2)}) copy-start(f32[192]{0:T(256)} %param.12) | copy-start | bytes 2308
  1.8 21.8 %copy-start.6 = (s32[2,6,12]{2,0,1:T(2,128)S(1)}, s32[2,6,12]{2,0,1:T(2,128)}, u32[]{:S(2)}) copy-start(s32[2,6,12]{2,0,1:T(2,128)} %param.20) | copy-start | bytes 1732
  1.8 26.8 %collective-permute-start.2 = (bf16[2,2,3,6,192]{4,1,3,2,0:T(2,128)(2,1)S(1)}, bf16[2,2,3,6,192]{4,1,3,2,0:T(2,128)(2,1)S(1)}, u32[]{:S(2)}, u32[]{:S(2)}) collective-permute-start(bf16[2,2,3,6,192]{4,1,3,2,0:T(2,128)(2,1)S(1)} %get-tuple-element.67), channel_id=1, source_target_pairs={{0,511},{1,480},{2,481},{3,482},{4,483},{5,484},{6,485},{7,486},{8... | collective-permute-start | bytes 82952 | tf_op jit(solution)/shard_map/ppermute | solution.py:335
  16.8 11.9 %collective-permute-start.1 = (bf16[2,2,3,6,192]{4,1,3,2,0:T(2,128)(2,1)S(1)}, bf16[2,2,3,6,192]{4,1,3,2,0:T(2,128)(2,1)S(1)}, u32[]{:S(2)}, u32[]{:S(2)}) collective-permute-start(bf16[2,2,3,6,192]{4,1,3,2,0:T(2,128)(2,1)S(1)} %get-tuple-element.68), channel_id=1, source_target_pairs={{0,480},{32,0},{64,32},{96,64},{128,96},{160,128},{192,160},{224,1... | collective-permute-start | bytes 82952 | tf_op jit(solution)/shard_map/ppermute | solution.py:333
  20.7 7.9 %collective-permute-start = (bf16[2,2,3,6,192]{4,1,3,2,0:T(2,128)(2,1)S(1)}, bf16[2,2,3,6,192]{4,1,3,2,0:T(2,128)(2,1)S(1)}, u32[]{:S(2)}, u32[]{:S(2)}) collective-permute-start(bf16[2,2,3,6,192]{4,1,3,2,0:T(2,128)(2,1)S(1)} %get-tuple-element.66), channel_id=1, source_target_pairs={{0,31},{1,0},{2,1},{3,2},{4,3},{5,4},{6,5},{7,6},{8,7},{9,8},{10,9... | collective-permute-start | bytes 82952 | tf_op jit(solution)/shard_map/ppermute | solution.py:334
  22.9 0.7 copy-start.7
  28.9 0.9 copy-start.4
  29.0 1.0 copy-start.3
  29.1 1.1 copy-start.2
  29.1 1.0 copy-start.5
  35.0 20.6 %all-to-all-start = ((bf16[32,112,128]{2,1,0:T(8,128)(2,1)}), bf16[32,112,128]{2,1,0:T(8,128)(2,1)S(1)}, u32[]{:S(2)}, u32[]{:S(2)}) async-start(bf16[32,112,128]{2,1,0:T(8,128)(2,1)} %bitcast.6), calls=%async_computation | async-start | bytes 1835008 | tf_op jit(solution)/shard_map/all_to_all | solution.py:342
  43.7 9.4 %collective-permute-start.3 = (bf16[80,128]{1,0:T(8,128)(2,1)S(1)}, bf16[80,128]{1,0:T(8,128)(2,1)S(1)}, u32[]{:S(2)}, u32[]{:S(2)}) collective-permute-start(bf16[80,128]{1,0:T(8,128)(2,1)S(1)} %dynamic-slice_bitcast_fusion), channel_id=1, source_target_pairs={{0,4},{1,5},{2,6},{3,7},{4,0},{5,1},{6,2},{7,3},{8,12},{9,13},{10,... | collective-permute-start | bytes 61448 | tf_op jit(solution)/shard_map/ppermute | solution.py:371
  56.4 12.0 %all-to-all-start.1 = ((bf16[4,192,128]{2,1,0:T(8,128)(2,1)}), bf16[4,192,128]{2,1,0:T(8,128)(2,1)S(1)}, u32[]{:S(2)}, u32[]{:S(2)}) async-start(bf16[4,192,128]{2,1,0:T(8,128)(2,1)} %broadcast_in_dim.6), calls=%async_computation.1 | async-start | bytes 393216 | tf_op jit(solution)/shard_map/all_to_all | solution.py:342
  60.2 8.2 %collective-permute-start.4 = (bf16[2,2,3,12,192]{4,3,2,1,0:T(8,128)(2,1)S(1)}, bf16[2,2,3,12,192]{4,3,2,1,0:T(8,128)(2,1)S(1)}, u32[]{:S(2)}, u32[]{:S(2)}) collective-permute-start(bf16[2,2,3,12,192]{4,3,2,1,0:T(8,128)(2,1)S(1)} %get-tuple-element.61), channel_id=1, source_target_pairs={{0,32},{32,64},{64,96},{96,128},{128,160},{160,192},{192,224},{224... | collective-permute-start | bytes 165896 | tf_op jit(solution)/shard_map/ppermute | solution.py:373
  69.2 11.0 %all-to-all-start.2 = ((bf16[4,192,128]{2,1,0:T(8,128)(2,1)}), bf16[4,192,128]{2,1,0:T(8,128)(2,1)S(1)}, u32[]{:S(2)}, u32[]{:S(2)}) async-start(bf16[4,192,128]{2,1,0:T(8,128)(2,1)} %broadcast_in_dim.7), calls=%async_computation.2 | async-start | bytes 393216 | tf_op jit(solution)/shard_map/all_to_all | solution.py:342
  72.6 10.3 %collective-permute-start.5 = (bf16[2,2,6,6,192]{4,3,2,1,0:T(8,128)(2,1)S(1)}, bf16[2,2,6,6,192]{4,3,2,1,0:T(8,128)(2,1)S(1)}, u32[]{:S(2)}, u32[]{:S(2)}) collective-permute-start(bf16[2,2,6,6,192]{4,3,2,1,0:T(8,128)(2,1)S(1)} %fusion.1), channel_id=1, source_target_pairs={{0,1},{1,2},{2,3},{3,4},{4,5},{5,6},{6,7},{7,8},{8,9},{9,10},{10,1... | collective-permute-start | bytes 165896 | tf_op jit(solution)/shard_map/ppermute | solution.py:377
  83.9 22.7 %all-to-all-start.3 = ((bf16[32,112,128]{2,1,0:T(8,128)(2,1)}), bf16[32,112,128]{2,1,0:T(8,128)(2,1)S(1)}, u32[]{:S(2)}, u32[]{:S(2)}) async-start(bf16[32,112,128]{2,1,0:T(8,128)(2,1)} %broadcast_in_dim.8), calls=%async_computation.3 | async-start | bytes 1835008 | tf_op jit(solution)/shard_map/all_to_all | solution.py:342
  91.6 12.5 %collective-permute-start.6 = (bf16[80,128]{1,0:T(8,128)(2,1)S(1)}, bf16[80,128]{1,0:T(8,128)(2,1)S(1)}, u32[]{:S(2)}, u32[]{:S(2)}) collective-permute-start(bf16[80,128]{1,0:T(8,128)(2,1)S(1)} %slice.63), channel_id=1, source_target_pairs={{0,4},{1,5},{2,6},{3,7},{4,0},{5,1},{6,2},{7,3},{8,12},{9,13},{10,... | collective-permute-start | bytes 61448 | tf_op jit(solution)/shard_map/ppermute | solution.py:383

commit v4 on v3

--- a/solution.py
+++ b/solution.py
@@ -19,6 +19,8 @@
 GROWS = 3584
 STEP = 44
 BROWS = 160
+LOW = 2
+FAR = 4
 EPS = 1e-05
 F32 = jnp.float32
 BF16 = jnp.bfloat16
@@ -152,7 +154,8 @@
 def block_kernel(
     x_ref,
     cot_ref,
-    gains_ref,
+    gain_one_ref,
+    gain_two_ref,
     qkv_ref,
     proj_ref,
     up_ref,
@@ -168,7 +171,8 @@
 ):
     factor = HEAD ** (-0.5)
     x = x_ref[...].astype(F32)
-    gain_one, gain_two = gains_ref[0:1], gains_ref[1:2]
+    gain_one = gain_one_ref[...]
+    gain_two = gain_two_ref[...]
     normal_one, inverse_one = norm_stats(x)
     normed = (normal_one * gain_one).astype(BF16)
     packed = dot(normed, qkv_ref[...]).astype(BF16)
@@ -272,49 +276,46 @@
     )(*args)
 
 
-def unpack_kernel(grads_ref, *refs):
-    outs, held, sems = refs[:6], refs[6:12], refs[12]
-    gain_one_ref, gain_two_ref, qkv_ref, proj_ref, up_ref, down_ref = held
+def unpack_kernel(
+    grads_ref, kept_ref, given_ref, gain_one_ref, gain_two_ref, qkv_ref, proj_ref, up_ref, down_ref, bias_ref
+):
     factor = TOKENS ** (-0.5)
-    copies = [pltpu.make_async_copy(held[k], outs[k], sems.at[k]) for k in range(6)]
 
     def rows(start, count):
         return grads_ref[start : start + count].astype(F32) * factor
 
     for t in range(6):
-        up_ref[:, LANES * t : LANES * (t + 1)] = rows(C * t, C)
-    copies[4].start()
-    for t in range(6):
-        down_ref[:, LANES * t : LANES * (t + 1)] = rows(C * (t + 6), C)
-    copies[5].start()
+        at = slice(LANES * t, LANES * (t + 1))
+        up_ref[:, at] = rows(C * t, C)
+        down_ref[:, at] = rows(C * (t + 6), C)
+        if t < 4:
+            qkv_ref[:, at] = rows(C * (t + 12), C)
     halves = rows(C * 17, C)
-    for t in range(4):
-        qkv_ref[:, LANES * t : LANES * (t + 1)] = rows(C * (t + 12), C)
     qkv_ref[:, 4 * LANES :] = halves[:, :64]
-    copies[2].start()
     proj_ref[:, :LANES] = rows(C * 16, C)
     proj_ref[:, LANES:] = halves[:, 64:]
-    copies[3].start()
     gains = rows(C * 18, 16)
     for k, ref in enumerate((gain_one_ref, gain_two_ref)):
         ref[...] = jnp.concatenate((gains[k : k + 1], gains[k + 2 : k + 3, : C - LANES]), axis=1)
-        copies[k].start()
-    for copy in copies:
-        copy.wait()
-
-
-def unpack(grads):
-    shapes = [(1, C), (1, C), (C, 3 * C), (C, C), (C, HID), (C, HID)]
+    first = lax.axis_index("lon") // FAR % LOW == 0
+    kept, given = kept_ref[...].astype(F32), given_ref[...].astype(F32)
+    sums = (jnp.where(first, kept, given), jnp.where(first, given, kept))
+    for h in range(HEADS):
+        for g in range(SLOTS):
+            half, row = divmod(h * SLOTS + g, BROWS // LOW)
+            count = min(LANES, NPOS - g * LANES)
+            bias_ref[h, :, g * LANES : g * LANES + count] = sums[half][row : row + 1, :count]
+
+
+def unpack(grads, kept, given):
+    shapes = [(1, C), (1, C), (C, 3 * C), (C, C), (C, HID), (C, HID), (HEADS, 1, NPOS)]
     return pl.pallas_call(
         unpack_kernel,
         out_shape=[jax.ShapeDtypeStruct(s, F32) for s in shapes],
-        in_specs=[pl.BlockSpec(memory_space=pltpu.VMEM)],
-        out_specs=[pl.BlockSpec(memory_space=pl.ANY)] * 6,
-        scratch_shapes=[pltpu.VMEM(s, F32) for s in shapes] + [pltpu.SemaphoreType.DMA((6,))],
         name="unpack",
         compiler_params=pltpu.CompilerParams(vmem_limit_bytes=16 * 1024 * 1024),
         cost_estimate=pl.CostEstimate(flops=500_000, bytes_accessed=2_700_000, transcendentals=0),
-    )(grads)
+    )(grads, kept, given)
 
 
 def neighbours(by):
@@ -348,7 +349,7 @@
 
 def finish(grid, grads, pairs, pos_flat):
     lat, lon = lax.axis_size("lat"), lax.axis_size("lon")
-    low, far = 2, 4
+    low, far = LOW, FAR
     high = lon // (low * far)
     place = lambda h, l, f: (h * low + l) * far + f
     over_low = spread_over(
@@ -371,18 +372,17 @@
     bias = total(jnp.stack((kept, lax.ppermute(given, "lon", other))))
     both = jnp.concatenate((mine, bias), axis=0)
     rows_got = lax.ppermute(grid[:, :, 3:], "lat", ring("lat", 1))
-    both = total(over_high(same(both, high)))
     both, rows_got = lax.optimization_barrier((both, rows_got))
     grid = jnp.concatenate((rows_got, grid[:, :, :3]), axis=2)
     cols_got = lax.ppermute(grid[:, :, :, 6:], "lon", ring("lon", 1))
+    both = total(over_high(same(both, high)))
+    both, cols_got = lax.optimization_barrier((both, cols_got))
     both = total(over_far(same(both, far)))
-    both, cols_got = lax.optimization_barrier((both, cols_got))
     grid = jnp.concatenate((cols_got, grid[:, :, :, :6]), axis=3)
     grads = over_low(same(both[:share], lat * low)).reshape(GROWS, LANES)
     kept = both[share:]
     given = lax.ppermute(kept, "lon", other)
-    first, second = jnp.where(at == 0, kept, given), jnp.where(at == 0, given, kept)
-    return grid, grads, jnp.concatenate((first, second), axis=0).astype(F32)
+    return grid, grads, kept, given
 
 
 def local(
@@ -404,16 +404,16 @@
     out, delta, grads, pairs = block(
         moved[0].reshape(WT, C),
         moved[1].reshape(WT, C),
-        jnp.stack((gain_one, gain_two)),
+        gain_one.reshape(1, C),
+        gain_two.reshape(1, C),
         qkv_weight,
         proj_weight,
         up_weight,
         down_weight.T,
         bias,
     )
-    back, grads, grad_bias = finish(jnp.stack((out, delta)).reshape((2,) + grid), grads, pairs, pos_flat)
-    totals = unpack(grads)
-    grad_bias = grad_bias[: HEADS * SLOTS].reshape(HEADS, SLOTS * LANES)[:, :NPOS]
+    back, grads, kept, given = finish(jnp.stack((out, delta)).reshape((2,) + grid), grads, pairs, pos_flat)
+    totals = unpack(grads, kept, given)
     return (
         back[0],
         back[1],
@@ -421,7 +421,7 @@
         totals[1].reshape(C),
         *totals[2:5],
         totals[5].T,
-        grad_bias.reshape(HEADS, 1, 1, NPOS),
+        totals[6].reshape(HEADS, 1, 1, NPOS),
     )
 
 

time: 109 us -> 106 us (0.972)
  blocking collectives: 0 us -> 10.5 us
  waiting for transfers between devices: 30.1 us -> 21.6 us
  local copies, waits for them, and re-layouts: 6.75 us -> 4.63 us
  starting transfers between devices: 54.3 us -> 52.2 us
    ppermute x1, starting transfers between devices: 2.17 us -> 14.4 us  [shift_in(): from_lon = lax.ppermute(grid[:, :, 3:, :6], 'lon', ring('lon', -1))]
    ppermute x1, starting transfers between devices: 15 us -> 3.01 us  [shift_in(): from_both = lax.ppermute(grid[:, :, :3, :6], ('lat', 'lon'), neighbours(-1))]
    all_to_all x0 -> x1, blocking collectives: none -> 10.5 us  [spread_over(): lax.all_to_all(parts, axis, 0, 0, axis_index_groups=groups)]
    all_to_all x4 -> x3, waiting for transfers between devices: 13.7 us -> 8.75 us  [spread_over(): lax.all_to_all(parts, axis, 0, 0, axis_index_groups=groups)]
    ppermute x1, waiting for transfers between devices: 6.1 us -> 2.42 us  [finish(): bias = total(jnp.stack((kept, lax.ppermute(given, 'lon', other))))]
    all_to_all x4 -> x3, starting transfers between devices: 20.4 us -> 16.9 us  [spread_over(): lax.all_to_all(parts, axis, 0, 0, axis_index_groups=groups)]
    ppermute x1, starting transfers between devices: 1.92 us -> 3.64 us  [finish(): rows_got = lax.ppermute(grid[:, :, 3:], 'lat', ring('lat', 1))]
  transfers between devices with their start and end apart: 11 -> 10, of which waited for: 7 -> 6; matrix products, arithmetic and copies ran while one was open for 2% -> 2% of each run, Pallas kernels for 7% -> 7%
where the time goes in v4:
time: 106 us
  starting transfers between devices  52.2 us (49%)
  waiting for transfers between devices  21.6 us (20%)
  Pallas kernels  14 us (13%)
  blocking collectives  10.5 us (10%)
  local copies, waits for them, and re-layouts  4.63 us (4%)
  other arithmetic  1.71 us (2%)
    all_to_all x3, starting transfers between devices, spread_over(): lax.all_to_all(parts, axis, 0, 0, axis_index_groups=groups)  16.9 us
    ppermute x1, starting transfers between devices, shift_in(): from_lon = lax.ppermute(grid[:, :, 3:, :6], 'lon', ring('lon', -1))  14.4 us
    all_to_all x1, blocking collectives, spread_over(): lax.all_to_all(parts, axis, 0, 0, axis_index_groups=groups)  10.5 us
    all_to_all x3, waiting for transfers between devices, spread_over(): lax.all_to_all(parts, axis, 0, 0, axis_index_groups=groups)  8.75 us
    ppermute x1, waiting for transfers between devices, finish(): given = lax.ppermute(kept, 'lon', other)  7.67 us
    pallas_call x1, Pallas kernels, bias_pairs(): pl.pallas_call(gather_kernel, out_shape=[jax.ShapeDtypeStruct((HEADS * WT...  4.86 us
    pallas_call x1, Pallas kernels, block(): pl.pallas_call(block_kernel, out_shape=[jax.ShapeDtypeStruct(s, d) for s,...  4.82 us
    ppermute x1, starting transfers between devices, finish(): cols_got = lax.ppermute(grid[:, :, :, 6:], 'lon', ring('lon', 1))  4.01 us
  transfers between devices with their start and end apart: 10, of which 6 were waited for; matrix products, arithmetic and copies ran while one was open for 2% of the time, Pallas kernels for 7%

profile of v4, /device:TPU:1, one launch (start us, length us, event | category | flops | bytes accessed | tf_op | source)
XLA Modules:
  0.0 105.7 jit_solution(9834662224070095777)
XLA Ops:
  0.7 1.1 %fusion.3 = (bf16[2,2,3,6,192]{4,1,3,2,0:T(2,128)(2,1)S(1)}, bf16[2,2,3,6,192]{4,1,3,2,0:T(2,128)(2,1)S(1)}, bf16[2,2,3,6,192]{4,1,3,2,0:T(2,128)(2,1)S(1)}, bf16[2,2,3,6,192]{4,1,3,2,0:T(2,128)(2,1)S(1)}) fusion(bf16[1,2,6,12,192]{4,1,3,2,0:T(2,128)(2,1)} %bitcast.30, bf16[1,2,6,12,192]{4,1,3,2,0:T(2,128)(2,1)} %bitcast.31), kind=kLoop, calls=%fused_computation.16 | loop fusion | flops 55296 | bytes 221184 | tf_op jit(solution)/shard_map/stack | solution.py:402
  1.8 14.4 %collective-permute-start = (bf16[2,2,3,6,192]{4,1,3,2,0:T(2,128)(2,1)S(1)}, bf16[2,2,3,6,192]{4,1,3,2,0:T(2,128)(2,1)S(1)}, u32[]{:S(2)}, u32[]{:S(2)}) collective-permute-start(bf16[2,2,3,6,192]{4,1,3,2,0:T(2,128)(2,1)S(1)} %get-tuple-element.77), channel_id=1, source_target_pairs={{0,31},{1,0},{2,1},{3,2},{4,3},{5,4},{6,5},{7,6},{8,7},{9,8},{10,9... | collective-permute-start | bytes 82952 | tf_op jit(solution)/shard_map/ppermute | solution.py:335
  16.2 3.0 %collective-permute-start.2 = (bf16[2,2,3,6,192]{4,1,3,2,0:T(2,128)(2,1)S(1)}, bf16[2,2,3,6,192]{4,1,3,2,0:T(2,128)(2,1)S(1)}, u32[]{:S(2)}, u32[]{:S(2)}) collective-permute-start(bf16[2,2,3,6,192]{4,1,3,2,0:T(2,128)(2,1)S(1)} %get-tuple-element.78), channel_id=1, source_target_pairs={{0,511},{1,480},{2,481},{3,482},{4,483},{5,484},{6,485},{7,486},{8... | collective-permute-start | bytes 82952 | tf_op jit(solution)/shard_map/ppermute | solution.py:336
  19.2 3.7 %collective-permute-start.1 = (bf16[2,2,3,6,192]{4,1,3,2,0:T(2,128)(2,1)S(1)}, bf16[2,2,3,6,192]{4,1,3,2,0:T(2,128)(2,1)S(1)}, u32[]{:S(2)}, u32[]{:S(2)}) collective-permute-start(bf16[2,2,3,6,192]{4,1,3,2,0:T(2,128)(2,1)S(1)} %get-tuple-element.79), channel_id=1, source_target_pairs={{0,480},{32,0},{64,32},{96,64},{128,96},{160,128},{192,160},{224,1... | collective-permute-start | bytes 82952 | tf_op jit(solution)/shard_map/ppermute | solution.py:334
  23.0 4.9 %bias_pairs.1 = (f32[864,144]{1,0:T(8,128)S(1)}, s32[176,128]{1,0:T(8,128)S(1)}) custom-call(f32[6,1,3312]{2,1,0:T(1,128)S(1)} %bitcast.24, s32[144,144]{1,0:T(8,128)S(1)} %copy-done, s32[1,144]{1,0:T(1,128)S(1)} %reshape.62.mask_ref), custom_call_target="tpu_custom_call" | custom-call | flops 10000000 | bytes 1200000 | tf_op jit(solution)/shard_map/bias_pairs/pallas_call | solution.py:104
  27.9 0.2 maximum_maximum_fusion
  28.2 0.1 fusion.6
  28.5 0.6 copy-done.4
  29.1 0.2 copy-done.3
  29.3 0.1 copy-done.2
  29.4 4.8 %block.1 = (bf16[144,192]{1,0:T(8,128)(2,1)S(1)}, bf16[144,192]{1,0:T(8,128)(2,1)S(1)}, bf16[3584,128]{1,0:T(8,128)(2,1)}, f32[6,176,128]{2,1,0:T(8,128)S(1)}) custom-call(bf16[144,192]{1,0:T(8,128)(2,1)S(1)} %reshape_squeeze.6.x_ref, bf16[144,192]{1,0:T(8,128)(2,1)S(1)} %reshape_squeeze.7.cot_ref, f32[1,192]{1,0:T(1,128)S(1)} %bitcast.28, ...), custom_call_target="tpu_custom_call" | custom-call | flops 900000000 | bytes 4000000 | tf_op jit(solution)/shard_map/block/pallas_call | solution.py:265
  34.3 5.6 %all-to-all-start = ((bf16[32,112,128]{2,1,0:T(8,128)(2,1)}), bf16[32,112,128]{2,1,0:T(8,128)(2,1)S(1)}, u32[]{:S(2)}, u32[]{:S(2)}) async-start(bf16[32,112,128]{2,1,0:T(8,128)(2,1)} %bitcast.6), calls=%async_computation | async-start | bytes 1835008 | tf_op jit(solution)/shard_map/all_to_all | solution.py:343
  39.9 3.0 %bias_grad.1 = bf16[160,128]{1,0:T(8,128)(2,1)S(1)} custom-call(f32[6,176,128]{2,1,0:T(8,128)S(1)} %get-tuple-element.28.pairs_ref, s32[176,128]{1,0:T(8,128)S(1)} %get-tuple-element.29.pos_ref), custom_call_target="tpu_custom_call" | custom-call | flops 1100000000 | bytes 700000 | tf_op jit(solution)/shard_map/bias_grad/pallas_call | solution.py:144
  42.9 3.3 %collective-permute-start.3 = (bf16[80,128]{1,0:T(8,128)(2,1)S(1)}, bf16[80,128]{1,0:T(8,128)(2,1)S(1)}, u32[]{:S(2)}, u32[]{:S(2)}) collective-permute-start(bf16[80,128]{1,0:T(8,128)(2,1)S(1)} %dynamic-slice_bitcast_fusion), channel_id=1, source_target_pairs={{0,4},{1,5},{2,6},{3,7},{4,0},{5,1},{6,2},{7,3},{8,12},{9,13},{10,... | collective-permute-start | bytes 61448 | tf_op jit(solution)/shard_map/ppermute | solution.py:372
  46.3 3.6 %collective-permute-start.4 = (bf16[2,2,3,12,192]{4,3,2,1,0:T(8,128)(2,1)S(1)}, bf16[2,2,3,12,192]{4,3,2,1,0:T(8,128)(2,1)S(1)}, u32[]{:S(2)}, u32[]{:S(2)}) collective-permute-start(bf16[2,2,3,12,192]{4,3,2,1,0:T(8,128)(2,1)S(1)} %get-tuple-element.72), channel_id=1, source_target_pairs={{0,32},{32,64},{64,96},{96,128},{128,160},{160,192},{192,224},{224... | collective-permute-start | bytes 165896 | tf_op jit(solution)/shard_map/ppermute | solution.py:374
  50.0 2.4 %collective-permute-done.3 = bf16[80,128]{1,0:T(8,128)(2,1)S(1)} collective-permute-done((bf16[80,128]{1,0:T(8,128)(2,1)S(1)}, bf16[80,128]{1,0:T(8,128)(2,1)S(1)}, u32[]{:S(2)}, u32[]{:S(2)}) %collective-permute-start.3) | collective-permute-done | bytes 20512 | tf_op jit(solution)/shard_map/ppermute | solution.py:372
  52.4 2.6 %all-to-all-done = bf16[32,112,128]{2,1,0:T(8,128)(2,1)S(1)} async-done(((bf16[32,112,128]{2,1,0:T(8,128)(2,1)}), bf16[32,112,128]{2,1,0:T(8,128)(2,1)S(1)}, u32[]{:S(2)}, u32[]{:S(2)}) %all-to-all-start) | async-done | bytes 917536 | tf_op jit(solution)/shard_map/all_to_all | solution.py:343
  55.0 0.1 reduce_sum.48
  55.1 0.7 broadcast_in_dim.6
  55.8 3.8 %all-to-all-start.1 = ((bf16[4,192,128]{2,1,0:T(8,128)(2,1)}), bf16[4,192,128]{2,1,0:T(8,128)(2,1)S(1)}, u32[]{:S(2)}, u32[]{:S(2)}) async-start(bf16[4,192,128]{2,1,0:T(8,128)(2,1)} %broadcast_in_dim.6), calls=%async_computation.1 | async-start | bytes 393216 | tf_op jit(solution)/shard_map/all_to_all | solution.py:343
  59.7 4.0 %collective-permute-start.5 = (bf16[2,2,6,6,192]{4,3,2,1,0:T(8,128)(2,1)S(1)}, bf16[2,2,6,6,192]{4,3,2,1,0:T(8,128)(2,1)S(1)}, u32[]{:S(2)}, u32[]{:S(2)}) collective-permute-start(bf16[2,2,6,6,192]{4,3,2,1,0:T(8,128)(2,1)S(1)} %fusion.1), channel_id=1, source_target_pairs={{0,1},{1,2},{2,3},{3,4},{4,5},{5,6},{6,7},{7,8},{8,9},{9,10},{10,1... | collective-permute-start | bytes 165896 | tf_op jit(solution)/shard_map/ppermute | solution.py:377
  63.7 3.7 %all-to-all-done.1 = bf16[4,192,128]{2,1,0:T(8,128)(2,1)S(1)} async-done(((bf16[4,192,128]{2,1,0:T(8,128)(2,1)}), bf16[4,192,128]{2,1,0:T(8,128)(2,1)S(1)}, u32[]{:S(2)}, u32[]{:S(2)}) %all-to-all-start.1) | async-done | bytes 196640 | tf_op jit(solution)/shard_map/all_to_all | solution.py:343
  67.4 2.8 %collective-permute-done.5 = bf16[2,2,6,6,192]{4,3,2,1,0:T(8,128)(2,1)S(1)} collective-permute-done((bf16[2,2,6,6,192]{4,3,2,1,0:T(8,128)(2,1)S(1)}, bf16[2,2,6,6,192]{4,3,2,1,0:T(8,128)(2,1)S(1)}, u32[]{:S(2)}, u32[]{:S(2)}) %collective-permute-start.5) | collective-permute-done | bytes 55328 | tf_op jit(solution)/shard_map/ppermute | solution.py:377
  70.2 10.5 %all_to_all.20 = bf16[4,192,128]{2,1,0:T(8,128)(2,1)S(1)} all-to-all(bf16[4,192,128]{2,1,0:T(8,128)(2,1)S(1)} %broadcast_in_dim.7), channel_id=1, replica_groups={{0,1,2,3},{4,5,6,7},{8,9,10,11},{12,13,14,15},{16,17,18,19},{20,21,22,2..., dimensions={0} | all-to-all | bytes 393216 | tf_op jit(solution)/shard_map/all_to_all | solution.py:343
  80.8 1.1 broadcast_in_dim.8
  81.8 7.5 %all-to-all-start.3 = ((bf16[32,112,128]{2,1,0:T(8,128)(2,1)}), bf16[32,112,128]{2,1,0:T(8,128)(2,1)S(1)}, u32[]{:S(2)}, u32[]{:S(2)}) async-start(bf16[32,112,128]{2,1,0:T(8,128)(2,1)} %broadcast_in_dim.8), calls=%async_computation.3 | async-start | bytes 1835008 | tf_op jit(solution)/shard_map/all_to_all | solution.py:343
  89.4 3.3 %collective-permute-start.6 = (bf16[80,128]{1,0:T(8,128)(2,1)S(1)}, bf16[80,128]{1,0:T(8,128)(2,1)S(1)}, u32[]{:S(2)}, u32[]{:S(2)}) collective-permute-start(bf16[80,128]{1,0:T(8,128)(2,1)S(1)} %slice.71.kept_ref), channel_id=1, source_target_pairs={{0,4},{1,5},{2,6},{3,7},{4,0},{5,1},{6,2},{7,3},{8,12},{9,13},{10,... | collective-permute-start | bytes 61448 | tf_op jit(solution)/shard_map/ppermute | solution.py:384
  92.8 0.7 copy.36
  93.5 0.7 copy.35
  94.2 7.7 %collective-permute-done.6.given_ref = bf16[80,128]{1,0:T(8,128)(2,1)S(1)} collective-permute-done((bf16[80,128]{1,0:T(8,128)(2,1)S(1)}, bf16[80,128]{1,0:T(8,128)(2,1)S(1)}, u32[]{:S(2)}, u32[]{:S(2)}) %collective-permute-start.6) | collective-permute-done | bytes 20512 | tf_op jit(solution)/shard_map/ppermute | solution.py:384
  101.8 2.5 %all-to-all-done.3 = bf16[32,112,128]{2,1,0:T(8,128)(2,1)S(1)} async-done(((bf16[32,112,128]{2,1,0:T(8,128)(2,1)}), bf16[32,112,128]{2,1,0:T(8,128)(2,1)S(1)}, u32[]{:S(2)}, u32[]{:S(2)}) %all-to-all-start.3) | async-done | bytes 917536 | tf_op jit(solution)/shard_map/all_to_all | solution.py:343
  104.3 1.4 %unpack.1 = (f32[1,192]{1,0:T(1,128)}, f32[1,192]{1,0:T(1,128)}, f32[192,576]{1,0:T(8,128)}, f32[192,192]{1,0:T(8,128)}, f32[192,768]{1,0:T(8,128)}, /*index=5*/f32[192,768]{1,0:T(8,128)}, f32[6,1,3312]{2,1,0:T(1,128)}) custom-call(bf16[3584,128]{1,0:T(8,128)(2,1)S(1)} %bitcast.23, bf16[80,128]{1,0:T(8,128)(2,1)S(1)} %slice.71.kept_ref, ...), custom_call_target="tpu_custom_call" | custom-call | flops 500000 | bytes 2700000 | tf_op jit(solution)/shard_map/unpack/pallas_call | solution.py:312
  (42 shorter events, 0.7 us)
Async XLA Ops:
  0.6 22.3 %copy-start.8 = (s32[2,6,12]{2,0,1:T(2,128)S(1)}, s32[2,6,12]{2,0,1:T(2,128)}, u32[]{:S(2)}) copy-start(s32[2,6,12]{2,0,1:T(2,128)} %param.20) | copy-start | bytes 1732
  0.7 22.4 %copy-start = (s32[144,144]{1,0:T(8,128)S(1)}, s32[144,144]{1,0:T(8,128)}, u32[]{:S(2)}) copy-start(s32[144,144]{1,0:T(8,128)} %pos_ref.1) | copy-start | bytes 248836
  0.7 22.4 %copy-start.1 = (f32[6,1,1,3312]{3,2,1,0:T(1,128)S(1)}, f32[6,1,1,3312]{3,2,1,0:T(1,128)}, u32[]{:S(2)}) copy-start(f32[6,1,1,3312]{3,2,1,0:T(1,128)} %param.18) | copy-start | bytes 238468
  1.8 26.1 %collective-permute-start = (bf16[2,2,3,6,192]{4,1,3,2,0:T(2,128)(2,1)S(1)}, bf16[2,2,3,6,192]{4,1,3,2,0:T(2,128)(2,1)S(1)}, u32[]{:S(2)}, u32[]{:S(2)}) collective-permute-start(bf16[2,2,3,6,192]{4,1,3,2,0:T(2,128)(2,1)S(1)} %get-tuple-element.77), channel_id=1, source_target_pairs={{0,31},{1,0},{2,1},{3,2},{4,3},{5,4},{6,5},{7,6},{8,7},{9,8},{10,9... | collective-permute-start | bytes 82952 | tf_op jit(solution)/shard_map/ppermute | solution.py:335
  16.2 11.7 %collective-permute-start.2 = (bf16[2,2,3,6,192]{4,1,3,2,0:T(2,128)(2,1)S(1)}, bf16[2,2,3,6,192]{4,1,3,2,0:T(2,128)(2,1)S(1)}, u32[]{:S(2)}, u32[]{:S(2)}) collective-permute-start(bf16[2,2,3,6,192]{4,1,3,2,0:T(2,128)(2,1)S(1)} %get-tuple-element.78), channel_id=1, source_target_pairs={{0,511},{1,480},{2,481},{3,482},{4,483},{5,484},{6,485},{7,486},{8... | collective-permute-start | bytes 82952 | tf_op jit(solution)/shard_map/ppermute | solution.py:336
  19.2 8.7 %collective-permute-start.1 = (bf16[2,2,3,6,192]{4,1,3,2,0:T(2,128)(2,1)S(1)}, bf16[2,2,3,6,192]{4,1,3,2,0:T(2,128)(2,1)S(1)}, u32[]{:S(2)}, u32[]{:S(2)}) collective-permute-start(bf16[2,2,3,6,192]{4,1,3,2,0:T(2,128)(2,1)S(1)} %get-tuple-element.79), channel_id=1, source_target_pairs={{0,480},{32,0},{64,32},{96,64},{128,96},{160,128},{192,160},{224,1... | collective-permute-start | bytes 82952 | tf_op jit(solution)/shard_map/ppermute | solution.py:334
  28.2 0.9 copy-start.4
  28.3 1.0 copy-start.3
  28.3 1.1 copy-start.2
  28.4 1.0 copy-start.5
  28.4 1.0 copy-start.7
  28.5 1.0 copy-start.6
  34.3 20.7 %all-to-all-start = ((bf16[32,112,128]{2,1,0:T(8,128)(2,1)}), bf16[32,112,128]{2,1,0:T(8,128)(2,1)S(1)}, u32[]{:S(2)}, u32[]{:S(2)}) async-start(bf16[32,112,128]{2,1,0:T(8,128)(2,1)} %bitcast.6), calls=%async_computation | async-start | bytes 1835008 | tf_op jit(solution)/shard_map/all_to_all | solution.py:343
  42.9 9.5 %collective-permute-start.3 = (bf16[80,128]{1,0:T(8,128)(2,1)S(1)}, bf16[80,128]{1,0:T(8,128)(2,1)S(1)}, u32[]{:S(2)}, u32[]{:S(2)}) collective-permute-start(bf16[80,128]{1,0:T(8,128)(2,1)S(1)} %dynamic-slice_bitcast_fusion), channel_id=1, source_target_pairs={{0,4},{1,5},{2,6},{3,7},{4,0},{5,1},{6,2},{7,3},{8,12},{9,13},{10,... | collective-permute-start | bytes 61448 | tf_op jit(solution)/shard_map/ppermute | solution.py:372
  46.3 8.8 %collective-permute-start.4 = (bf16[2,2,3,12,192]{4,3,2,1,0:T(8,128)(2,1)S(1)}, bf16[2,2,3,12,192]{4,3,2,1,0:T(8,128)(2,1)S(1)}, u32[]{:S(2)}, u32[]{:S(2)}) collective-permute-start(bf16[2,2,3,12,192]{4,3,2,1,0:T(8,128)(2,1)S(1)} %get-tuple-element.72), channel_id=1, source_target_pairs={{0,32},{32,64},{64,96},{96,128},{128,160},{160,192},{192,224},{224... | collective-permute-start | bytes 165896 | tf_op jit(solution)/shard_map/ppermute | solution.py:374
  55.8 11.6 %all-to-all-start.1 = ((bf16[4,192,128]{2,1,0:T(8,128)(2,1)}), bf16[4,192,128]{2,1,0:T(8,128)(2,1)S(1)}, u32[]{:S(2)}, u32[]{:S(2)}) async-start(bf16[4,192,128]{2,1,0:T(8,128)(2,1)} %broadcast_in_dim.6), calls=%async_computation.1 | async-start | bytes 393216 | tf_op jit(solution)/shard_map/all_to_all | solution.py:343
  59.7 10.5 %collective-permute-start.5 = (bf16[2,2,6,6,192]{4,3,2,1,0:T(8,128)(2,1)S(1)}, bf16[2,2,6,6,192]{4,3,2,1,0:T(8,128)(2,1)S(1)}, u32[]{:S(2)}, u32[]{:S(2)}) collective-permute-start(bf16[2,2,6,6,192]{4,3,2,1,0:T(8,128)(2,1)S(1)} %fusion.1), channel_id=1, source_target_pairs={{0,1},{1,2},{2,3},{3,4},{4,5},{5,6},{6,7},{7,8},{8,9},{9,10},{10,1... | collective-permute-start | bytes 165896 | tf_op jit(solution)/shard_map/ppermute | solution.py:377
  81.8 22.5 %all-to-all-start.3 = ((bf16[32,112,128]{2,1,0:T(8,128)(2,1)}), bf16[32,112,128]{2,1,0:T(8,128)(2,1)S(1)}, u32[]{:S(2)}, u32[]{:S(2)}) async-start(bf16[32,112,128]{2,1,0:T(8,128)(2,1)} %broadcast_in_dim.8), calls=%async_computation.3 | async-start | bytes 1835008 | tf_op jit(solution)/shard_map/all_to_all | solution.py:343
  89.4 12.4 %collective-permute-start.6 = (bf16[80,128]{1,0:T(8,128)(2,1)S(1)}, bf16[80,128]{1,0:T(8,128)(2,1)S(1)}, u32[]{:S(2)}, u32[]{:S(2)}) collective-permute-start(bf16[80,128]{1,0:T(8,128)(2,1)S(1)} %slice.71.kept_ref), channel_id=1, source_target_pairs={{0,4},{1,5},{2,6},{3,7},{4,0},{5,1},{6,2},{7,3},{8,12},{9,13},{10,... | collective-permute-start | bytes 61448 | tf_op jit(solution)/shard_map/ppermute | solution.py:384

commit v5 on v4

--- a/solution.py
+++ b/solution.py
@@ -331,12 +331,19 @@
 
 
 def shift_in(grid):
-    from_lat = lax.ppermute(grid[:, :, :3, 6:], "lat", ring("lat", -1))
-    from_lon = lax.ppermute(grid[:, :, 3:, :6], "lon", ring("lon", -1))
-    from_both = lax.ppermute(grid[:, :, :3, :6], ("lat", "lon"), neighbours(-1))
+    def moved(piece, axis, pairs):
+        return lax.ppermute(piece.reshape(-1, C), axis, pairs).reshape(piece.shape)
+
+    from_lat = moved(grid[:, :, :3, 6:], "lat", ring("lat", -1))
+    from_lon = moved(grid[:, :, 3:, :6], "lon", ring("lon", -1))
+    from_both = moved(grid[:, :, :3, :6], ("lat", "lon"), neighbours(-1))
     top = jnp.concatenate((grid[:, :, 3:, 6:], from_lon), axis=3)
     low = jnp.concatenate((from_lat, from_both), axis=3)
     return jnp.concatenate((top, low), axis=2)
+
+
+def flat_permute(piece, axis):
+    return lax.ppermute(piece.reshape(-1, C), axis, ring(axis, 1)).reshape(piece.shape)
 
 
 def spread_over(axis, groups=None):
@@ -371,10 +378,10 @@
     given = lax.dynamic_index_in_dim(own, 1 - at, 0, keepdims=False)
     bias = total(jnp.stack((kept, lax.ppermute(given, "lon", other))))
     both = jnp.concatenate((mine, bias), axis=0)
-    rows_got = lax.ppermute(grid[:, :, 3:], "lat", ring("lat", 1))
+    rows_got = flat_permute(grid[:, :, 3:], "lat")
     both, rows_got = lax.optimization_barrier((both, rows_got))
     grid = jnp.concatenate((rows_got, grid[:, :, :3]), axis=2)
-    cols_got = lax.ppermute(grid[:, :, :, 6:], "lon", ring("lon", 1))
+    cols_got = flat_permute(grid[:, :, :, 6:], "lon")
     both = total(over_high(same(both, high)))
     both, cols_got = lax.optimization_barrier((both, cols_got))
     both = total(over_far(same(both, far)))

time: 106 us -> 106 us (level)
  other arithmetic: 1.71 us -> 0.48 us
  local copies, waits for them, and re-layouts: 4.63 us -> 5.81 us
    ppermute x5, waiting for transfers between devices: 2.78 us -> 7.23 us  [the longest x2 7.22 us: flat_permute(): lax.ppermute(piece.reshape(-1, C), axis, ring(axis, 1)).reshape(piece.shape)]
    all_to_all x3, waiting for transfers between devices: 8.75 us -> 4.97 us  [spread_over(): lax.all_to_all(parts, axis, 0, 0, axis_index_groups=groups)]
    all_to_all x3, starting transfers between devices: 16.9 us -> 14.7 us  [spread_over(): lax.all_to_all(parts, axis, 0, 0, axis_index_groups=groups)]
    ppermute x5, starting transfers between devices: 28.7 us -> 30.1 us  [the longest x3 22.4 us: moved(): return lax.ppermute(piece.reshape(-1, C), axis, pairs).reshape(piece.shape)]
    another operation x1, other arithmetic: 1.12 us -> 0.05 us  [local(): moved = shift_in(jnp.stack((tokens, cotangent)))]
  transfers between devices with their start and end apart: 10 -> 10, of which waited for: 6 -> 5; matrix products, arithmetic and copies ran while one was open for 2% -> 2% of each run, Pallas kernels for 7% -> 7%
where the time goes in v5:
time: 106 us; the launch traced here: 105 us
  starting transfers between devices  51.4 us (48%)
  waiting for transfers between devices  22.2 us (21%)
  Pallas kernels  14 us (13%)
  blocking collectives  10.4 us (10%)
  local copies, waits for them, and re-layouts  5.81 us (5%)
    ppermute x3, starting transfers between devices, moved(): return lax.ppermute(piece.reshape(-1, C), axis, pairs).reshape(piece.shape)  22.4 us
    all_to_all x3, starting transfers between devices, spread_over(): lax.all_to_all(parts, axis, 0, 0, axis_index_groups=groups)  14.7 us
    all_to_all x1, blocking collectives, spread_over(): lax.all_to_all(parts, axis, 0, 0, axis_index_groups=groups)  10.4 us
    ppermute x1, waiting for transfers between devices, finish(): given = lax.ppermute(kept, 'lon', other)  7.67 us
    ppermute x2, starting transfers between devices, flat_permute(): lax.ppermute(piece.reshape(-1, C), axis, ring(axis, 1)).reshape(piece.shape)  7.65 us
    ppermute x2, waiting for transfers between devices, flat_permute(): lax.ppermute(piece.reshape(-1, C), axis, ring(axis, 1)).reshape(piece.shape)  7.22 us
    all_to_all x3, waiting for transfers between devices, spread_over(): lax.all_to_all(parts, axis, 0, 0, axis_index_groups=groups)  4.97 us
    pallas_call x1, Pallas kernels, bias_pairs(): pl.pallas_call(gather_kernel, out_shape=[jax.ShapeDtypeStruct((HEADS * WT...  4.86 us
  transfers between devices with their start and end apart: 10, of which 5 were waited for; matrix products, arithmetic and copies ran while one was open for 2% of the time, Pallas kernels for 7%

profile of v5, /device:TPU:1, one launch (start us, length us, event | category | flops | bytes accessed | tf_op | source)
XLA Modules:
  0.0 105.3 jit_solution(13231802155260867374)
XLA Ops:
  0.6 0.9 copy_bitcast_fusion
  1.7 8.9 %collective-permute-start.1 = (bf16[72,192]{1,0:T(8,128)(2,1)S(1)}, bf16[72,192]{1,0:T(8,128)(2,1)S(1)}, u32[]{:S(2)}, u32[]{:S(2)}) collective-permute-start(bf16[72,192]{1,0:T(8,128)(2,1)S(1)} %reshape.91), channel_id=1, source_target_pairs={{0,480},{32,0},{64,32},{96,64},{128,96},{160,128},{192,160},{224,1... | collective-permute-start | bytes 82952 | tf_op jit(solution)/shard_map/ppermute | solution.py:335
  10.7 11.3 %collective-permute-start.2 = (bf16[72,192]{1,0:T(8,128)(2,1)S(1)}, bf16[72,192]{1,0:T(8,128)(2,1)S(1)}, u32[]{:S(2)}, u32[]{:S(2)}) collective-permute-start(bf16[72,192]{1,0:T(8,128)(2,1)S(1)} %reshape.93), channel_id=1, source_target_pairs={{0,511},{1,480},{2,481},{3,482},{4,483},{5,484},{6,485},{7,486},{8... | collective-permute-start | bytes 82952 | tf_op jit(solution)/shard_map/ppermute | solution.py:335
  22.0 2.2 %collective-permute-start = (bf16[72,192]{1,0:T(8,128)(2,1)S(1)}, bf16[72,192]{1,0:T(8,128)(2,1)S(1)}, u32[]{:S(2)}, u32[]{:S(2)}) collective-permute-start(bf16[72,192]{1,0:T(8,128)(2,1)S(1)} %reshape.89), channel_id=1, source_target_pairs={{0,31},{1,0},{2,1},{3,2},{4,3},{5,4},{6,5},{7,6},{8,7},{9,8},{10,9... | collective-permute-start | bytes 82952 | tf_op jit(solution)/shard_map/ppermute | solution.py:335
  24.3 0.1 reshape.98.mask_ref
  24.4 4.9 %bias_pairs.1 = (f32[864,144]{1,0:T(8,128)S(1)}, s32[176,128]{1,0:T(8,128)S(1)}) custom-call(f32[6,1,3312]{2,1,0:T(1,128)S(1)} %bitcast.26, s32[144,144]{1,0:T(8,128)S(1)} %copy-done, s32[1,144]{1,0:T(1,128)S(1)} %reshape.98.mask_ref), custom_call_target="tpu_custom_call" | custom-call | flops 10000000 | bytes 1200000 | tf_op jit(solution)/shard_map/bias_pairs/pallas_call | solution.py:104
  29.4 0.1 maximum_maximum_fusion
  29.6 0.7 copy-done.4
  30.3 0.2 copy-done.2
  30.4 0.1 copy-done.3
  30.6 4.8 %block.1 = (bf16[144,192]{1,0:T(8,128)(2,1)S(1)}, bf16[144,192]{1,0:T(8,128)(2,1)S(1)}, bf16[3584,128]{1,0:T(8,128)(2,1)}, f32[6,176,128]{2,1,0:T(8,128)S(1)}) custom-call(bf16[144,192]{1,0:T(8,128)(2,1)S(1)} %reshape_squeeze.6.x_ref, bf16[144,192]{1,0:T(8,128)(2,1)S(1)} %reshape_squeeze.7.cot_ref, f32[1,192]{1,0:T(1,128)S(1)} %bitcast.30, ...), custom_call_target="tpu_custom_call" | custom-call | flops 900000000 | bytes 4000000 | tf_op jit(solution)/shard_map/block/pallas_call | solution.py:265
  35.4 3.8 %all-to-all-start = ((bf16[32,112,128]{2,1,0:T(8,128)(2,1)}), bf16[32,112,128]{2,1,0:T(8,128)(2,1)S(1)}, u32[]{:S(2)}, u32[]{:S(2)}) async-start(bf16[32,112,128]{2,1,0:T(8,128)(2,1)} %bitcast.6), calls=%async_computation | async-start | bytes 1835008 | tf_op jit(solution)/shard_map/all_to_all | solution.py:350
  39.2 3.0 %bias_grad.1 = bf16[160,128]{1,0:T(8,128)(2,1)S(1)} custom-call(f32[6,176,128]{2,1,0:T(8,128)S(1)} %get-tuple-element.28.pairs_ref, s32[176,128]{1,0:T(8,128)S(1)} %get-tuple-element.29.pos_ref), custom_call_target="tpu_custom_call" | custom-call | flops 1100000000 | bytes 700000 | tf_op jit(solution)/shard_map/bias_grad/pallas_call | solution.py:144
  42.2 3.3 %collective-permute-start.3 = (bf16[80,128]{1,0:T(8,128)(2,1)S(1)}, bf16[80,128]{1,0:T(8,128)(2,1)S(1)}, u32[]{:S(2)}, u32[]{:S(2)}) collective-permute-start(bf16[80,128]{1,0:T(8,128)(2,1)S(1)} %dynamic-slice_bitcast_fusion), channel_id=1, source_target_pairs={{0,4},{1,5},{2,6},{3,7},{4,0},{5,1},{6,2},{7,3},{8,12},{9,13},{10,... | collective-permute-start | bytes 61448 | tf_op jit(solution)/shard_map/ppermute | solution.py:379
  45.6 3.6 %collective-permute-start.4 = (bf16[144,192]{1,0:T(8,128)(2,1)S(1)}, bf16[144,192]{1,0:T(8,128)(2,1)S(1)}, u32[]{:S(2)}, u32[]{:S(2)}) collective-permute-start(bf16[144,192]{1,0:T(8,128)(2,1)S(1)} %reshape.101), channel_id=1, source_target_pairs={{0,32},{32,64},{64,96},{96,128},{128,160},{160,192},{192,224},{224... | collective-permute-start | bytes 165896 | tf_op jit(solution)/shard_map/ppermute | solution.py:346
  49.3 2.4 %collective-permute-done.3 = bf16[80,128]{1,0:T(8,128)(2,1)S(1)} collective-permute-done((bf16[80,128]{1,0:T(8,128)(2,1)S(1)}, bf16[80,128]{1,0:T(8,128)(2,1)S(1)}, u32[]{:S(2)}, u32[]{:S(2)}) %collective-permute-start.3) | collective-permute-done | bytes 20512 | tf_op jit(solution)/shard_map/ppermute | solution.py:379
  51.7 2.5 %all-to-all-done = bf16[32,112,128]{2,1,0:T(8,128)(2,1)S(1)} async-done(((bf16[32,112,128]{2,1,0:T(8,128)(2,1)}), bf16[32,112,128]{2,1,0:T(8,128)(2,1)S(1)}, u32[]{:S(2)}, u32[]{:S(2)}) %all-to-all-start) | async-done | bytes 917536 | tf_op jit(solution)/shard_map/all_to_all | solution.py:350
  54.2 0.1 reduce_sum.48
  54.4 0.7 broadcast_in_dim.6
  55.1 4.0 %all-to-all-start.1 = ((bf16[4,192,128]{2,1,0:T(8,128)(2,1)}), bf16[4,192,128]{2,1,0:T(8,128)(2,1)S(1)}, u32[]{:S(2)}, u32[]{:S(2)}) async-start(bf16[4,192,128]{2,1,0:T(8,128)(2,1)} %broadcast_in_dim.6), calls=%async_computation.1 | async-start | bytes 393216 | tf_op jit(solution)/shard_map/all_to_all | solution.py:350
  59.2 4.0 %collective-permute-start.5 = (bf16[144,192]{1,0:T(8,128)(2,1)S(1)}, bf16[144,192]{1,0:T(8,128)(2,1)S(1)}, u32[]{:S(2)}, u32[]{:S(2)}) collective-permute-start(bf16[144,192]{1,0:T(8,128)(2,1)S(1)} %reshape.103), channel_id=1, source_target_pairs={{0,1},{1,2},{2,3},{3,4},{4,5},{5,6},{6,7},{7,8},{8,9},{9,10},{10,1... | collective-permute-start | bytes 165896 | tf_op jit(solution)/shard_map/ppermute | solution.py:346
  63.2 7.2 %collective-permute-done.5 = bf16[144,192]{1,0:T(8,128)(2,1)S(1)} collective-permute-done((bf16[144,192]{1,0:T(8,128)(2,1)S(1)}, bf16[144,192]{1,0:T(8,128)(2,1)S(1)}, u32[]{:S(2)}, u32[]{:S(2)}) %collective-permute-start.5) | collective-permute-done | bytes 55328 | tf_op jit(solution)/shard_map/ppermute | solution.py:346
  70.5 10.4 %all_to_all.20 = bf16[4,192,128]{2,1,0:T(8,128)(2,1)S(1)} all-to-all(bf16[4,192,128]{2,1,0:T(8,128)(2,1)S(1)} %broadcast_in_dim.7), channel_id=1, replica_groups={{0,1,2,3},{4,5,6,7},{8,9,10,11},{12,13,14,15},{16,17,18,19},{20,21,22,2..., dimensions={0} | all-to-all | bytes 393216 | tf_op jit(solution)/shard_map/all_to_all | solution.py:350
  81.0 1.1 broadcast_in_dim.8
  82.0 7.0 %all-to-all-start.3 = ((bf16[32,112,128]{2,1,0:T(8,128)(2,1)}), bf16[32,112,128]{2,1,0:T(8,128)(2,1)S(1)}, u32[]{:S(2)}, u32[]{:S(2)}) async-start(bf16[32,112,128]{2,1,0:T(8,128)(2,1)} %broadcast_in_dim.8), calls=%async_computation.3 | async-start | bytes 1835008 | tf_op jit(solution)/shard_map/all_to_all | solution.py:350
  89.0 0.1 fusion
  89.1 3.3 %collective-permute-start.6 = (bf16[80,128]{1,0:T(8,128)(2,1)S(1)}, bf16[80,128]{1,0:T(8,128)(2,1)S(1)}, u32[]{:S(2)}, u32[]{:S(2)}) collective-permute-start(bf16[80,128]{1,0:T(8,128)(2,1)S(1)} %slice.71.kept_ref), channel_id=1, source_target_pairs={{0,4},{1,5},{2,6},{3,7},{4,0},{5,1},{6,2},{7,3},{8,12},{9,13},{10,... | collective-permute-start | bytes 61448 | tf_op jit(solution)/shard_map/ppermute | solution.py:391
  92.4 0.7 copy.36
  93.1 0.7 copy.35
  93.8 7.7 %collective-permute-done.6.given_ref = bf16[80,128]{1,0:T(8,128)(2,1)S(1)} collective-permute-done((bf16[80,128]{1,0:T(8,128)(2,1)S(1)}, bf16[80,128]{1,0:T(8,128)(2,1)S(1)}, u32[]{:S(2)}, u32[]{:S(2)}) %collective-permute-start.6) | collective-permute-done | bytes 20512 | tf_op jit(solution)/shard_map/ppermute | solution.py:391
  101.5 2.5 %all-to-all-done.3 = bf16[32,112,128]{2,1,0:T(8,128)(2,1)S(1)} async-done(((bf16[32,112,128]{2,1,0:T(8,128)(2,1)}), bf16[32,112,128]{2,1,0:T(8,128)(2,1)S(1)}, u32[]{:S(2)}, u32[]{:S(2)}) %all-to-all-start.3) | async-done | bytes 917536 | tf_op jit(solution)/shard_map/all_to_all | solution.py:350
  104.0 1.4 %unpack.1 = (f32[1,192]{1,0:T(1,128)}, f32[1,192]{1,0:T(1,128)}, f32[192,576]{1,0:T(8,128)}, f32[192,192]{1,0:T(8,128)}, f32[192,768]{1,0:T(8,128)}, /*index=5*/f32[192,768]{1,0:T(8,128)}, f32[6,1,3312]{2,1,0:T(1,128)}) custom-call(bf16[3584,128]{1,0:T(8,128)(2,1)S(1)} %bitcast.25, bf16[80,128]{1,0:T(8,128)(2,1)S(1)} %slice.71.kept_ref, ...), custom_call_target="tpu_custom_call" | custom-call | flops 500000 | bytes 2700000 | tf_op jit(solution)/shard_map/unpack/pallas_call | solution.py:312
  (51 shorter events, 0.9 us)
Async XLA Ops:
  1.7 22.7 %copy-start = (s32[144,144]{1,0:T(8,128)S(1)}, s32[144,144]{1,0:T(8,128)}, u32[]{:S(2)}) copy-start(s32[144,144]{1,0:T(8,128)} %pos_ref.1) | copy-start | bytes 248836
  1.7 27.5 %collective-permute-start.1 = (bf16[72,192]{1,0:T(8,128)(2,1)S(1)}, bf16[72,192]{1,0:T(8,128)(2,1)S(1)}, u32[]{:S(2)}, u32[]{:S(2)}) collective-permute-start(bf16[72,192]{1,0:T(8,128)(2,1)S(1)} %reshape.91), channel_id=1, source_target_pairs={{0,480},{32,0},{64,32},{96,64},{128,96},{160,128},{192,160},{224,1... | collective-permute-start | bytes 82952 | tf_op jit(solution)/shard_map/ppermute | solution.py:335
  10.7 13.7 %copy-start.1 = (f32[6,1,1,3312]{3,2,1,0:T(1,128)S(1)}, f32[6,1,1,3312]{3,2,1,0:T(1,128)}, u32[]{:S(2)}) copy-start(f32[6,1,1,3312]{3,2,1,0:T(1,128)} %param.18) | copy-start | bytes 238468
  10.7 18.6 %collective-permute-start.2 = (bf16[72,192]{1,0:T(8,128)(2,1)S(1)}, bf16[72,192]{1,0:T(8,128)(2,1)S(1)}, u32[]{:S(2)}, u32[]{:S(2)}) collective-permute-start(bf16[72,192]{1,0:T(8,128)(2,1)S(1)} %reshape.93), channel_id=1, source_target_pairs={{0,511},{1,480},{2,481},{3,482},{4,483},{5,484},{6,485},{7,486},{8... | collective-permute-start | bytes 82952 | tf_op jit(solution)/shard_map/ppermute | solution.py:335
  22.0 2.2 %copy-start.8 = (s32[2,6,12]{2,0,1:T(2,128)S(1)}, s32[2,6,12]{2,0,1:T(2,128)}, u32[]{:S(2)}) copy-start(s32[2,6,12]{2,0,1:T(2,128)} %param.20) | copy-start | bytes 1732
  22.0 7.3 %collective-permute-start = (bf16[72,192]{1,0:T(8,128)(2,1)S(1)}, bf16[72,192]{1,0:T(8,128)(2,1)S(1)}, u32[]{:S(2)}, u32[]{:S(2)}) collective-permute-start(bf16[72,192]{1,0:T(8,128)(2,1)S(1)} %reshape.89), channel_id=1, source_target_pairs={{0,31},{1,0},{2,1},{3,2},{4,3},{5,4},{6,5},{7,6},{8,7},{9,8},{10,9... | collective-permute-start | bytes 82952 | tf_op jit(solution)/shard_map/ppermute | solution.py:335
  29.3 0.9 copy-start.4
  29.4 1.0 copy-start.2
  29.4 1.1 %copy-start.3 = (bf16[768,192]{0,1:T(8,128)(2,1)S(1)}, bf16[768,192]{0,1:T(8,128)(2,1)}, u32[]{:S(2)}) copy-start(bf16[768,192]{0,1:T(8,128)(2,1)} %param.17) | copy-start | bytes 884740
  29.5 1.0 copy-start.5
  29.5 1.0 copy-start.7
  29.6 1.0 copy-start.6
  35.4 18.8 %all-to-all-start = ((bf16[32,112,128]{2,1,0:T(8,128)(2,1)}), bf16[32,112,128]{2,1,0:T(8,128)(2,1)S(1)}, u32[]{:S(2)}, u32[]{:S(2)}) async-start(bf16[32,112,128]{2,1,0:T(8,128)(2,1)} %bitcast.6), calls=%async_computation | async-start | bytes 1835008 | tf_op jit(solution)/shard_map/all_to_all | solution.py:350
  42.2 9.5 %collective-permute-start.3 = (bf16[80,128]{1,0:T(8,128)(2,1)S(1)}, bf16[80,128]{1,0:T(8,128)(2,1)S(1)}, u32[]{:S(2)}, u32[]{:S(2)}) collective-permute-start(bf16[80,128]{1,0:T(8,128)(2,1)S(1)} %dynamic-slice_bitcast_fusion), channel_id=1, source_target_pairs={{0,4},{1,5},{2,6},{3,7},{4,0},{5,1},{6,2},{7,3},{8,12},{9,13},{10,... | collective-permute-start | bytes 61448 | tf_op jit(solution)/shard_map/ppermute | solution.py:379
  45.6 6.1 %collective-permute-start.4 = (bf16[144,192]{1,0:T(8,128)(2,1)S(1)}, bf16[144,192]{1,0:T(8,128)(2,1)S(1)}, u32[]{:S(2)}, u32[]{:S(2)}) collective-permute-start(bf16[144,192]{1,0:T(8,128)(2,1)S(1)} %reshape.101), channel_id=1, source_target_pairs={{0,32},{32,64},{64,96},{96,128},{128,160},{160,192},{192,224},{224... | collective-permute-start | bytes 165896 | tf_op jit(solution)/shard_map/ppermute | solution.py:346
  55.1 15.4 %all-to-all-start.1 = ((bf16[4,192,128]{2,1,0:T(8,128)(2,1)}), bf16[4,192,128]{2,1,0:T(8,128)(2,1)S(1)}, u32[]{:S(2)}, u32[]{:S(2)}) async-start(bf16[4,192,128]{2,1,0:T(8,128)(2,1)} %broadcast_in_dim.6), calls=%async_computation.1 | async-start | bytes 393216 | tf_op jit(solution)/shard_map/all_to_all | solution.py:350
  59.2 11.2 %collective-permute-start.5 = (bf16[144,192]{1,0:T(8,128)(2,1)S(1)}, bf16[144,192]{1,0:T(8,128)(2,1)S(1)}, u32[]{:S(2)}, u32[]{:S(2)}) collective-permute-start(bf16[144,192]{1,0:T(8,128)(2,1)S(1)} %reshape.103), channel_id=1, source_target_pairs={{0,1},{1,2},{2,3},{3,4},{4,5},{5,6},{6,7},{7,8},{8,9},{9,10},{10,1... | collective-permute-start | bytes 165896 | tf_op jit(solution)/shard_map/ppermute | solution.py:346
  82.0 22.0 %all-to-all-start.3 = ((bf16[32,112,128]{2,1,0:T(8,128)(2,1)}), bf16[32,112,128]{2,1,0:T(8,128)(2,1)S(1)}, u32[]{:S(2)}, u32[]{:S(2)}) async-start(bf16[32,112,128]{2,1,0:T(8,128)(2,1)} %broadcast_in_dim.8), calls=%async_computation.3 | async-start | bytes 1835008 | tf_op jit(solution)/shard_map/all_to_all | solution.py:350
  89.1 12.4 %collective-permute-start.6 = (bf16[80,128]{1,0:T(8,128)(2,1)S(1)}, bf16[80,128]{1,0:T(8,128)(2,1)S(1)}, u32[]{:S(2)}, u32[]{:S(2)}) collective-permute-start(bf16[80,128]{1,0:T(8,128)(2,1)S(1)} %slice.71.kept_ref), channel_id=1, source_target_pairs={{0,4},{1,5},{2,6},{3,7},{4,0},{5,1},{6,2},{7,3},{8,12},{9,13},{10,... | collective-permute-start | bytes 61448 | tf_op jit(solution)/shard_map/ppermute | solution.py:391

commit v6 on v5

--- a/solution.py
+++ b/solution.py
@@ -163,11 +163,13 @@
     bias_ref,
     out_ref,
     delta_ref,
-    grads_ref,
+    grads_out_ref,
     pairs_ref,
     scores_ref,
     prob_ref,
     low_ref,
+    grads_ref,
+    sems,
 ):
     factor = HEAD ** (-0.5)
     x = x_ref[...].astype(F32)
@@ -217,6 +219,10 @@
     for t in range(6):
         grads_ref[C * t : C * (t + 1)] = grad_up[:, LANES * t : LANES * (t + 1)]
         grads_ref[C * (t + 6) : C * (t + 7)] = grad_down[:, LANES * t : LANES * (t + 1)]
+    cut = C * 12
+    early = pltpu.make_async_copy(grads_ref.at[:cut], grads_out_ref.at[:cut], sems.at[0])
+    late = pltpu.make_async_copy(grads_ref.at[cut:], grads_out_ref.at[cut:], sems.at[1])
+    early.start()
     delta_hidden = dot_nt(delta_up, up_ref[...])
     delta_input, grad_gain_two = norm_back(delta_hidden, normal_two, inverse_two, gain_two)
     delta_middle = (cot.astype(F32) + delta_input).astype(BF16)
@@ -253,6 +259,9 @@
     grads_ref[C * 18 :] = jnp.concatenate(
         (wide[:, :LANES], wide[:, LANES:], jnp.zeros((124, LANES), F32)), axis=0
     ).astype(BF16)
+    late.start()
+    early.wait()
+    late.wait()
 
 
 def block(*args):
@@ -269,7 +278,10 @@
             pltpu.VMEM((HEADS * WT, WT), F32),
             pltpu.VMEM((HEADS * WT, WT), F32),
             pltpu.VMEM((HEADS * WT, WT), BF16),
+            pltpu.VMEM((GROWS, LANES), BF16),
+            pltpu.SemaphoreType.DMA((2,)),
         ],
+        out_specs=[pl.BlockSpec(memory_space=pl.ANY if k == 2 else pltpu.VMEM) for k in range(4)],
         name="block",
         compiler_params=pltpu.CompilerParams(vmem_limit_bytes=24 * 1024 * 1024),
         cost_estimate=pl.CostEstimate(flops=900_000_000, bytes_accessed=4_000_000, transcendentals=300_000),

time: 106 us -> 106 us (level)
  no operation moved by 1% of the time
where the time goes in v6:
time: 106 us; the launch traced here: 105 us
  starting transfers between devices  51.4 us (48%)
  waiting for transfers between devices  22.2 us (21%)
  Pallas kernels  13.8 us (13%)
  blocking collectives  10.4 us (10%)
  local copies, waits for them, and re-layouts  5.81 us (5%)
    ppermute x3, starting transfers between devices, moved(): return lax.ppermute(piece.reshape(-1, C), axis, pairs).reshape(piece.shape)  22.4 us
    all_to_all x3, starting transfers between devices, spread_over(): lax.all_to_all(parts, axis, 0, 0, axis_index_groups=groups)  14.8 us
    all_to_all x1, blocking collectives, spread_over(): lax.all_to_all(parts, axis, 0, 0, axis_index_groups=groups)  10.4 us
    ppermute x1, waiting for transfers between devices, finish(): given = lax.ppermute(kept, 'lon', other)  7.67 us
    ppermute x2, starting transfers between devices, flat_permute(): lax.ppermute(piece.reshape(-1, C), axis, ring(axis, 1)).reshape(piece.shape)  7.65 us
    ppermute x2, waiting for transfers between devices, flat_permute(): lax.ppermute(piece.reshape(-1, C), axis, ring(axis, 1)).reshape(piece.shape)  7.22 us
    all_to_all x3, waiting for transfers between devices, spread_over(): lax.all_to_all(parts, axis, 0, 0, axis_index_groups=groups)  4.97 us
    pallas_call x1, Pallas kernels, bias_pairs(): pl.pallas_call(gather_kernel, out_shape=[jax.ShapeDtypeStruct((HEADS * WT...  4.86 us
  transfers between devices with their start and end apart: 10, of which 5 were waited for; matrix products, arithmetic and copies ran while one was open for 2% of the time, Pallas kernels for 7%

profile of v6, /device:TPU:1, one launch (start us, length us, event | category | flops | bytes accessed | tf_op | source)
XLA Modules:
  0.0 105.2 jit_solution(15698319204636851502)
XLA Ops:
  0.6 0.9 copy_bitcast_fusion
  1.7 8.9 %collective-permute-start.1 = (bf16[72,192]{1,0:T(8,128)(2,1)S(1)}, bf16[72,192]{1,0:T(8,128)(2,1)S(1)}, u32[]{:S(2)}, u32[]{:S(2)}) collective-permute-start(bf16[72,192]{1,0:T(8,128)(2,1)S(1)} %reshape.91), channel_id=1, source_target_pairs={{0,480},{32,0},{64,32},{96,64},{128,96},{160,128},{192,160},{224,1... | collective-permute-start | bytes 82952 | tf_op jit(solution)/shard_map/ppermute | solution.py:347
  10.7 11.3 %collective-permute-start.2 = (bf16[72,192]{1,0:T(8,128)(2,1)S(1)}, bf16[72,192]{1,0:T(8,128)(2,1)S(1)}, u32[]{:S(2)}, u32[]{:S(2)}) collective-permute-start(bf16[72,192]{1,0:T(8,128)(2,1)S(1)} %reshape.93), channel_id=1, source_target_pairs={{0,511},{1,480},{2,481},{3,482},{4,483},{5,484},{6,485},{7,486},{8... | collective-permute-start | bytes 82952 | tf_op jit(solution)/shard_map/ppermute | solution.py:347
  22.0 2.2 %collective-permute-start = (bf16[72,192]{1,0:T(8,128)(2,1)S(1)}, bf16[72,192]{1,0:T(8,128)(2,1)S(1)}, u32[]{:S(2)}, u32[]{:S(2)}) collective-permute-start(bf16[72,192]{1,0:T(8,128)(2,1)S(1)} %reshape.89), channel_id=1, source_target_pairs={{0,31},{1,0},{2,1},{3,2},{4,3},{5,4},{6,5},{7,6},{8,7},{9,8},{10,9... | collective-permute-start | bytes 82952 | tf_op jit(solution)/shard_map/ppermute | solution.py:347
  24.3 0.1 reshape.98.mask_ref
  24.4 4.9 %bias_pairs.1 = (f32[864,144]{1,0:T(8,128)S(1)}, s32[176,128]{1,0:T(8,128)S(1)}) custom-call(f32[6,1,3312]{2,1,0:T(1,128)S(1)} %bitcast.26, s32[144,144]{1,0:T(8,128)S(1)} %copy-done, s32[1,144]{1,0:T(1,128)S(1)} %reshape.98.mask_ref), custom_call_target="tpu_custom_call" | custom-call | flops 10000000 | bytes 1200000 | tf_op jit(solution)/shard_map/bias_pairs/pallas_call | solution.py:104
  29.4 0.1 maximum_maximum_fusion
  29.6 0.7 copy-done.4
  30.3 0.2 copy-done.2
  30.4 0.1 copy-done.3
  30.6 4.6 %block.1 = (bf16[144,192]{1,0:T(8,128)(2,1)S(1)}, bf16[144,192]{1,0:T(8,128)(2,1)S(1)}, bf16[3584,128]{1,0:T(8,128)(2,1)}, f32[6,176,128]{2,1,0:T(8,128)S(1)}) custom-call(bf16[144,192]{1,0:T(8,128)(2,1)S(1)} %reshape_squeeze.6.x_ref, bf16[144,192]{1,0:T(8,128)(2,1)S(1)} %reshape_squeeze.7.cot_ref, f32[1,192]{1,0:T(1,128)S(1)} %bitcast.30, ...), custom_call_target="tpu_custom_call" | custom-call | flops 900000000 | bytes 4000000 | tf_op jit(solution)/shard_map/block/pallas_call | solution.py:274
  35.2 3.8 %all-to-all-start = ((bf16[32,112,128]{2,1,0:T(8,128)(2,1)}), bf16[32,112,128]{2,1,0:T(8,128)(2,1)S(1)}, u32[]{:S(2)}, u32[]{:S(2)}) async-start(bf16[32,112,128]{2,1,0:T(8,128)(2,1)} %bitcast.6), calls=%async_computation | async-start | bytes 1835008 | tf_op jit(solution)/shard_map/all_to_all | solution.py:362
  39.0 3.0 %bias_grad.1 = bf16[160,128]{1,0:T(8,128)(2,1)S(1)} custom-call(f32[6,176,128]{2,1,0:T(8,128)S(1)} %get-tuple-element.28.pairs_ref, s32[176,128]{1,0:T(8,128)S(1)} %get-tuple-element.29.pos_ref), custom_call_target="tpu_custom_call" | custom-call | flops 1100000000 | bytes 700000 | tf_op jit(solution)/shard_map/bias_grad/pallas_call | solution.py:144
  42.0 3.3 %collective-permute-start.3 = (bf16[80,128]{1,0:T(8,128)(2,1)S(1)}, bf16[80,128]{1,0:T(8,128)(2,1)S(1)}, u32[]{:S(2)}, u32[]{:S(2)}) collective-permute-start(bf16[80,128]{1,0:T(8,128)(2,1)S(1)} %dynamic-slice_bitcast_fusion), channel_id=1, source_target_pairs={{0,4},{1,5},{2,6},{3,7},{4,0},{5,1},{6,2},{7,3},{8,12},{9,13},{10,... | collective-permute-start | bytes 61448 | tf_op jit(solution)/shard_map/ppermute | solution.py:391
  45.5 3.6 %collective-permute-start.4 = (bf16[144,192]{1,0:T(8,128)(2,1)S(1)}, bf16[144,192]{1,0:T(8,128)(2,1)S(1)}, u32[]{:S(2)}, u32[]{:S(2)}) collective-permute-start(bf16[144,192]{1,0:T(8,128)(2,1)S(1)} %reshape.101), channel_id=1, source_target_pairs={{0,32},{32,64},{64,96},{96,128},{128,160},{160,192},{192,224},{224... | collective-permute-start | bytes 165896 | tf_op jit(solution)/shard_map/ppermute | solution.py:358
  49.1 2.4 %collective-permute-done.3 = bf16[80,128]{1,0:T(8,128)(2,1)S(1)} collective-permute-done((bf16[80,128]{1,0:T(8,128)(2,1)S(1)}, bf16[80,128]{1,0:T(8,128)(2,1)S(1)}, u32[]{:S(2)}, u32[]{:S(2)}) %collective-permute-start.3) | collective-permute-done | bytes 20512 | tf_op jit(solution)/shard_map/ppermute | solution.py:391
  51.6 2.5 %all-to-all-done = bf16[32,112,128]{2,1,0:T(8,128)(2,1)S(1)} async-done(((bf16[32,112,128]{2,1,0:T(8,128)(2,1)}), bf16[32,112,128]{2,1,0:T(8,128)(2,1)S(1)}, u32[]{:S(2)}, u32[]{:S(2)}) %all-to-all-start) | async-done | bytes 917536 | tf_op jit(solution)/shard_map/all_to_all | solution.py:362
  54.1 0.1 reduce_sum.48
  54.2 0.7 broadcast_in_dim.6
  54.9 4.0 %all-to-all-start.1 = ((bf16[4,192,128]{2,1,0:T(8,128)(2,1)}), bf16[4,192,128]{2,1,0:T(8,128)(2,1)S(1)}, u32[]{:S(2)}, u32[]{:S(2)}) async-start(bf16[4,192,128]{2,1,0:T(8,128)(2,1)} %broadcast_in_dim.6), calls=%async_computation.1 | async-start | bytes 393216 | tf_op jit(solution)/shard_map/all_to_all | solution.py:362
  59.0 4.0 %collective-permute-start.5 = (bf16[144,192]{1,0:T(8,128)(2,1)S(1)}, bf16[144,192]{1,0:T(8,128)(2,1)S(1)}, u32[]{:S(2)}, u32[]{:S(2)}) collective-permute-start(bf16[144,192]{1,0:T(8,128)(2,1)S(1)} %reshape.103), channel_id=1, source_target_pairs={{0,1},{1,2},{2,3},{3,4},{4,5},{5,6},{6,7},{7,8},{8,9},{9,10},{10,1... | collective-permute-start | bytes 165896 | tf_op jit(solution)/shard_map/ppermute | solution.py:358
  63.1 7.2 %collective-permute-done.5 = bf16[144,192]{1,0:T(8,128)(2,1)S(1)} collective-permute-done((bf16[144,192]{1,0:T(8,128)(2,1)S(1)}, bf16[144,192]{1,0:T(8,128)(2,1)S(1)}, u32[]{:S(2)}, u32[]{:S(2)}) %collective-permute-start.5) | collective-permute-done | bytes 55328 | tf_op jit(solution)/shard_map/ppermute | solution.py:358
  70.4 10.4 %all_to_all.20 = bf16[4,192,128]{2,1,0:T(8,128)(2,1)S(1)} all-to-all(bf16[4,192,128]{2,1,0:T(8,128)(2,1)S(1)} %broadcast_in_dim.7), channel_id=1, replica_groups={{0,1,2,3},{4,5,6,7},{8,9,10,11},{12,13,14,15},{16,17,18,19},{20,21,22,2..., dimensions={0} | all-to-all | bytes 393216 | tf_op jit(solution)/shard_map/all_to_all | solution.py:362
  80.8 1.1 broadcast_in_dim.8
  81.9 7.0 %all-to-all-start.3 = ((bf16[32,112,128]{2,1,0:T(8,128)(2,1)}), bf16[32,112,128]{2,1,0:T(8,128)(2,1)S(1)}, u32[]{:S(2)}, u32[]{:S(2)}) async-start(bf16[32,112,128]{2,1,0:T(8,128)(2,1)} %broadcast_in_dim.8), calls=%async_computation.3 | async-start | bytes 1835008 | tf_op jit(solution)/shard_map/all_to_all | solution.py:362
  88.8 0.1 fusion
  88.9 3.3 %collective-permute-start.6 = (bf16[80,128]{1,0:T(8,128)(2,1)S(1)}, bf16[80,128]{1,0:T(8,128)(2,1)S(1)}, u32[]{:S(2)}, u32[]{:S(2)}) collective-permute-start(bf16[80,128]{1,0:T(8,128)(2,1)S(1)} %slice.71.kept_ref), channel_id=1, source_target_pairs={{0,4},{1,5},{2,6},{3,7},{4,0},{5,1},{6,2},{7,3},{8,12},{9,13},{10,... | collective-permute-start | bytes 61448 | tf_op jit(solution)/shard_map/ppermute | solution.py:403
  92.3 0.7 copy.36
  93.0 0.7 copy.35
  93.7 7.7 %collective-permute-done.6.given_ref = bf16[80,128]{1,0:T(8,128)(2,1)S(1)} collective-permute-done((bf16[80,128]{1,0:T(8,128)(2,1)S(1)}, bf16[80,128]{1,0:T(8,128)(2,1)S(1)}, u32[]{:S(2)}, u32[]{:S(2)}) %collective-permute-start.6) | collective-permute-done | bytes 20512 | tf_op jit(solution)/shard_map/ppermute | solution.py:403
  101.3 2.5 %all-to-all-done.3 = bf16[32,112,128]{2,1,0:T(8,128)(2,1)S(1)} async-done(((bf16[32,112,128]{2,1,0:T(8,128)(2,1)}), bf16[32,112,128]{2,1,0:T(8,128)(2,1)S(1)}, u32[]{:S(2)}, u32[]{:S(2)}) %all-to-all-start.3) | async-done | bytes 917536 | tf_op jit(solution)/shard_map/all_to_all | solution.py:362
  103.8 1.4 %unpack.1 = (f32[1,192]{1,0:T(1,128)}, f32[1,192]{1,0:T(1,128)}, f32[192,576]{1,0:T(8,128)}, f32[192,192]{1,0:T(8,128)}, f32[192,768]{1,0:T(8,128)}, /*index=5*/f32[192,768]{1,0:T(8,128)}, f32[6,1,3312]{2,1,0:T(1,128)}) custom-call(bf16[3584,128]{1,0:T(8,128)(2,1)S(1)} %bitcast.25, bf16[80,128]{1,0:T(8,128)(2,1)S(1)} %slice.71.kept_ref, ...), custom_call_target="tpu_custom_call" | custom-call | flops 500000 | bytes 2700000 | tf_op jit(solution)/shard_map/unpack/pallas_call | solution.py:324
  (51 shorter events, 0.9 us)
Async XLA Ops:
  1.7 22.7 %copy-start = (s32[144,144]{1,0:T(8,128)S(1)}, s32[144,144]{1,0:T(8,128)}, u32[]{:S(2)}) copy-start(s32[144,144]{1,0:T(8,128)} %pos_ref.1) | copy-start | bytes 248836
  1.7 27.5 %collective-permute-start.1 = (bf16[72,192]{1,0:T(8,128)(2,1)S(1)}, bf16[72,192]{1,0:T(8,128)(2,1)S(1)}, u32[]{:S(2)}, u32[]{:S(2)}) collective-permute-start(bf16[72,192]{1,0:T(8,128)(2,1)S(1)} %reshape.91), channel_id=1, source_target_pairs={{0,480},{32,0},{64,32},{96,64},{128,96},{160,128},{192,160},{224,1... | collective-permute-start | bytes 82952 | tf_op jit(solution)/shard_map/ppermute | solution.py:347
  10.7 13.7 %copy-start.1 = (f32[6,1,1,3312]{3,2,1,0:T(1,128)S(1)}, f32[6,1,1,3312]{3,2,1,0:T(1,128)}, u32[]{:S(2)}) copy-start(f32[6,1,1,3312]{3,2,1,0:T(1,128)} %param.18) | copy-start | bytes 238468
  10.7 18.6 %collective-permute-start.2 = (bf16[72,192]{1,0:T(8,128)(2,1)S(1)}, bf16[72,192]{1,0:T(8,128)(2,1)S(1)}, u32[]{:S(2)}, u32[]{:S(2)}) collective-permute-start(bf16[72,192]{1,0:T(8,128)(2,1)S(1)} %reshape.93), channel_id=1, source_target_pairs={{0,511},{1,480},{2,481},{3,482},{4,483},{5,484},{6,485},{7,486},{8... | collective-permute-start | bytes 82952 | tf_op jit(solution)/shard_map/ppermute | solution.py:347
  22.0 2.2 %copy-start.8 = (s32[2,6,12]{2,0,1:T(2,128)S(1)}, s32[2,6,12]{2,0,1:T(2,128)}, u32[]{:S(2)}) copy-start(s32[2,6,12]{2,0,1:T(2,128)} %param.20) | copy-start | bytes 1732
  22.0 7.3 %collective-permute-start = (bf16[72,192]{1,0:T(8,128)(2,1)S(1)}, bf16[72,192]{1,0:T(8,128)(2,1)S(1)}, u32[]{:S(2)}, u32[]{:S(2)}) collective-permute-start(bf16[72,192]{1,0:T(8,128)(2,1)S(1)} %reshape.89), channel_id=1, source_target_pairs={{0,31},{1,0},{2,1},{3,2},{4,3},{5,4},{6,5},{7,6},{8,7},{9,8},{10,9... | collective-permute-start | bytes 82952 | tf_op jit(solution)/shard_map/ppermute | solution.py:347
  29.3 0.9 copy-start.4
  29.4 1.0 copy-start.2
  29.4 1.1 %copy-start.3 = (bf16[768,192]{0,1:T(8,128)(2,1)S(1)}, bf16[768,192]{0,1:T(8,128)(2,1)}, u32[]{:S(2)}) copy-start(bf16[768,192]{0,1:T(8,128)(2,1)} %param.17) | copy-start | bytes 884740
  29.5 1.0 copy-start.5
  29.5 1.0 copy-start.7
  29.6 1.0 copy-start.6
  35.2 18.9 %all-to-all-start = ((bf16[32,112,128]{2,1,0:T(8,128)(2,1)}), bf16[32,112,128]{2,1,0:T(8,128)(2,1)S(1)}, u32[]{:S(2)}, u32[]{:S(2)}) async-start(bf16[32,112,128]{2,1,0:T(8,128)(2,1)} %bitcast.6), calls=%async_computation | async-start | bytes 1835008 | tf_op jit(solution)/shard_map/all_to_all | solution.py:362
  42.0 9.5 %collective-permute-start.3 = (bf16[80,128]{1,0:T(8,128)(2,1)S(1)}, bf16[80,128]{1,0:T(8,128)(2,1)S(1)}, u32[]{:S(2)}, u32[]{:S(2)}) collective-permute-start(bf16[80,128]{1,0:T(8,128)(2,1)S(1)} %dynamic-slice_bitcast_fusion), channel_id=1, source_target_pairs={{0,4},{1,5},{2,6},{3,7},{4,0},{5,1},{6,2},{7,3},{8,12},{9,13},{10,... | collective-permute-start | bytes 61448 | tf_op jit(solution)/shard_map/ppermute | solution.py:391
  45.5 6.1 %collective-permute-start.4 = (bf16[144,192]{1,0:T(8,128)(2,1)S(1)}, bf16[144,192]{1,0:T(8,128)(2,1)S(1)}, u32[]{:S(2)}, u32[]{:S(2)}) collective-permute-start(bf16[144,192]{1,0:T(8,128)(2,1)S(1)} %reshape.101), channel_id=1, source_target_pairs={{0,32},{32,64},{64,96},{96,128},{128,160},{160,192},{192,224},{224... | collective-permute-start | bytes 165896 | tf_op jit(solution)/shard_map/ppermute | solution.py:358
  54.9 15.4 %all-to-all-start.1 = ((bf16[4,192,128]{2,1,0:T(8,128)(2,1)}), bf16[4,192,128]{2,1,0:T(8,128)(2,1)S(1)}, u32[]{:S(2)}, u32[]{:S(2)}) async-start(bf16[4,192,128]{2,1,0:T(8,128)(2,1)} %broadcast_in_dim.6), calls=%async_computation.1 | async-start | bytes 393216 | tf_op jit(solution)/shard_map/all_to_all | solution.py:362
  59.0 11.2 %collective-permute-start.5 = (bf16[144,192]{1,0:T(8,128)(2,1)S(1)}, bf16[144,192]{1,0:T(8,128)(2,1)S(1)}, u32[]{:S(2)}, u32[]{:S(2)}) collective-permute-start(bf16[144,192]{1,0:T(8,128)(2,1)S(1)} %reshape.103), channel_id=1, source_target_pairs={{0,1},{1,2},{2,3},{3,4},{4,5},{5,6},{6,7},{7,8},{8,9},{9,10},{10,1... | collective-permute-start | bytes 165896 | tf_op jit(solution)/shard_map/ppermute | solution.py:358
  81.9 22.0 %all-to-all-start.3 = ((bf16[32,112,128]{2,1,0:T(8,128)(2,1)}), bf16[32,112,128]{2,1,0:T(8,128)(2,1)S(1)}, u32[]{:S(2)}, u32[]{:S(2)}) async-start(bf16[32,112,128]{2,1,0:T(8,128)(2,1)} %broadcast_in_dim.8), calls=%async_computation.3 | async-start | bytes 1835008 | tf_op jit(solution)/shard_map/all_to_all | solution.py:362
  88.9 12.4 %collective-permute-start.6 = (bf16[80,128]{1,0:T(8,128)(2,1)S(1)}, bf16[80,128]{1,0:T(8,128)(2,1)S(1)}, u32[]{:S(2)}, u32[]{:S(2)}) collective-permute-start(bf16[80,128]{1,0:T(8,128)(2,1)S(1)} %slice.71.kept_ref), channel_id=1, source_target_pairs={{0,4},{1,5},{2,6},{3,7},{4,0},{5,1},{6,2},{7,3},{8,12},{9,13},{10,... | collective-permute-start | bytes 61448 | tf_op jit(solution)/shard_map/ppermute | solution.py:403

commit v7 on v5

--- a/solution.py
+++ b/solution.py
@@ -17,7 +17,7 @@
 TAIL = WT - LANES
 ROWS = WT + 2 * TAIL
 GROWS = 3584
-STEP = 44
+STEP = 88
 BROWS = 160
 LOW = 2
 FAR = 4

time: 106 us -> 106 us (level)
  no operation moved by 1% of the time
where the time goes in v7:
time: 106 us; the launch traced here: 105 us
  starting transfers between devices  51.3 us (48%)
  waiting for transfers between devices  22.6 us (21%)
  Pallas kernels  13.7 us (13%)
  blocking collectives  10.4 us (10%)
  local copies, waits for them, and re-layouts  5.81 us (5%)
    ppermute x3, starting transfers between devices, moved(): return lax.ppermute(piece.reshape(-1, C), axis, pairs).reshape(piece.shape)  22.4 us
    all_to_all x3, starting transfers between devices, spread_over(): lax.all_to_all(parts, axis, 0, 0, axis_index_groups=groups)  14.7 us
    all_to_all x1, blocking collectives, spread_over(): lax.all_to_all(parts, axis, 0, 0, axis_index_groups=groups)  10.4 us
    ppermute x1, waiting for transfers between devices, finish(): given = lax.ppermute(kept, 'lon', other)  7.67 us
    ppermute x2, starting transfers between devices, flat_permute(): lax.ppermute(piece.reshape(-1, C), axis, ring(axis, 1)).reshape(piece.shape)  7.65 us
    ppermute x2, waiting for transfers between devices, flat_permute(): lax.ppermute(piece.reshape(-1, C), axis, ring(axis, 1)).reshape(piece.shape)  7.18 us
    all_to_all x3, waiting for transfers between devices, spread_over(): lax.all_to_all(parts, axis, 0, 0, axis_index_groups=groups)  5 us
    pallas_call x1, Pallas kernels, bias_pairs(): pl.pallas_call(gather_kernel, out_shape=[jax.ShapeDtypeStruct((HEADS * WT...  4.86 us
  transfers between devices with their start and end apart: 10, of which 5 were waited for; matrix products, arithmetic and copies ran while one was open for 2% of the time, Pallas kernels for 7%

profile of v7, /device:TPU:1, one launch (start us, length us, event | category | flops | bytes accessed | tf_op | source)
XLA Modules:
  0.0 105.3 jit_solution(11773867302630403984)
XLA Ops:
  0.6 0.9 copy_bitcast_fusion
  1.7 8.9 %collective-permute-start.1 = (bf16[72,192]{1,0:T(8,128)(2,1)S(1)}, bf16[72,192]{1,0:T(8,128)(2,1)S(1)}, u32[]{:S(2)}, u32[]{:S(2)}) collective-permute-start(bf16[72,192]{1,0:T(8,128)(2,1)S(1)} %reshape.91), channel_id=1, source_target_pairs={{0,480},{32,0},{64,32},{96,64},{128,96},{160,128},{192,160},{224,1... | collective-permute-start | bytes 82952 | tf_op jit(solution)/shard_map/ppermute | solution.py:335
  10.7 11.3 %collective-permute-start.2 = (bf16[72,192]{1,0:T(8,128)(2,1)S(1)}, bf16[72,192]{1,0:T(8,128)(2,1)S(1)}, u32[]{:S(2)}, u32[]{:S(2)}) collective-permute-start(bf16[72,192]{1,0:T(8,128)(2,1)S(1)} %reshape.93), channel_id=1, source_target_pairs={{0,511},{1,480},{2,481},{3,482},{4,483},{5,484},{6,485},{7,486},{8... | collective-permute-start | bytes 82952 | tf_op jit(solution)/shard_map/ppermute | solution.py:335
  22.0 2.2 %collective-permute-start = (bf16[72,192]{1,0:T(8,128)(2,1)S(1)}, bf16[72,192]{1,0:T(8,128)(2,1)S(1)}, u32[]{:S(2)}, u32[]{:S(2)}) collective-permute-start(bf16[72,192]{1,0:T(8,128)(2,1)S(1)} %reshape.89), channel_id=1, source_target_pairs={{0,31},{1,0},{2,1},{3,2},{4,3},{5,4},{6,5},{7,6},{8,7},{9,8},{10,9... | collective-permute-start | bytes 82952 | tf_op jit(solution)/shard_map/ppermute | solution.py:335
  24.3 0.1 reshape.98.mask_ref
  24.4 4.9 %bias_pairs.1 = (f32[864,144]{1,0:T(8,128)S(1)}, s32[176,128]{1,0:T(8,128)S(1)}) custom-call(f32[6,1,3312]{2,1,0:T(1,128)S(1)} %bitcast.26, s32[144,144]{1,0:T(8,128)S(1)} %copy-done, s32[1,144]{1,0:T(1,128)S(1)} %reshape.98.mask_ref), custom_call_target="tpu_custom_call" | custom-call | flops 10000000 | bytes 1200000 | tf_op jit(solution)/shard_map/bias_pairs/pallas_call | solution.py:104
  29.4 0.1 maximum_maximum_fusion
  29.6 0.7 copy-done.4
  30.3 0.2 copy-done.2
  30.4 0.1 copy-done.3
  30.6 4.8 %block.1 = (bf16[144,192]{1,0:T(8,128)(2,1)S(1)}, bf16[144,192]{1,0:T(8,128)(2,1)S(1)}, bf16[3584,128]{1,0:T(8,128)(2,1)}, f32[6,176,128]{2,1,0:T(8,128)S(1)}) custom-call(bf16[144,192]{1,0:T(8,128)(2,1)S(1)} %reshape_squeeze.6.x_ref, bf16[144,192]{1,0:T(8,128)(2,1)S(1)} %reshape_squeeze.7.cot_ref, f32[1,192]{1,0:T(1,128)S(1)} %bitcast.30, ...), custom_call_target="tpu_custom_call" | custom-call | flops 900000000 | bytes 4000000 | tf_op jit(solution)/shard_map/block/pallas_call | solution.py:265
  35.4 3.8 %all-to-all-start = ((bf16[32,112,128]{2,1,0:T(8,128)(2,1)}), bf16[32,112,128]{2,1,0:T(8,128)(2,1)S(1)}, u32[]{:S(2)}, u32[]{:S(2)}) async-start(bf16[32,112,128]{2,1,0:T(8,128)(2,1)} %bitcast.6), calls=%async_computation | async-start | bytes 1835008 | tf_op jit(solution)/shard_map/all_to_all | solution.py:350
  39.2 2.6 %bias_grad.1 = bf16[160,128]{1,0:T(8,128)(2,1)S(1)} custom-call(f32[6,176,128]{2,1,0:T(8,128)S(1)} %get-tuple-element.28.pairs_ref, s32[176,128]{1,0:T(8,128)S(1)} %get-tuple-element.29.pos_ref), custom_call_target="tpu_custom_call" | custom-call | flops 1100000000 | bytes 700000 | tf_op jit(solution)/shard_map/bias_grad/pallas_call | solution.py:144
  41.9 3.3 %collective-permute-start.3 = (bf16[80,128]{1,0:T(8,128)(2,1)S(1)}, bf16[80,128]{1,0:T(8,128)(2,1)S(1)}, u32[]{:S(2)}, u32[]{:S(2)}) collective-permute-start(bf16[80,128]{1,0:T(8,128)(2,1)S(1)} %dynamic-slice_bitcast_fusion), channel_id=1, source_target_pairs={{0,4},{1,5},{2,6},{3,7},{4,0},{5,1},{6,2},{7,3},{8,12},{9,13},{10,... | collective-permute-start | bytes 61448 | tf_op jit(solution)/shard_map/ppermute | solution.py:379
  45.3 3.6 %collective-permute-start.4 = (bf16[144,192]{1,0:T(8,128)(2,1)S(1)}, bf16[144,192]{1,0:T(8,128)(2,1)S(1)}, u32[]{:S(2)}, u32[]{:S(2)}) collective-permute-start(bf16[144,192]{1,0:T(8,128)(2,1)S(1)} %reshape.101), channel_id=1, source_target_pairs={{0,32},{32,64},{64,96},{96,128},{128,160},{160,192},{192,224},{224... | collective-permute-start | bytes 165896 | tf_op jit(solution)/shard_map/ppermute | solution.py:346
  49.0 2.7 %collective-permute-done.3 = bf16[80,128]{1,0:T(8,128)(2,1)S(1)} collective-permute-done((bf16[80,128]{1,0:T(8,128)(2,1)S(1)}, bf16[80,128]{1,0:T(8,128)(2,1)S(1)}, u32[]{:S(2)}, u32[]{:S(2)}) %collective-permute-start.3) | collective-permute-done | bytes 20512 | tf_op jit(solution)/shard_map/ppermute | solution.py:379
  51.7 2.5 %all-to-all-done = bf16[32,112,128]{2,1,0:T(8,128)(2,1)S(1)} async-done(((bf16[32,112,128]{2,1,0:T(8,128)(2,1)}), bf16[32,112,128]{2,1,0:T(8,128)(2,1)S(1)}, u32[]{:S(2)}, u32[]{:S(2)}) %all-to-all-start) | async-done | bytes 917536 | tf_op jit(solution)/shard_map/all_to_all | solution.py:350
  54.2 0.1 reduce_sum.48
  54.4 0.7 broadcast_in_dim.6
  55.1 4.0 %all-to-all-start.1 = ((bf16[4,192,128]{2,1,0:T(8,128)(2,1)}), bf16[4,192,128]{2,1,0:T(8,128)(2,1)S(1)}, u32[]{:S(2)}, u32[]{:S(2)}) async-start(bf16[4,192,128]{2,1,0:T(8,128)(2,1)} %broadcast_in_dim.6), calls=%async_computation.1 | async-start | bytes 393216 | tf_op jit(solution)/shard_map/all_to_all | solution.py:350
  59.2 4.0 %collective-permute-start.5 = (bf16[144,192]{1,0:T(8,128)(2,1)S(1)}, bf16[144,192]{1,0:T(8,128)(2,1)S(1)}, u32[]{:S(2)}, u32[]{:S(2)}) collective-permute-start(bf16[144,192]{1,0:T(8,128)(2,1)S(1)} %reshape.103), channel_id=1, source_target_pairs={{0,1},{1,2},{2,3},{3,4},{4,5},{5,6},{6,7},{7,8},{8,9},{9,10},{10,1... | collective-permute-start | bytes 165896 | tf_op jit(solution)/shard_map/ppermute | solution.py:346
  63.2 7.2 %collective-permute-done.5 = bf16[144,192]{1,0:T(8,128)(2,1)S(1)} collective-permute-done((bf16[144,192]{1,0:T(8,128)(2,1)S(1)}, bf16[144,192]{1,0:T(8,128)(2,1)S(1)}, u32[]{:S(2)}, u32[]{:S(2)}) %collective-permute-start.5) | collective-permute-done | bytes 55328 | tf_op jit(solution)/shard_map/ppermute | solution.py:346
  70.5 10.4 %all_to_all.20 = bf16[4,192,128]{2,1,0:T(8,128)(2,1)S(1)} all-to-all(bf16[4,192,128]{2,1,0:T(8,128)(2,1)S(1)} %broadcast_in_dim.7), channel_id=1, replica_groups={{0,1,2,3},{4,5,6,7},{8,9,10,11},{12,13,14,15},{16,17,18,19},{20,21,22,2..., dimensions={0} | all-to-all | bytes 393216 | tf_op jit(solution)/shard_map/all_to_all | solution.py:350
  81.0 1.1 broadcast_in_dim.8
  82.0 6.9 %all-to-all-start.3 = ((bf16[32,112,128]{2,1,0:T(8,128)(2,1)}), bf16[32,112,128]{2,1,0:T(8,128)(2,1)S(1)}, u32[]{:S(2)}, u32[]{:S(2)}) async-start(bf16[32,112,128]{2,1,0:T(8,128)(2,1)} %broadcast_in_dim.8), calls=%async_computation.3 | async-start | bytes 1835008 | tf_op jit(solution)/shard_map/all_to_all | solution.py:350
  88.9 0.1 fusion
  89.0 3.3 %collective-permute-start.6 = (bf16[80,128]{1,0:T(8,128)(2,1)S(1)}, bf16[80,128]{1,0:T(8,128)(2,1)S(1)}, u32[]{:S(2)}, u32[]{:S(2)}) collective-permute-start(bf16[80,128]{1,0:T(8,128)(2,1)S(1)} %slice.71.kept_ref), channel_id=1, source_target_pairs={{0,4},{1,5},{2,6},{3,7},{4,0},{5,1},{6,2},{7,3},{8,12},{9,13},{10,... | collective-permute-start | bytes 61448 | tf_op jit(solution)/shard_map/ppermute | solution.py:391
  92.3 0.7 copy.36
  93.1 0.7 copy.35
  93.8 7.7 %collective-permute-done.6.given_ref = bf16[80,128]{1,0:T(8,128)(2,1)S(1)} collective-permute-done((bf16[80,128]{1,0:T(8,128)(2,1)S(1)}, bf16[80,128]{1,0:T(8,128)(2,1)S(1)}, u32[]{:S(2)}, u32[]{:S(2)}) %collective-permute-start.6) | collective-permute-done | bytes 20512 | tf_op jit(solution)/shard_map/ppermute | solution.py:391
  101.4 2.5 %all-to-all-done.3 = bf16[32,112,128]{2,1,0:T(8,128)(2,1)S(1)} async-done(((bf16[32,112,128]{2,1,0:T(8,128)(2,1)}), bf16[32,112,128]{2,1,0:T(8,128)(2,1)S(1)}, u32[]{:S(2)}, u32[]{:S(2)}) %all-to-all-start.3) | async-done | bytes 917536 | tf_op jit(solution)/shard_map/all_to_all | solution.py:350
  103.9 1.4 %unpack.1 = (f32[1,192]{1,0:T(1,128)}, f32[1,192]{1,0:T(1,128)}, f32[192,576]{1,0:T(8,128)}, f32[192,192]{1,0:T(8,128)}, f32[192,768]{1,0:T(8,128)}, /*index=5*/f32[192,768]{1,0:T(8,128)}, f32[6,1,3312]{2,1,0:T(1,128)}) custom-call(bf16[3584,128]{1,0:T(8,128)(2,1)S(1)} %bitcast.25, bf16[80,128]{1,0:T(8,128)(2,1)S(1)} %slice.71.kept_ref, ...), custom_call_target="tpu_custom_call" | custom-call | flops 500000 | bytes 2700000 | tf_op jit(solution)/shard_map/unpack/pallas_call | solution.py:312
  (51 shorter events, 0.9 us)
Async XLA Ops:
  1.7 22.7 %copy-start = (s32[144,144]{1,0:T(8,128)S(1)}, s32[144,144]{1,0:T(8,128)}, u32[]{:S(2)}) copy-start(s32[144,144]{1,0:T(8,128)} %pos_ref.1) | copy-start | bytes 248836
  1.7 27.5 %collective-permute-start.1 = (bf16[72,192]{1,0:T(8,128)(2,1)S(1)}, bf16[72,192]{1,0:T(8,128)(2,1)S(1)}, u32[]{:S(2)}, u32[]{:S(2)}) collective-permute-start(bf16[72,192]{1,0:T(8,128)(2,1)S(1)} %reshape.91), channel_id=1, source_target_pairs={{0,480},{32,0},{64,32},{96,64},{128,96},{160,128},{192,160},{224,1... | collective-permute-start | bytes 82952 | tf_op jit(solution)/shard_map/ppermute | solution.py:335
  10.7 13.7 %copy-start.1 = (f32[6,1,1,3312]{3,2,1,0:T(1,128)S(1)}, f32[6,1,1,3312]{3,2,1,0:T(1,128)}, u32[]{:S(2)}) copy-start(f32[6,1,1,3312]{3,2,1,0:T(1,128)} %param.18) | copy-start | bytes 238468
  10.7 18.6 %collective-permute-start.2 = (bf16[72,192]{1,0:T(8,128)(2,1)S(1)}, bf16[72,192]{1,0:T(8,128)(2,1)S(1)}, u32[]{:S(2)}, u32[]{:S(2)}) collective-permute-start(bf16[72,192]{1,0:T(8,128)(2,1)S(1)} %reshape.93), channel_id=1, source_target_pairs={{0,511},{1,480},{2,481},{3,482},{4,483},{5,484},{6,485},{7,486},{8... | collective-permute-start | bytes 82952 | tf_op jit(solution)/shard_map/ppermute | solution.py:335
  22.0 2.2 %copy-start.8 = (s32[2,6,12]{2,0,1:T(2,128)S(1)}, s32[2,6,12]{2,0,1:T(2,128)}, u32[]{:S(2)}) copy-start(s32[2,6,12]{2,0,1:T(2,128)} %param.20) | copy-start | bytes 1732
  22.0 7.3 %collective-permute-start = (bf16[72,192]{1,0:T(8,128)(2,1)S(1)}, bf16[72,192]{1,0:T(8,128)(2,1)S(1)}, u32[]{:S(2)}, u32[]{:S(2)}) collective-permute-start(bf16[72,192]{1,0:T(8,128)(2,1)S(1)} %reshape.89), channel_id=1, source_target_pairs={{0,31},{1,0},{2,1},{3,2},{4,3},{5,4},{6,5},{7,6},{8,7},{9,8},{10,9... | collective-permute-start | bytes 82952 | tf_op jit(solution)/shard_map/ppermute | solution.py:335
  29.3 0.9 copy-start.4
  29.4 1.0 copy-start.2
  29.4 1.1 %copy-start.3 = (bf16[768,192]{0,1:T(8,128)(2,1)S(1)}, bf16[768,192]{0,1:T(8,128)(2,1)}, u32[]{:S(2)}) copy-start(bf16[768,192]{0,1:T(8,128)(2,1)} %param.17) | copy-start | bytes 884740
  29.5 1.0 copy-start.5
  29.5 1.0 copy-start.7
  29.6 1.0 copy-start.6
  35.4 18.8 %all-to-all-start = ((bf16[32,112,128]{2,1,0:T(8,128)(2,1)}), bf16[32,112,128]{2,1,0:T(8,128)(2,1)S(1)}, u32[]{:S(2)}, u32[]{:S(2)}) async-start(bf16[32,112,128]{2,1,0:T(8,128)(2,1)} %bitcast.6), calls=%async_computation | async-start | bytes 1835008 | tf_op jit(solution)/shard_map/all_to_all | solution.py:350
  41.9 9.8 %collective-permute-start.3 = (bf16[80,128]{1,0:T(8,128)(2,1)S(1)}, bf16[80,128]{1,0:T(8,128)(2,1)S(1)}, u32[]{:S(2)}, u32[]{:S(2)}) collective-permute-start(bf16[80,128]{1,0:T(8,128)(2,1)S(1)} %dynamic-slice_bitcast_fusion), channel_id=1, source_target_pairs={{0,4},{1,5},{2,6},{3,7},{4,0},{5,1},{6,2},{7,3},{8,12},{9,13},{10,... | collective-permute-start | bytes 61448 | tf_op jit(solution)/shard_map/ppermute | solution.py:379
  45.3 6.4 %collective-permute-start.4 = (bf16[144,192]{1,0:T(8,128)(2,1)S(1)}, bf16[144,192]{1,0:T(8,128)(2,1)S(1)}, u32[]{:S(2)}, u32[]{:S(2)}) collective-permute-start(bf16[144,192]{1,0:T(8,128)(2,1)S(1)} %reshape.101), channel_id=1, source_target_pairs={{0,32},{32,64},{64,96},{96,128},{128,160},{160,192},{192,224},{224... | collective-permute-start | bytes 165896 | tf_op jit(solution)/shard_map/ppermute | solution.py:346
  55.1 15.4 %all-to-all-start.1 = ((bf16[4,192,128]{2,1,0:T(8,128)(2,1)}), bf16[4,192,128]{2,1,0:T(8,128)(2,1)S(1)}, u32[]{:S(2)}, u32[]{:S(2)}) async-start(bf16[4,192,128]{2,1,0:T(8,128)(2,1)} %broadcast_in_dim.6), calls=%async_computation.1 | async-start | bytes 393216 | tf_op jit(solution)/shard_map/all_to_all | solution.py:350
  59.2 11.2 %collective-permute-start.5 = (bf16[144,192]{1,0:T(8,128)(2,1)S(1)}, bf16[144,192]{1,0:T(8,128)(2,1)S(1)}, u32[]{:S(2)}, u32[]{:S(2)}) collective-permute-start(bf16[144,192]{1,0:T(8,128)(2,1)S(1)} %reshape.103), channel_id=1, source_target_pairs={{0,1},{1,2},{2,3},{3,4},{4,5},{5,6},{6,7},{7,8},{8,9},{9,10},{10,1... | collective-permute-start | bytes 165896 | tf_op jit(solution)/shard_map/ppermute | solution.py:346
  82.0 21.9 %all-to-all-start.3 = ((bf16[32,112,128]{2,1,0:T(8,128)(2,1)}), bf16[32,112,128]{2,1,0:T(8,128)(2,1)S(1)}, u32[]{:S(2)}, u32[]{:S(2)}) async-start(bf16[32,112,128]{2,1,0:T(8,128)(2,1)} %broadcast_in_dim.8), calls=%async_computation.3 | async-start | bytes 1835008 | tf_op jit(solution)/shard_map/all_to_all | solution.py:350
  89.0 12.4 %collective-permute-start.6 = (bf16[80,128]{1,0:T(8,128)(2,1)S(1)}, bf16[80,128]{1,0:T(8,128)(2,1)S(1)}, u32[]{:S(2)}, u32[]{:S(2)}) collective-permute-start(bf16[80,128]{1,0:T(8,128)(2,1)S(1)} %slice.71.kept_ref), channel_id=1, source_target_pairs={{0,4},{1,5},{2,6},{3,7},{4,0},{5,1},{6,2},{7,3},{8,12},{9,13},{10,... | collective-permute-start | bytes 61448 | tf_op jit(solution)/shard_map/ppermute | solution.py:391
